TPU v7x, 32 devices: a whole 2x2x4 slice. The times are simulated.
32 devices in a mesh: fsdp: 8 (over y, x, core), tp: 4 (over z).
Axes of the slice: x: 2, y: 2, z: 4, core: 2. Of those that a mesh axis runs over, the one named last changes fastest.
Arguments:
- tokens: bfloat16 [8192, 2048], P(('fsdp', 'tp')), may hold values from -6 to 6
- attn_gain: bfloat16 [2048], P('fsdp'), may hold values from 0.5 to 1.5
- query_weight: bfloat16 [2048, 2048], P('fsdp', 'tp'), may hold values from -0.125 to 0.125
- key_weight: bfloat16 [2048, 256], P('fsdp', 'tp'), may hold values from -0.125 to 0.125
- value_weight: bfloat16 [2048, 256], P('fsdp', 'tp'), may hold values from -0.125 to 0.125
- output_weight: bfloat16 [2048, 2048], P('tp', 'fsdp'), may hold values from -3 to 3
- mlp_gain: bfloat16 [2048], P('fsdp'), may hold values from 0.5 to 1.5
- gate_weight: bfloat16 [2048, 5632], P('fsdp', 'tp'), may hold values from -0.125 to 0.125
- up_weight: bfloat16 [2048, 5632], P('fsdp', 'tp'), may hold values from -0.125 to 0.125
- down_weight: bfloat16 [5632, 2048], P('tp', 'fsdp'), may hold values from -0.078125 to 0.078125
- out_grad: bfloat16 [8192, 2048], P(('fsdp', 'tp')), may hold values from -6 to 6
- lengths: int32 [2], replicated, may hold values from 1024 to 4096, as said below
Outputs:
- layer_out: bfloat16 [8192, 2048], P(('fsdp', 'tp'))
- tokens_grad: float32 [8192, 2048], P(('fsdp', 'tp'))
- grad_attn_gain: float32 [2048], P('fsdp')
- grad_query: float32 [2048, 2048], P('fsdp', 'tp')
- grad_key: float32 [2048, 256], P('fsdp', 'tp')
- grad_value: float32 [2048, 256], P('fsdp', 'tp')
- grad_output: float32 [2048, 2048], P('tp', 'fsdp')
- grad_mlp_gain: float32 [2048], P('fsdp')
- grad_gate: float32 [2048, 5632], P('fsdp', 'tp')
- grad_up: float32 [2048, 5632], P('fsdp', 'tp')
- grad_down: float32 [5632, 2048], P('tp', 'fsdp')
Inputs may be any that keep to these rules, and one draw needn't show every extreme that they name: `lengths`: one sequence, which one drawn from the seed, is exactly 4096 long, the others at least 1024 and shorter than 4096; their sum is less than 8192.
All inputs are finite; a program needn't handle non-finite values.
Results may differ from a plain program's by a relative error of at most 0.025.
Values may be sent and summed in bfloat16 or wider, within the bound.
A program may use at most 256 MiB of HBM per device.

v0:
```python
import jax
import jax.numpy as jnp
from jax import lax
from jax.sharding import PartitionSpec as P

HEAD_DIM = 64
MAX_SPAN = 4096


epsilon = 1e-05


def passed_along(block, axis, distance):
    devices = range(lax.axis_size(axis))
    route = [(i - distance, i) for i in devices if i - distance in devices]
    return lax.ppermute(block, axis, route)


def stream_layout(slots, lengths):
    seq_count = lengths.shape[0]
    seq_index = jnp.arange(seq_count, dtype=jnp.int32)
    ends = jnp.cumsum(lengths)
    starts = ends - lengths
    segment = jnp.sum((slots[:, None] >= ends[None, :]).astype(jnp.int32), axis=1)
    start_of = jnp.sum(
        jnp.where(segment[:, None] == seq_index[None, :], starts[None, :], 0), axis=1
    )
    position = jnp.where((segment < seq_count) & (slots >= 0), slots - start_of, 0)
    segment = jnp.where(slots < 0, -1, segment)
    return (segment, position)


def rotary_tables(positions, head_width):
    ladder = jnp.arange(head_width // 2).astype(jnp.float32)
    frequency = 10000.0 ** (-2.0 * ladder / head_width)
    angle_half = positions.astype(jnp.float32)[:, None] * frequency[None, :]
    angles = jnp.concatenate([angle_half, angle_half], axis=1)
    return (jnp.cos(angles)[:, None, :], jnp.sin(angles)[:, None, :])


def rotate(values, cosine, sine_table):
    middle = values.shape[-1] // 2
    turned = jnp.concatenate([-values[..., middle:], values[..., :middle]], axis=-1)
    return values * cosine + turned * sine_table


def rotate_back(values, cosine, sine_table):
    middle = values.shape[-1] // 2
    scaled = values * sine_table
    turned = jnp.concatenate([scaled[..., middle:], -scaled[..., :middle]], axis=-1)
    return values * cosine + turned


def inner_rows(left, right):
    return lax.dot_general(
        left, right, (((0,), (0,)), ((), ())), preferred_element_type=jnp.float32
    )


def outer_cols(left, right):
    return lax.dot_general(
        left, right, (((1,), (1,)), ((), ())), preferred_element_type=jnp.float32
    )


def norm_back(grad_normed, gain_wide, normed, inverse):
    scaled_grad = grad_normed * gain_wide
    return inverse * (scaled_grad - normed * jnp.mean(scaled_grad * normed, axis=1, keepdims=True))


def local(
    tokens,
    attn_gain,
    query_weight,
    key_weight,
    value_weight,
    output_weight,
    mlp_gain,
    gate_weight,
    up_weight,
    down_weight,
    out_grad,
    lengths,
):
    row_count = tokens.shape[0]
    tp_count = lax.axis_size("tp")
    block_rows = row_count * tp_count
    slot_total = block_rows * lax.axis_size("fsdp")
    longest = min(MAX_SPAN, slot_total // 2)
    reach_count = (longest - 2) // block_rows + 1
    window = (reach_count + 1) * block_rows
    front_rows = reach_count * block_rows
    block_index = lax.axis_index("fsdp")
    tp_index = lax.axis_index("tp")
    head_width = HEAD_DIM
    query_width = query_weight.shape[1]
    key_width = key_weight.shape[1]
    heads_here = query_width // head_width
    score_scale = head_width ** (-0.5)
    seq_count = lengths.shape[0]
    row_base = (block_index * tp_count + tp_index) * row_count
    my_slots = row_base + jnp.arange(row_count, dtype=jnp.int32)
    my_segments, my_positions = stream_layout(my_slots, lengths)
    valid_rows = (my_segments < seq_count)[:, None]
    gathered = (
        lax.all_gather(query_weight, "fsdp", axis=0, tiled=True),
        lax.all_gather(key_weight, "fsdp", axis=0, tiled=True),
        lax.all_gather(value_weight, "fsdp", axis=0, tiled=True),
        lax.all_gather(output_weight, "fsdp", axis=1, tiled=True),
        lax.all_gather(gate_weight, "fsdp", axis=0, tiled=True),
        lax.all_gather(up_weight, "fsdp", axis=0, tiled=True),
        lax.all_gather(down_weight, "fsdp", axis=1, tiled=True),
        lax.all_gather(attn_gain, "fsdp", axis=0, tiled=True),
        lax.all_gather(mlp_gain, "fsdp", axis=0, tiled=True),
    )
    (
        full_query,
        full_key,
        full_value,
        full_output,
        full_gate,
        full_up,
        full_down,
        gain_first,
        gain_second,
    ) = gathered
    w_inner = jnp.concatenate([full_query, full_key, full_value], axis=1)
    gain_first_wide = gain_first.astype(jnp.float32)
    gain_second_wide = gain_second.astype(jnp.float32)
    tokens_wide = tokens.astype(jnp.float32)
    inverse_first = lax.rsqrt(jnp.mean(tokens_wide * tokens_wide, axis=1, keepdims=True) + epsilon)
    normed_first = tokens_wide * inverse_first
    scaled_first = (normed_first * gain_first_wide).astype(jnp.bfloat16)
    rows_first = lax.all_gather(scaled_first, "tp", axis=0, tiled=True)
    projected = jnp.dot(rows_first, w_inner, preferred_element_type=jnp.float32)
    block_base = block_index * block_rows
    key_slots = block_base - front_rows + jnp.arange(window, dtype=jnp.int32)
    key_segments, key_positions = stream_layout(key_slots, lengths)
    query_segments = key_segments[front_rows:]
    block_positions = key_positions[front_rows:]
    cosine, sine_table = rotary_tables(block_positions, head_width)
    queries = rotate(
        projected[:, :query_width].reshape(block_rows, heads_here, head_width), cosine, sine_table
    ).astype(jnp.bfloat16)
    keys_local = rotate(
        projected[:, query_width : query_width + key_width].reshape(block_rows, 1, head_width),
        cosine,
        sine_table,
    )
    keys_local = keys_local.reshape(block_rows, head_width).astype(jnp.bfloat16)
    values_local = projected[:, query_width + key_width :].astype(jnp.bfloat16)
    pair_local = jnp.concatenate([keys_local, values_local], axis=1)
    pieces = []
    for offset in range(reach_count, 0, -1):
        pieces.append(passed_along(pair_local, "fsdp", offset))
    pair_window = jnp.concatenate(pieces + [pair_local], axis=0)
    key_window = pair_window[:, :head_width]
    value_window = pair_window[:, head_width:]
    key_seen = (key_segments[None, :] == query_segments[:, None]) & (
        key_positions[None, :] <= block_positions[:, None]
    )

    def head_scores(query_head):
        scores = outer_cols(query_head, key_window) * score_scale
        return jnp.where(key_seen, scores, -1e30)

    def head_forward(query_head):
        scores = head_scores(query_head)
        largest = jnp.max(scores, axis=1, keepdims=True)
        raised = jnp.exp(scores - largest)
        row_total = jnp.sum(raised, axis=1, keepdims=True)
        attn_probs = (raised / row_total).astype(jnp.bfloat16)
        head_out = jnp.dot(attn_probs, value_window, preferred_element_type=jnp.float32)
        return (head_out, (largest + jnp.log(row_total))[:, 0])

    query_heads = jnp.moveaxis(queries, 1, 0)
    head_outs, log_totals = lax.map(head_forward, query_heads)
    attended = jnp.moveaxis(head_outs, 0, 1).reshape(block_rows, query_width).astype(jnp.bfloat16)
    attn_share = lax.psum_scatter(
        jnp.dot(attended, full_output, preferred_element_type=jnp.float32).astype(jnp.bfloat16),
        "tp",
        scatter_dimension=0,
        tiled=True,
    ).astype(jnp.float32)
    middle = tokens_wide + attn_share
    inverse_second = lax.rsqrt(jnp.mean(middle * middle, axis=1, keepdims=True) + epsilon)
    normed_second = middle * inverse_second
    scaled_second = (normed_second * gain_second_wide).astype(jnp.bfloat16)
    rows_second = lax.all_gather(scaled_second, "tp", axis=0, tiled=True)
    gate_proj = jnp.dot(rows_second, full_gate, preferred_element_type=jnp.float32)
    up_proj = jnp.dot(rows_second, full_up, preferred_element_type=jnp.float32)
    gate_sigmoid = jax.nn.sigmoid(gate_proj)
    gate_active = gate_proj * gate_sigmoid
    hidden = (gate_active * up_proj).astype(jnp.bfloat16)
    mlp_share = lax.psum_scatter(
        jnp.dot(hidden, full_down, preferred_element_type=jnp.float32).astype(jnp.bfloat16),
        "tp",
        scatter_dimension=0,
        tiled=True,
    ).astype(jnp.float32)
    layer_out = jnp.where(valid_rows, middle + mlp_share, 0.0).astype(jnp.bfloat16)
    grad_rows = jnp.where(valid_rows, out_grad.astype(jnp.float32), 0.0)
    grad_low = grad_rows.astype(jnp.bfloat16)
    regathered = (
        lax.all_gather(query_weight, "fsdp", axis=0, tiled=True),
        lax.all_gather(key_weight, "fsdp", axis=0, tiled=True),
        lax.all_gather(value_weight, "fsdp", axis=0, tiled=True),
        lax.all_gather(output_weight, "fsdp", axis=1, tiled=True),
        lax.all_gather(gate_weight, "fsdp", axis=0, tiled=True),
        lax.all_gather(up_weight, "fsdp", axis=0, tiled=True),
        lax.all_gather(down_weight, "fsdp", axis=1, tiled=True),
        lax.all_gather(attn_gain, "fsdp", axis=0, tiled=True),
        lax.all_gather(mlp_gain, "fsdp", axis=0, tiled=True),
    )
    (
        full_query,
        full_key,
        full_value,
        full_output,
        full_gate,
        full_up,
        full_down,
        gain_first,
        gain_second,
    ) = regathered
    w_inner = jnp.concatenate([full_query, full_key, full_value], axis=1)
    grad_down_rows = lax.all_gather(grad_low, "tp", axis=0, tiled=True)
    grad_down_w = inner_rows(hidden, grad_down_rows)
    grad_hidden = outer_cols(grad_down_rows, full_down)
    grad_up_low = (grad_hidden * gate_active).astype(jnp.bfloat16)
    grad_gate_low = (
        grad_hidden * up_proj * gate_sigmoid * (1.0 + gate_proj * (1.0 - gate_sigmoid))
    ).astype(jnp.bfloat16)
    grad_gate_w = inner_rows(rows_second, grad_gate_low)
    grad_up_w = inner_rows(rows_second, grad_up_low)
    grad_second = lax.psum_scatter(
        (outer_cols(grad_gate_low, full_gate) + outer_cols(grad_up_low, full_up)).astype(
            jnp.bfloat16
        ),
        "tp",
        scatter_dimension=0,
        tiled=True,
    ).astype(jnp.float32)
    gain_second_part = jnp.sum(grad_second * normed_second, axis=0)
    grad_middle = grad_rows + norm_back(
        grad_second, gain_second_wide, normed_second, inverse_second
    )
    middle_low = grad_middle.astype(jnp.bfloat16)
    grad_attn_rows = lax.all_gather(middle_low, "tp", axis=0, tiled=True)
    grad_output_w = inner_rows(attended, grad_attn_rows)
    grad_attended = outer_cols(grad_attn_rows, full_output).astype(jnp.bfloat16)
    grad_heads = jnp.moveaxis(grad_attended.reshape(block_rows, heads_here, head_width), 1, 0)

    def head_backward(packed):
        query_head, grad_head, log_total = packed
        attn_probs = jnp.exp(head_scores(query_head) - log_total[:, None])
        probs_low = attn_probs.astype(jnp.bfloat16)
        grad_value_head = inner_rows(probs_low, grad_head)
        grad_probs = outer_cols(grad_head, value_window)
        grad_scores = (
            attn_probs * (grad_probs - jnp.sum(attn_probs * grad_probs, axis=1, keepdims=True))
        ).astype(jnp.bfloat16)
        grad_query_head = (
            jnp.dot(grad_scores, key_window, preferred_element_type=jnp.float32) * score_scale
        )
        grad_key_head = inner_rows(grad_scores, query_head) * score_scale
        return (grad_query_head, grad_key_head, grad_value_head)

    grad_query_heads, grad_key_heads, grad_value_heads = lax.map(
        head_backward, (query_heads, grad_heads, log_totals)
    )
    grad_pair = jnp.concatenate(
        [jnp.sum(grad_key_heads, axis=0), jnp.sum(grad_value_heads, axis=0)], axis=1
    )
    own_grad = grad_pair[front_rows:]
    for offset in range(1, reach_count + 1):
        piece_start = (reach_count - offset) * block_rows
        own_grad = own_grad + passed_along(
            grad_pair[piece_start : piece_start + block_rows].astype(jnp.bfloat16), "fsdp", -offset
        ).astype(jnp.float32)
    grad_key_lin = rotate_back(
        own_grad[:, :head_width].reshape(block_rows, 1, head_width), cosine, sine_table
    )
    grad_key_low = grad_key_lin.reshape(block_rows, head_width).astype(jnp.bfloat16)
    grad_value_low = own_grad[:, head_width:].astype(jnp.bfloat16)
    grad_query_lin = rotate_back(jnp.moveaxis(grad_query_heads, 0, 1), cosine, sine_table)
    grad_query_low = grad_query_lin.reshape(block_rows, query_width).astype(jnp.bfloat16)
    grad_inner = jnp.concatenate([grad_query_low, grad_key_low, grad_value_low], axis=1)
    grad_inner_w = inner_rows(rows_first, grad_inner)
    grad_first = lax.psum_scatter(
        outer_cols(grad_inner, w_inner).astype(jnp.bfloat16), "tp", scatter_dimension=0, tiled=True
    ).astype(jnp.float32)
    gain_first_part = jnp.sum(grad_first * normed_first, axis=0)
    tokens_grad = grad_middle + norm_back(grad_first, gain_first_wide, normed_first, inverse_first)
    reduced = (
        lax.psum_scatter(
            grad_inner_w[:, :query_width].astype(jnp.bfloat16),
            "fsdp",
            scatter_dimension=0,
            tiled=True,
        ).astype(jnp.float32),
        lax.psum_scatter(
            grad_inner_w[:, query_width : query_width + key_width].astype(jnp.bfloat16),
            "fsdp",
            scatter_dimension=0,
            tiled=True,
        ).astype(jnp.float32),
        lax.psum_scatter(
            grad_inner_w[:, query_width + key_width :].astype(jnp.bfloat16),
            "fsdp",
            scatter_dimension=0,
            tiled=True,
        ).astype(jnp.float32),
        lax.psum_scatter(
            grad_output_w.astype(jnp.bfloat16), "fsdp", scatter_dimension=1, tiled=True
        ).astype(jnp.float32),
        lax.psum_scatter(
            grad_gate_w.astype(jnp.bfloat16), "fsdp", scatter_dimension=0, tiled=True
        ).astype(jnp.float32),
        lax.psum_scatter(
            grad_up_w.astype(jnp.bfloat16), "fsdp", scatter_dimension=0, tiled=True
        ).astype(jnp.float32),
        lax.psum_scatter(
            grad_down_w.astype(jnp.bfloat16), "fsdp", scatter_dimension=1, tiled=True
        ).astype(jnp.float32),
        lax.psum_scatter(
            gain_first_part.astype(jnp.bfloat16), "fsdp", scatter_dimension=0, tiled=True
        ).astype(jnp.float32),
        lax.psum_scatter(
            gain_second_part.astype(jnp.bfloat16), "fsdp", scatter_dimension=0, tiled=True
        ).astype(jnp.float32),
    )
    gain_sums = lax.psum((reduced[7], reduced[8]), "tp")
    return (
        layer_out,
        tokens_grad,
        gain_sums[0],
        reduced[0],
        reduced[1],
        reduced[2],
        reduced[3],
        gain_sums[1],
        reduced[4],
        reduced[5],
        reduced[6],
    )


def solution(mesh):
    in_specs = (
        P(("fsdp", "tp"), None),
        P("fsdp"),
        P("fsdp", "tp"),
        P("fsdp", "tp"),
        P("fsdp", "tp"),
        P("tp", "fsdp"),
        P("fsdp"),
        P("fsdp", "tp"),
        P("fsdp", "tp"),
        P("tp", "fsdp"),
        P(("fsdp", "tp"), None),
        P(),
    )
    out_specs = (
        P(("fsdp", "tp"), None),
        P(("fsdp", "tp"), None),
        P("fsdp"),
        P("fsdp", "tp"),
        P("fsdp", "tp"),
        P("fsdp", "tp"),
        P("tp", "fsdp"),
        P("fsdp"),
        P("fsdp", "tp"),
        P("fsdp", "tp"),
        P("tp", "fsdp"),
    )
    return jax.shard_map(local, mesh=mesh, in_specs=in_specs, out_specs=out_specs, check_vma=False)
```

profile of v0, /device:TPU:0, one launch (start us, length us, event | category | flops | bytes accessed | tf_op | source)
XLA Modules:
  0.0 1812.8 jit_solution(10962112741223576199)
XLA Ops:
  8.6 10.3 all-gather
  26.6 11.2 all_gather.49
  48.2 76.6 %all-gather.12.cloned.1.call-done = bf16[1024,2048]{1,0:T(8,128)(2,1)} async-done(((bf16[256,2048]{1,0:T(8,128)(2,1)}), bf16[1024,2048]{1,0:T(8,128)(2,1)}) %all-gather.12.cloned.1.call-update) | async-done | bytes 4194320 | tf_op jit(solution)/shard_map/all_gather | solution.py:134
  167.7 152.7 %while.30 = (s32[]{:T(128)}, bf16[8,1024,64]{1,2,0:T(8,128)(2,1)}, f32[8,1024]{1,0:T(8,128)}, bf16[8,1024,64]{2,1,0:T(8,128)(2,1)}, bf16[5120,64]{1,0:T(8,128)(2...) while((s32[]{:T(128)}, bf16[8,1024,64]{1,2,0:T(8,128)(2,1)}, ...), condition=%wide.region_8.9_spmd.clone.clone, body=%wide.region_5.8_spmd.clone.sunk.clone | while | flops 1399847936 | bytes 66150520 | solution.py:177
  327.4 10.6 all-gather.1
  338.0 67.8 %reduce-scatter.12.cloned.1.call-done = bf16[256,2048]{1,0:T(8,128)(2,1)} async-done(((bf16[1024,2048]{1,0:T(8,128)(2,1)}), bf16[256,2048]{1,0:T(8,128)(2,1)}) %reduce-scatter.12.cloned.1.call-update) | async-done | bytes 1048592 | tf_op jit(solution)/shard_map/reduce_scatter | solution.py:179
  413.2 38.4 %all-gather.22.cloned.1.call-done = bf16[2048,1408]{1,0:T(8,128)(2,1)} async-done(((bf16[256,1408]{1,0:T(8,128)(2,1)}), bf16[2048,1408]{1,0:T(8,128)(2,1)}) %all-gather.22.cloned.1.call-update) | async-done | bytes 5767184 | tf_op jit(solution)/shard_map/all_gather | solution.py:111
  451.6 82.9 %all-gather.18.cloned.1.call-done = bf16[1024,2048]{1,0:T(8,128)(2,1)} async-done(((bf16[256,2048]{1,0:T(8,128)(2,1)}), bf16[1024,2048]{1,0:T(8,128)(2,1)}) %all-gather.18.cloned.1.call-update) | async-done | bytes 4194320 | tf_op jit(solution)/shard_map/all_gather | solution.py:189
  534.5 11.7 fusion.93
  546.2 32.2 %all-gather.20.cloned.1.call-done = bf16[2048,1408]{1,0:T(8,128)(2,1)} async-done(((bf16[256,1408]{1,0:T(8,128)(2,1)}), bf16[2048,1408]{1,0:T(8,128)(2,1)}) %all-gather.20.cloned.1.call-update) | async-done | bytes 5767184 | tf_op jit(solution)/shard_map/all_gather | solution.py:110
  578.4 11.7 fusion.92
  590.1 71.4 %all-gather.26.cloned.1.call-done = bf16[1024,2048]{1,0:T(8,128)(2,1)} async-done(((bf16[256,2048]{1,0:T(8,128)(2,1)}), bf16[1024,2048]{1,0:T(8,128)(2,1)}) %all-gather.26.cloned.1.call-update) | async-done | bytes 4194320 | tf_op jit(solution)/shard_map/all_gather | solution.py:227
  661.4 45.0 %all-gather.24.cloned.1.call-done = bf16[1408,2048]{1,0:T(8,128)(2,1)} async-done(((bf16[1408,256]{1,0:T(8,128)(2,1)}), bf16[1408,2048]{1,0:T(8,128)(2,1)}) %all-gather.24.cloned.1.call-update) | async-done | bytes 5767184 | tf_op jit(solution)/shard_map/all_gather | solution.py:112
  706.4 16.8 multiply_convert_fusion.1
  731.8 11.2 add_convert_fusion
  743.1 76.9 %reduce-scatter.16.cloned.1.call-done = bf16[256,2048]{1,0:T(8,128)(2,1)} async-done(((bf16[1024,2048]{1,0:T(8,128)(2,1)}), bf16[256,2048]{1,0:T(8,128)(2,1)}) %reduce-scatter.16.cloned.1.call-update) | async-done | bytes 1048592 | tf_op jit(solution)/shard_map/reduce_scatter | solution.py:236
  824.8 10.4 convolution_convert_fusion
  837.2 10.8 convolution_convert_fusion.1
  849.8 11.0 convolution_convert_fusion.2
  860.8 45.4 %all-gather.28.cloned.1.call-done = bf16[1024,2048]{1,0:T(8,128)(2,1)} async-done(((bf16[256,2048]{1,0:T(8,128)(2,1)}), bf16[1024,2048]{1,0:T(8,128)(2,1)}) %all-gather.28.cloned.1.call-update) | async-done | bytes 4194320 | tf_op jit(solution)/shard_map/all_gather | solution.py:249
  915.1 529.6 %while.31 = (s32[]{:T(128)}, f32[8,1024,64]{1,2,0:T(8,128)}, f32[8,5120,64]{1,2,0:T(8,128)}, f32[8,5120,64]{1,2,0:T(8,128)}, bf16[8,1024,64]{2,1,0:T(8,128)(2,1)...) while((s32[]{:T(128)}, f32[8,1024,64]{1,2,0:T(8,128)}, ...), condition=%wide.region_16.17_spmd.clone.clone, body=%wide.region_14.16_spmd.clone.sunk.clone | while | flops 3418749952 | bytes 292362496 | solution.py:269
  915.9 10.3 fusion.178
  926.3 15.7 multiply_reduce_fusion.4
  942.0 18.9 %multiply_convert_fusion.7 = bf16[1024,5120]{1,0:T(8,128)(2,1)} fusion(f32[1024,5120]{1,0:T(8,128)} %get-tuple-element.543, f32[1024,5120]{1,0:T(8,128)} %fusion.178, f32[1024]{0:T(1024)S(1)} %get-tuple-element.544), kind=kLoop, calls=%fused_computation.13.clone.1.clone | loop fusion | flops 15728640 | bytes 52432896 | tf_op jit(solution)/shard_map/while/body/eval_jaxpr/convert_element_type | solution.py:262
  992.7 16.6 multiply_reduce_fusion.4
  1009.3 18.9 %multiply_convert_fusion.7 = bf16[1024,5120]{1,0:T(8,128)(2,1)} fusion(f32[1024,5120]{1,0:T(8,128)} %get-tuple-element.543, f32[1024,5120]{1,0:T(8,128)} %fusion.178, f32[1024]{0:T(1024)S(1)} %get-tuple-element.544), kind=kLoop, calls=%fused_computation.13.clone.1.clone | loop fusion | flops 15728640 | bytes 52432896 | tf_op jit(solution)/shard_map/while/body/eval_jaxpr/convert_element_type | solution.py:262
  1037.0 9.6 fusion.179
  1051.6 10.1 fusion.178
  1061.7 15.8 multiply_reduce_fusion.4
  1077.5 18.9 %multiply_convert_fusion.7 = bf16[1024,5120]{1,0:T(8,128)(2,1)} fusion(f32[1024,5120]{1,0:T(8,128)} %get-tuple-element.543, f32[1024,5120]{1,0:T(8,128)} %fusion.178, f32[1024]{0:T(1024)S(1)} %get-tuple-element.544), kind=kLoop, calls=%fused_computation.13.clone.1.clone | loop fusion | flops 15728640 | bytes 52432896 | tf_op jit(solution)/shard_map/while/body/eval_jaxpr/convert_element_type | solution.py:262
  1127.9 15.7 multiply_reduce_fusion.4
  1143.6 18.2 %multiply_convert_fusion.7 = bf16[1024,5120]{1,0:T(8,128)(2,1)} fusion(f32[1024,5120]{1,0:T(8,128)} %get-tuple-element.543, f32[1024,5120]{1,0:T(8,128)} %fusion.178, f32[1024]{0:T(1024)S(1)} %get-tuple-element.544), kind=kLoop, calls=%fused_computation.13.clone.1.clone | loop fusion | flops 15728640 | bytes 52432896 | tf_op jit(solution)/shard_map/while/body/eval_jaxpr/convert_element_type | solution.py:262
  1193.3 15.7 multiply_reduce_fusion.4
  1209.0 18.2 %multiply_convert_fusion.7 = bf16[1024,5120]{1,0:T(8,128)(2,1)} fusion(f32[1024,5120]{1,0:T(8,128)} %get-tuple-element.543, f32[1024,5120]{1,0:T(8,128)} %fusion.178, f32[1024]{0:T(1024)S(1)} %get-tuple-element.544), kind=kLoop, calls=%fused_computation.13.clone.1.clone | loop fusion | flops 15728640 | bytes 52432896 | tf_op jit(solution)/shard_map/while/body/eval_jaxpr/convert_element_type | solution.py:262
  1258.7 15.7 multiply_reduce_fusion.4
  1274.4 18.2 %multiply_convert_fusion.7 = bf16[1024,5120]{1,0:T(8,128)(2,1)} fusion(f32[1024,5120]{1,0:T(8,128)} %get-tuple-element.543, f32[1024,5120]{1,0:T(8,128)} %fusion.178, f32[1024]{0:T(1024)S(1)} %get-tuple-element.544), kind=kLoop, calls=%fused_computation.13.clone.1.clone | loop fusion | flops 15728640 | bytes 52432896 | tf_op jit(solution)/shard_map/while/body/eval_jaxpr/convert_element_type | solution.py:262
  1324.1 15.7 multiply_reduce_fusion.4
  1339.8 18.2 %multiply_convert_fusion.7 = bf16[1024,5120]{1,0:T(8,128)(2,1)} fusion(f32[1024,5120]{1,0:T(8,128)} %get-tuple-element.543, f32[1024,5120]{1,0:T(8,128)} %fusion.178, f32[1024]{0:T(1024)S(1)} %get-tuple-element.544), kind=kLoop, calls=%fused_computation.13.clone.1.clone | loop fusion | flops 15728640 | bytes 52432896 | tf_op jit(solution)/shard_map/while/body/eval_jaxpr/convert_element_type | solution.py:262
  1389.5 15.7 multiply_reduce_fusion.4
  1405.2 18.2 %multiply_convert_fusion.7 = bf16[1024,5120]{1,0:T(8,128)(2,1)} fusion(f32[1024,5120]{1,0:T(8,128)} %get-tuple-element.543, f32[1024,5120]{1,0:T(8,128)} %fusion.178, f32[1024]{0:T(1024)S(1)} %get-tuple-element.544), kind=kLoop, calls=%fused_computation.13.clone.1.clone | loop fusion | flops 15728640 | bytes 52432896 | tf_op jit(solution)/shard_map/while/body/eval_jaxpr/convert_element_type | solution.py:262
  1493.6 11.1 convolution_convert_fusion.4
  1517.4 35.1 %reduce-scatter.24.cloned.1.call-done = bf16[256,64]{0,1:T(8,128)(2,1)} async-done(((bf16[2048,64]{0,1:T(8,128)(2,1)}), bf16[256,64]{0,1:T(8,128)(2,1)}) %reduce-scatter.24.cloned.1.call-update) | async-done | bytes 32784 | tf_op jit(solution)/shard_map/reduce_scatter | solution.py:308
  1553.9 43.3 %reduce-scatter.26.cloned.1.call-done = bf16[512,256]{1,0:T(8,128)(2,1)} async-done(((bf16[512,2048]{1,0:T(8,128)(2,1)}), bf16[512,256]{1,0:T(8,128)(2,1)}) %reduce-scatter.26.cloned.1.call-update) | async-done | bytes 262160 | tf_op jit(solution)/shard_map/reduce_scatter | solution.py:314
  1599.0 43.2 %reduce-scatter.20.cloned.1.call-done = bf16[256,512]{0,1:T(8,128)(2,1)} async-done(((bf16[2048,512]{0,1:T(8,128)(2,1)}), bf16[256,512]{0,1:T(8,128)(2,1)}) %reduce-scatter.20.cloned.1.call-update) | async-done | bytes 262160 | tf_op jit(solution)/shard_map/reduce_scatter | solution.py:296
  1644.1 77.3 %reduce-scatter.18.cloned.1.call-done = bf16[256,2048]{1,0:T(8,128)(2,1)} async-done(((bf16[1024,2048]{1,0:T(8,128)(2,1)}), bf16[256,2048]{1,0:T(8,128)(2,1)}) %reduce-scatter.18.cloned.1.call-update) | async-done | bytes 1048592 | tf_op jit(solution)/shard_map/reduce_scatter | solution.py:290
  1723.5 14.0 all-reduce.3
  1737.6 11.9 all-reduce.2
  1749.5 51.6 %reduce-scatter.14.cloned.1.call-done = bf16[256,2048]{1,0:T(8,128)(2,1)} async-done(((bf16[1024,2048]{1,0:T(8,128)(2,1)}), bf16[256,2048]{1,0:T(8,128)(2,1)}) %reduce-scatter.14.cloned.1.call-update) | async-done | bytes 1048592 | tf_op jit(solution)/shard_map/reduce_scatter | solution.py:195
  (382 shorter events, 552.1 us)
Async XLA Ops:
  7.2 41.0 %all-gather.14.cloned.1.call-start = ((), (), s32[]{:S(2)}) async-start(), calls=%async_computation.12 | async-start | bytes 2359296 | tf_op jit(solution)/shard_map/all_gather | solution.py:106
  7.9 116.9 %all-gather.12.cloned.1.call-start = ((), (), s32[]{:S(2)}) async-start(), calls=%async_computation.11 | async-start | bytes 5242880 | tf_op jit(solution)/shard_map/all_gather | solution.py:134
  23.7 296.7 %all-gather.16.cloned.1.call-start = ((), (), s32[]{:S(2)}) async-start(), calls=%async_computation.13 | async-start | bytes 2359296 | tf_op jit(solution)/shard_map/all_gather | solution.py:109
  24.4 381.5 %reduce-scatter.12.cloned.1.call-start = ((), (), s32[]{:S(2)}) async-start(), calls=%async_computation.14 | async-start | bytes 5242880 | tf_op jit(solution)/shard_map/reduce_scatter | solution.py:179
  38.1 92.7 %copy-start.23 = (bf16[2048,64]{1,0:T(8,128)(2,1)}, bf16[2048,64]{1,0:T(8,128)(2,1)S(1)}, u32[]{:S(2)}) copy-start(bf16[2048,64]{1,0:T(8,128)(2,1)S(1)} %copy.49) | copy-start | bytes 786436
  48.2 82.7 %copy-start.20 = (f32[1024,32]{0,1:T(8,128)}, f32[1024,32]{0,1:T(8,128)S(1)}, u32[]{:S(2)}) copy-start(f32[1024,32]{0,1:T(8,128)S(1)} %broadcast_multiply_fusion) | copy-start | bytes 393220
  133.0 30.7 %collective-permute-start.3 = (bf16[1024,128]{0,1:T(8,128)(2,1)}, bf16[1024,128]{0,1:T(8,128)(2,1)}, u32[]{:S(2)}, u32[]{:S(2)}) collective-permute-start(bf16[1024,128]{0,1:T(8,128)(2,1)} %pad_maximum_fusion.8), channel_id=1, source_target_pairs={{0,4},{4,8},{8,12},{12,16},{16,20},{20,24},{24,28},{1,5},{5,9},{9,... | collective-permute-start | bytes 786440 | tf_op jit(solution)/shard_map/ppermute | solution.py:16
  135.6 27.2 %collective-permute-start.2 = (bf16[1024,128]{0,1:T(8,128)(2,1)}, bf16[1024,128]{0,1:T(8,128)(2,1)}, u32[]{:S(2)}, u32[]{:S(2)}) collective-permute-start(bf16[1024,128]{0,1:T(8,128)(2,1)} %pad_maximum_fusion.8), channel_id=1, source_target_pairs={{0,8},{4,12},{8,16},{12,20},{16,24},{20,28},{1,9},{5,13},{9,17},{1... | collective-permute-start | bytes 786440 | tf_op jit(solution)/shard_map/ppermute | solution.py:16
  139.2 22.6 %collective-permute-start.1 = (bf16[1024,128]{0,1:T(8,128)(2,1)}, bf16[1024,128]{0,1:T(8,128)(2,1)}, u32[]{:S(2)}, u32[]{:S(2)}) collective-permute-start(bf16[1024,128]{0,1:T(8,128)(2,1)} %pad_maximum_fusion.8), channel_id=1, source_target_pairs={{0,12},{4,16},{8,20},{12,24},{16,28},{1,13},{5,17},{9,21},{13,25},... | collective-permute-start | bytes 786440 | tf_op jit(solution)/shard_map/ppermute | solution.py:16
  143.4 17.4 collective-permute-start
  326.7 79.1 %copy-start.2 = (bf16[256,2048]{1,0:T(8,128)(2,1)S(1)}, bf16[256,2048]{1,0:T(8,128)(2,1)}, u32[]{:S(2)}) copy-start(bf16[256,2048]{1,0:T(8,128)(2,1)} %param.16) | copy-start | bytes 3145732
  326.8 124.9 %all-gather.22.cloned.1.call-start = ((), (), s32[]{:S(2)}) async-start(), calls=%async_computation.17 | async-start | bytes 6488064 | tf_op jit(solution)/shard_map/all_gather | solution.py:111
  327.3 207.1 %all-gather.18.cloned.1.call-start = ((), (), s32[]{:S(2)}) async-start(), calls=%async_computation.15 | async-start | bytes 5242880 | tf_op jit(solution)/shard_map/all_gather | solution.py:189
  338.0 484.8 %copy-start.25 = (f32[8,1,256]{2,1,0:T(1,128)}, f32[8,1,256]{2,1,0:T(1,128)S(1)}, u32[]{:S(2)}) copy-start(f32[8,1,256]{2,1,0:T(1,128)S(1)} %convert_element_type.231) | copy-start | bytes 24580
  407.5 415.2 %copy-start.35 = (f32[256]{0:T(256)}, f32[256]{0:T(256)S(1)}, u32[]{:S(2)}) copy-start(f32[256]{0:T(256)S(1)} %add_rsqrt_fusion) | copy-start | bytes 3076
  410.2 168.2 %all-gather.20.cloned.1.call-start = ((), (), s32[]{:S(2)}) async-start(), calls=%async_computation.16 | async-start | bytes 6488064 | tf_op jit(solution)/shard_map/all_gather | solution.py:110
  411.0 250.4 %all-gather.26.cloned.1.call-start = ((), (), s32[]{:S(2)}) async-start(), calls=%async_computation.20 | async-start | bytes 5242880 | tf_op jit(solution)/shard_map/all_gather | solution.py:227
  411.2 411.6 %copy-start.42 = (pred[256]{0:T(512)(128)(4,1)}, pred[256]{0:T(512)(128)(4,1)S(1)}, u32[]{:S(2)}) copy-start(pred[256]{0:T(512)(128)(4,1)S(1)} %fusion.81) | copy-start | bytes 772
  412.4 294.0 %all-gather.24.cloned.1.call-start = ((), (), s32[]{:S(2)}) async-start(), calls=%async_computation.18 | async-start | bytes 6488064 | tf_op jit(solution)/shard_map/all_gather | solution.py:112
  413.2 406.8 %reduce-scatter.16.cloned.1.call-start = ((), (), s32[]{:S(2)}) async-start(), calls=%async_computation.21 | async-start | bytes 5242880 | tf_op jit(solution)/shard_map/reduce_scatter | solution.py:236
  743.0 76.9 %copy-start.8 = (bf16[256,2048]{1,0:T(8,128)(2,1)S(1)}, bf16[256,2048]{1,0:T(8,128)(2,1)}, u32[]{:S(2)}) copy-start(bf16[256,2048]{1,0:T(8,128)(2,1)} %reduce-scatter.12.cloned.1.call-done) | copy-start | bytes 3145732
  743.0 163.2 %all-gather.28.cloned.1.call-start = ((), (), s32[]{:S(2)}) async-start(), calls=%async_computation.22 | async-start | bytes 5242880 | tf_op jit(solution)/shard_map/all_gather | solution.py:249
  824.8 681.8 %reduce-scatter.32.cloned.1.call-start = ((), (), s32[]{:S(2)}) async-start(), calls=%async_computation.30 | async-start | bytes 6488064 | tf_op jit(solution)/shard_map/reduce_scatter | solution.py:323
  835.3 673.7 %reduce-scatter.30.cloned.1.call-start = ((), (), s32[]{:S(2)}) async-start(), calls=%async_computation.29 | async-start | bytes 6488064 | tf_op jit(solution)/shard_map/reduce_scatter | solution.py:320
  848.0 663.4 %reduce-scatter.28.cloned.1.call-start = ((), (), s32[]{:S(2)}) async-start(), calls=%async_computation.28 | async-start | bytes 6488064 | tf_op jit(solution)/shard_map/reduce_scatter | solution.py:317
  860.7 45.5 %copy-start.48 = (bf16[512,2048]{1,0:T(8,128)(2,1)S(1)}, bf16[512,2048]{1,0:T(8,128)(2,1)}, u32[]{:S(2)}) copy-start(bf16[512,2048]{1,0:T(8,128)(2,1)} %all-gather.16.cloned.1.call-done) | copy-start | bytes 6291460
  860.8 655.3 %reduce-scatter.22.cloned.1.call-start = ((), (), s32[]{:S(2)}) async-start(), calls=%async_computation.25 | async-start | bytes 294912 | tf_op jit(solution)/shard_map/reduce_scatter | solution.py:302
  942.0 23.6 %copy-start = (f32[1024,5120]{1,0:T(8,128)S(1)}, f32[1024,5120]{1,0:T(8,128)}, u32[]{:S(2)}) copy-start(f32[1024,5120]{1,0:T(8,128)} %get-tuple-element.543) | copy-start | bytes 62914564 | tf_op jit(solution)/shard_map/while
  1009.3 23.7 %copy-start = (f32[1024,5120]{1,0:T(8,128)S(1)}, f32[1024,5120]{1,0:T(8,128)}, u32[]{:S(2)}) copy-start(f32[1024,5120]{1,0:T(8,128)} %get-tuple-element.543) | copy-start | bytes 62914564 | tf_op jit(solution)/shard_map/while
  1454.5 7.1 collective-permute-start.4
  1455.9 10.9 collective-permute-start.7
  1457.2 9.6 collective-permute-start.6
  1458.5 11.1 collective-permute-start.5
  1475.7 76.8 %reduce-scatter.24.cloned.1.call-start = ((), (), s32[]{:S(2)}) async-start(), calls=%async_computation.26 | async-start | bytes 294912 | tf_op jit(solution)/shard_map/reduce_scatter | solution.py:308
  1476.3 121.0 %reduce-scatter.26.cloned.1.call-start = ((), (), s32[]{:S(2)}) async-start(), calls=%async_computation.27 | async-start | bytes 2359296 | tf_op jit(solution)/shard_map/reduce_scatter | solution.py:314
  1482.6 159.7 %reduce-scatter.20.cloned.1.call-start = ((), (), s32[]{:S(2)}) async-start(), calls=%async_computation.24 | async-start | bytes 2359296 | tf_op jit(solution)/shard_map/reduce_scatter | solution.py:296
  1484.1 237.4 %reduce-scatter.18.cloned.1.call-start = ((), (), s32[]{:S(2)}) async-start(), calls=%async_computation.23 | async-start | bytes 5242880 | tf_op jit(solution)/shard_map/reduce_scatter | solution.py:290
  1491.8 309.3 %reduce-scatter.14.cloned.1.call-start = ((), (), s32[]{:S(2)}) async-start(), calls=%async_computation.19 | async-start | bytes 5242880 | tf_op jit(solution)/shard_map/reduce_scatter | solution.py:195
  1508.9 212.5 %copy-start.3 = (bf16[256,2048]{1,0:T(8,128)(2,1)S(1)}, bf16[256,2048]{1,0:T(8,128)(2,1)}, u32[]{:S(2)}) copy-start(bf16[256,2048]{1,0:T(8,128)(2,1)} %param.16) | copy-start | bytes 3145732
  1508.9 212.5 %copy-start.28 = (f32[8,1,256]{2,1,0:T(1,128)S(1)}, f32[8,1,256]{2,1,0:T(1,128)}, u32[]{:S(2)}) copy-start(f32[8,1,256]{2,1,0:T(1,128)} %copy-done.27) | copy-start | bytes 24580
  1508.9 212.5 %copy-start.38 = (f32[256]{0:T(256)S(1)}, f32[256]{0:T(256)}, u32[]{:S(2)}) copy-start(f32[256]{0:T(256)} %copy-done.37) | copy-start | bytes 3076
  1511.3 212.2 %copy-start.39 = (bf16[2048]{0:T(1024)(128)(2,1)S(1)}, bf16[2048]{0:T(1024)(128)(2,1)}, u32[]{:S(2)}) copy-start(bf16[2048]{0:T(1024)(128)(2,1)} %get-tuple-element.268) | copy-start | bytes 12292
  1511.3 289.8 %copy-start.9 = (bf16[256,2048]{1,0:T(8,128)(2,1)S(1)}, bf16[256,2048]{1,0:T(8,128)(2,1)}, u32[]{:S(2)}) copy-start(bf16[256,2048]{1,0:T(8,128)(2,1)} %reduce-scatter.12.cloned.1.call-done) | copy-start | bytes 3145732
  1511.3 289.8 %copy-start.11 = (bf16[256,2048]{1,0:T(8,128)(2,1)S(1)}, bf16[256,2048]{1,0:T(8,128)(2,1)}, u32[]{:S(2)}) copy-start(bf16[256,2048]{1,0:T(8,128)(2,1)} %param.26) | copy-start | bytes 3145732
  1511.4 289.8 %copy-start.26 = (f32[8,1,256]{2,1,0:T(1,128)S(1)}, f32[8,1,256]{2,1,0:T(1,128)}, u32[]{:S(2)}) copy-start(f32[8,1,256]{2,1,0:T(1,128)} %copy-done.25) | copy-start | bytes 24580
  1511.4 289.8 %copy-start.36 = (f32[256]{0:T(256)S(1)}, f32[256]{0:T(256)}, u32[]{:S(2)}) copy-start(f32[256]{0:T(256)} %copy-done.35) | copy-start | bytes 3076
  1511.4 289.8 %copy-start.41 = (f32[256]{0:T(256)S(1)}, f32[256]{0:T(256)}, u32[]{:S(2)}) copy-start(f32[256]{0:T(256)} %copy-done.40) | copy-start | bytes 3076
  1511.4 289.8 %copy-start.43 = (pred[256]{0:T(512)(128)(4,1)S(1)}, pred[256]{0:T(512)(128)(4,1)}, u32[]{:S(2)}) copy-start(pred[256]{0:T(512)(128)(4,1)} %copy-done.42) | copy-start | bytes 772
  (58 other events, 445.0 us)
Sparse Core Ops, SparseCore 0:
  9.9 31.9 all-gather.13
  44.0 80.7 all-gather.11
  126.7 34.0 all-gather.15
  326.9 78.9 reduce-scatter.11
  407.7 43.8 all-gather.21
  453.7 80.7 all-gather.17
  536.5 41.8 all-gather.19
  580.6 80.7 all-gather.25
  663.5 42.8 all-gather.23
  743.1 76.7 reduce-scatter.15
  824.9 81.2 all-gather.27
  909.5 57.5 reduce-scatter.31
  970.9 59.0 reduce-scatter.29
  1033.3 59.0 reduce-scatter.27
  1475.9 40.1 reduce-scatter.21
  1518.9 33.5 reduce-scatter.23
  1556.0 41.1 reduce-scatter.25
  1601.0 41.2 reduce-scatter.19
  1644.7 76.7 reduce-scatter.17
  1723.6 77.5 reduce-scatter.13
where the time goes:
time: 1820 us; the launch traced here: 1810 us
  waiting for transfers between devices  805 us (44%)
  matrix products  580 us (32%)
  other arithmetic  242 us (13%)
  local copies, waits for them, and re-layouts  83.9 us (5%)
  blocking collectives  66.9 us (4%)
  starting transfers between devices  18.5 us (1%)
    dot_general x29, matrix products, outer_cols(): lax.dot_general(left, right, (((1,), (1,)), ((), ())), preferred_element_...  305 us
    convert_element_type x8, other arithmetic, head_backward(): grad_scores = (attn_probs * (grad_probs - jnp.sum(attn_probs * grad_probs...  148 us
    dot_general x21, matrix products, inner_rows(): lax.dot_general(left, right, (((0,), (0,)), ((), ())), preferred_element_...  108 us
    all_gather x1, waiting for transfers between devices, local(): rows_second = lax.all_gather(scaled_second, 'tp', axis=0, tiled=True)  82.9 us
    reduce_scatter x1, waiting for transfers between devices, local(): lax.psum_scatter(outer_cols(grad_inner, w_inner).astype(jnp.bfloat16), 't...  77.3 us
    reduce_scatter x1, waiting for transfers between devices, local(): lax.psum_scatter((outer_cols(grad_gate_low, full_gate) + outer_cols(grad_...  76.9 us
    all_gather x1, waiting for transfers between devices, local(): rows_first = lax.all_gather(scaled_first, 'tp', axis=0, tiled=True)  76.6 us
    all_gather x1, waiting for transfers between devices, local(): grad_down_rows = lax.all_gather(grad_low, 'tp', axis=0, tiled=True)  71.4 us
  transfers between devices with their start and end apart: 28, of which 18 were waited for; matrix products, arithmetic and copies ran while one was open for 45% of the time, Pallas kernels for 0%

commit v1 on v0

--- a/solution.py
+++ b/solution.py
@@ -1,6 +1,8 @@
 import jax
 import jax.numpy as jnp
 from jax import lax
+from jax.experimental import pallas as pl
+from jax.experimental.pallas import tpu as pltpu
 from jax.sharding import PartitionSpec as P
 
 HEAD_DIM = 64
@@ -19,7 +21,7 @@
 def stream_layout(slots, lengths):
     seq_count = lengths.shape[0]
     seq_index = jnp.arange(seq_count, dtype=jnp.int32)
-    ends = jnp.cumsum(lengths)
+    ends = jnp.sum(jnp.where(seq_index[:, None] >= seq_index[None, :], lengths[None, :], 0), axis=1)
     starts = ends - lengths
     segment = jnp.sum((slots[:, None] >= ends[None, :]).astype(jnp.int32), axis=1)
     start_of = jnp.sum(
@@ -346,7 +348,764 @@
     )
 
 
+MESH = pl.DeviceIdType.MESH
+CORE, ALONG_X, ALONG_Y = 1, 2, 4
+PARTS = 4
+
+
+def greet(partners):
+    barrier = pltpu.get_barrier_semaphore()
+    for partner in partners:
+        pl.semaphore_signal(barrier, inc=1, device_id=partner, device_id_type=MESH)
+    pl.semaphore_wait(barrier, len(partners))
+
+
+def remote(source, target, sent, arrived, partner):
+    return pltpu.make_async_remote_copy(
+        src_ref=source,
+        dst_ref=target,
+        send_sem=sent,
+        recv_sem=arrived,
+        device_id=partner,
+        device_id_type=MESH,
+    )
+
+
+def comm_params(number, vmem=None):
+    return pltpu.CompilerParams(
+        collective_id=number, has_side_effects=True, vmem_limit_bytes=vmem
+    )
+
+
+ANYWHERE = pl.BlockSpec(memory_space=pl.ANY)
+IN_VMEM = pl.BlockSpec(memory_space=pltpu.VMEM)
+
+
+def plane_gather(rows, number):
+    height, width = rows.shape
+    piece = height // PARTS
+
+    def kernel(x_ref, o_ref, local_sem, sent, arrived):
+        f = lax.axis_index("fsdp")
+        t = lax.axis_index("tp")
+        near = [(f ^ k, t) for k in (CORE, ALONG_X, ALONG_Y)]
+        greet(near)
+        keep = pltpu.make_async_copy(
+            x_ref, o_ref.at[pl.ds(pl.multiple_of(f * height, height), height)], local_sem
+        )
+        keep.start()
+        copies = []
+
+        def send(owner, j, way, slot, first=False):
+            place = o_ref.at[pl.ds(pl.multiple_of(owner * height + j * piece, piece), piece)]
+            source = x_ref.at[pl.ds(j * piece, piece)] if first else place
+            c = remote(source, place, sent.at[slot, j], arrived.at[slot, j], near[way])
+            c.start()
+            copies.append(c)
+            return c
+
+        along = {}
+        for k in range(PARTS):
+            jx, jy = k, (k + PARTS // 2) % PARTS
+            along[1, jx] = send(f, jx, 1, 1, True)
+            along[2, jy] = send(f, jy, 2, 2, True)
+        own = [send(f, j, 0, 0, True) for j in range(PARTS)]
+        passed = {}
+        for k in range(PARTS):
+            jx, jy = k, (k + PARTS // 2) % PARTS
+            along[1, jx].wait_recv()
+            if jx < PARTS // 2:
+                passed[jx] = send(f ^ ALONG_X, jx, 2, 6)
+            passed["x", jx] = send(f ^ ALONG_X, jx, 0, 3)
+            along[2, jy].wait_recv()
+            if jy >= PARTS // 2:
+                passed[jy] = send(f ^ ALONG_Y, jy, 1, 6)
+            passed["y", jy] = send(f ^ ALONG_Y, jy, 0, 4)
+        for k in range(PARTS // 2):
+            for j in (k, k + PARTS // 2):
+                passed[j].wait_recv()
+                passed["d", j] = send(f ^ ALONG_X ^ ALONG_Y, j, 0, 5)
+        for j in range(PARTS):
+            own[j].wait_recv()
+            for kind in "xyd":
+                passed[kind, j].wait_recv()
+        for c in copies:
+            c.wait_send()
+        keep.wait()
+
+    return pl.pallas_call(
+        kernel,
+        out_shape=jax.ShapeDtypeStruct((8 * height, width), rows.dtype),
+        in_specs=[ANYWHERE],
+        out_specs=ANYWHERE,
+        scratch_shapes=[
+            pltpu.SemaphoreType.DMA,
+            pltpu.SemaphoreType.DMA((7, PARTS)),
+            pltpu.SemaphoreType.DMA((7, PARTS)),
+        ],
+        compiler_params=comm_params(number),
+        name=f"plane_gather_{number}",
+    )(rows)
+
+
+def plane_sum(parts, number):
+    total, width = parts.shape
+    height = total // 8
+    half = height // 2
+
+    def kernel(p_ref, o_ref, ra, s, rx, ry, rlast, sent, arrived):
+        f = lax.axis_index("fsdp")
+        t = lax.axis_index("tp")
+        core, along_x, along_y = [(f ^ k, t) for k in (CORE, ALONG_X, ALONG_Y)]
+        greet((core, along_x, along_y))
+        masks = (ALONG_X ^ ALONG_Y, ALONG_X, ALONG_Y, 0)
+
+        def chunk(owner):
+            return p_ref.at[pl.ds(pl.multiple_of(owner * height, height), height)]
+
+        copies = []
+
+        def send(source, target, slot, partner):
+            c = remote(source, target, sent.at[slot], arrived.at[slot], partner)
+            c.start()
+            copies.append(c)
+            return c
+
+        first = [send(chunk(f ^ CORE ^ m), ra.at[i], i, core) for i, m in enumerate(masks)]
+        top, low = pl.ds(0, half), pl.ds(half, half)
+
+        def gather_own(i):
+            first[i].wait_recv()
+            s[i] = (
+                chunk(f ^ masks[i])[...].astype(jnp.float32) + ra[i].astype(jnp.float32)
+            ).astype(jnp.bfloat16)
+
+        gather_own(0)
+        x0 = send(s.at[0, top], rx.at[0], 4, along_x)
+        y0 = send(s.at[0, low], ry.at[0], 5, along_y)
+        gather_own(1)
+        x1 = send(s.at[1, top], rx.at[1], 6, along_x)
+        gather_own(2)
+        y1 = send(s.at[2, low], ry.at[1], 7, along_y)
+        gather_own(3)
+        x0.wait_recv()
+        s[2, top] = (s[2, top].astype(jnp.float32) + rx[0].astype(jnp.float32)).astype(jnp.bfloat16)
+        y2 = send(s.at[2, top], rlast.at[0], 8, along_y)
+        y0.wait_recv()
+        s[1, low] = (s[1, low].astype(jnp.float32) + ry[0].astype(jnp.float32)).astype(jnp.bfloat16)
+        x2 = send(s.at[1, low], rlast.at[1], 9, along_x)
+        x1.wait_recv()
+        o_ref[top] = s[3, top].astype(jnp.float32) + rx[1].astype(jnp.float32)
+        y1.wait_recv()
+        o_ref[low] = s[3, low].astype(jnp.float32) + ry[1].astype(jnp.float32)
+        y2.wait_recv()
+        o_ref[top] += rlast[0].astype(jnp.float32)
+        x2.wait_recv()
+        o_ref[low] += rlast[1].astype(jnp.float32)
+        for c in copies:
+            c.wait_send()
+
+    return pl.pallas_call(
+        kernel,
+        out_shape=jax.ShapeDtypeStruct((height, width), jnp.float32),
+        in_specs=[IN_VMEM],
+        out_specs=IN_VMEM,
+        scratch_shapes=[
+            pltpu.VMEM((4, height, width), jnp.bfloat16),
+            pltpu.VMEM((4, height, width), jnp.bfloat16),
+            pltpu.VMEM((2, half, width), jnp.bfloat16),
+            pltpu.VMEM((2, half, width), jnp.bfloat16),
+            pltpu.VMEM((2, half, width), jnp.bfloat16),
+            pltpu.SemaphoreType.DMA((10,)),
+            pltpu.SemaphoreType.DMA((10,)),
+        ],
+        compiler_params=comm_params(number, 48 << 20),
+        name=f"plane_sum_{number}",
+    )(parts)
+
+
+def plane_exchange(arrays, out_shapes, slices, number):
+    count = len(arrays)
+    pairs = len(slices(0, 0, None, None))
+
+    def kernel(*refs):
+        sources, targets = refs[:count], refs[count : count + len(out_shapes)]
+        local_sem, sent, arrived = refs[-3:]
+        f = lax.axis_index("fsdp")
+        t = lax.axis_index("tp")
+        greet([(f ^ k, t) for k in range(1, 8)])
+        copies = []
+        for k in (6, 7, 2, 4, 3, 5, 1):
+            j = f ^ k
+            for i, (source, target) in enumerate(slices(j, f, sources, targets)):
+                c = remote(source, target, sent.at[k, i], arrived.at[k, i], (j, t))
+                c.start()
+                copies.append(c)
+        kept = []
+        for i, (source, target) in enumerate(slices(f, f, sources, targets)):
+            c = pltpu.make_async_copy(source, target, local_sem.at[i])
+            c.start()
+            kept.append(c)
+        for c in kept + copies:
+            c.wait()
+
+    return pl.pallas_call(
+        kernel,
+        out_shape=[jax.ShapeDtypeStruct(shape, jnp.bfloat16) for shape in out_shapes],
+        in_specs=[ANYWHERE] * count,
+        out_specs=[ANYWHERE] * len(out_shapes),
+        scratch_shapes=[
+            pltpu.SemaphoreType.DMA((pairs,)),
+            pltpu.SemaphoreType.DMA((8, pairs)),
+            pltpu.SemaphoreType.DMA((8, pairs)),
+        ],
+        compiler_params=comm_params(number),
+        name=f"plane_exchange_{number}",
+    )(*arrays)
+
+
+def columns(index, width):
+    return pl.ds(pl.multiple_of(index * width, width), width)
+
+
+def pair_gather(pair, number):
+    rows, width = pair.shape
+    half = rows // 2
+
+    def kernel(x_ref, o_ref, local_sem, sent, arrived):
+        f = lax.axis_index("fsdp")
+        t = lax.axis_index("tp")
+        mine = pl.ds(pl.multiple_of(lax.rem(f, 2) * half, half), half)
+        others = [(f, lax.rem(t + k, 4)) for k in (1, 2, 3)]
+        greet(others + [(f ^ CORE, t)])
+        keep = pltpu.make_async_copy(x_ref, o_ref.at[t], local_sem)
+        keep.start()
+        out = []
+        for k in (2, 1, 3):
+            c = remote(
+                x_ref.at[mine], o_ref.at[t, mine], sent.at[k], arrived.at[k], (f, lax.rem(t + k, 4))
+            )
+            c.start()
+            out.append((k, c))
+        on = []
+        for k, c in sorted(out, key=lambda item: item[0]):
+            c.wait_recv()
+            place = o_ref.at[lax.rem(t + 4 - k, 4), mine]
+            d = remote(place, place, sent.at[3 + k], arrived.at[3 + k], (f ^ CORE, t))
+            d.start()
+            on.append(d)
+        for d in on:
+            d.wait()
+        for k, c in out:
+            c.wait_send()
+        keep.wait()
+
+    return pl.pallas_call(
+        kernel,
+        out_shape=jax.ShapeDtypeStruct((4, rows, width), pair.dtype),
+        in_specs=[ANYWHERE],
+        out_specs=ANYWHERE,
+        scratch_shapes=[
+            pltpu.SemaphoreType.DMA,
+            pltpu.SemaphoreType.DMA((7,)),
+            pltpu.SemaphoreType.DMA((7,)),
+        ],
+        compiler_params=comm_params(number),
+        name=f"pair_gather_{number}",
+    )(pair)
+
+
+def pair_sum(parts, number):
+    _, chunks, height, width = parts.shape
+    half = chunks // 2
+
+    def kernel(p_ref, o_ref, ra, s, rz, sent, arrived):
+        f = lax.axis_index("fsdp")
+        t = lax.axis_index("tp")
+        side = lax.rem(f, 2)
+        mine, other = pl.ds(side * half, half), pl.ds((1 - side) * half, half)
+        core = (f ^ CORE, t)
+        greet([(f, lax.rem(t + k, 4)) for k in (1, 2, 3)] + [core])
+        first = []
+        for k in (2, 1, 3, 0):
+            plane = lax.rem(t + k, 4)
+            c = remote(p_ref.at[plane, other], ra.at[k], sent.at[k], arrived.at[k], core)
+            c.start()
+            first.append((k, c))
+        out = []
+        for k, c in first:
+            c.wait_recv()
+            plane = lax.rem(t + k, 4)
+            total = p_ref[plane, mine].astype(jnp.float32) + ra[k].astype(jnp.float32)
+            if k:
+                s[k] = total.astype(jnp.bfloat16)
+                d = remote(s.at[k], rz.at[k], sent.at[3 + k], arrived.at[3 + k], (f, plane))
+                d.start()
+                out.append((k, d))
+            else:
+                o_ref[mine] = total
+        for k, d in out:
+            d.wait_recv()
+            o_ref[mine] += rz[k].astype(jnp.float32)
+        back = remote(o_ref.at[mine], o_ref.at[mine], sent.at[7], arrived.at[7], core)
+        back.start()
+        back.wait()
+        for k, c in first + out:
+            c.wait_send()
+
+    return pl.pallas_call(
+        kernel,
+        out_shape=jax.ShapeDtypeStruct((chunks, height, width), jnp.float32),
+        in_specs=[IN_VMEM],
+        out_specs=IN_VMEM,
+        scratch_shapes=[
+            pltpu.VMEM((4, half, height, width), jnp.bfloat16),
+            pltpu.VMEM((4, half, height, width), jnp.bfloat16),
+            pltpu.VMEM((4, half, height, width), jnp.bfloat16),
+            pltpu.SemaphoreType.DMA((8,)),
+            pltpu.SemaphoreType.DMA((8,)),
+        ],
+        compiler_params=comm_params(number, 32 << 20),
+        name=f"pair_sum_{number}",
+    )(parts)
+
+
+def dot_nn(left, right):
+    return jnp.dot(left, right, preferred_element_type=jnp.float32)
+
+
+def seen_keys(begin_row, first_key, first_query, shape):
+    key_slot = first_key + lax.broadcasted_iota(jnp.int32, shape, 0)
+    query_slot = first_query + lax.broadcasted_iota(jnp.int32, (1, shape[1]), 1)
+    return (key_slot <= query_slot) & (key_slot >= begin_row)
+
+
+def head_lanes(block, heads):
+    return jnp.concatenate([block[h * HEAD_DIM : (h + 1) * HEAD_DIM] for h in range(heads)], axis=1)
+
+
+def attend(info, begins, queries, pair):
+    depth, slots = queries.shape
+    heads = depth // HEAD_DIM
+    size = slots // 8
+    span = heads * size
+
+    def kernel(info_ref, begin_ref, q_ref, kv_ref, o_ref, l_ref, q_s, m_s, t_s, a_s):
+        f = pl.program_id(0)
+        low, middle, own = info_ref[f, 0], info_ref[f, 1], info_ref[f, 2]
+        q_s[...] = head_lanes(q_ref[...], heads)
+        m_s[...] = jnp.full_like(m_s, -1e30)
+        t_s[...] = jnp.zeros_like(t_s)
+        a_s[...] = jnp.zeros_like(a_s)
+
+        def step(g, masked):
+            block = kv_ref[lax.rem(g, 4), pl.ds(pl.multiple_of(lax.div(g, 4) * size, size), size)]
+            keys, values = block[:, :HEAD_DIM], block[:, HEAD_DIM:]
+            value_cols = values.astype(jnp.float32).T.astype(jnp.bfloat16)
+            if masked:
+                seen = seen_keys(begin_ref[0], g * size, own * size, (size, size))
+            for h in range(heads):
+                lanes = pl.ds(h * size, size)
+                scores = dot_nn(keys, q_s[:, lanes])
+                if masked:
+                    scores = jnp.where(seen, scores, -1e30)
+                largest = m_s[:, lanes]
+                higher = jnp.maximum(largest, jnp.max(scores, axis=0, keepdims=True))
+                raised = jnp.exp(scores - higher)
+                fade = jnp.exp(largest - higher)
+                m_s[:, lanes] = higher
+                t_s[:, lanes] = t_s[:, lanes] * fade + jnp.sum(raised, axis=0, keepdims=True)
+                a_s[:, lanes] = a_s[:, lanes] * fade + dot_nn(
+                    value_cols, raised.astype(jnp.bfloat16)
+                )
+
+        def masked_step(g, carry):
+            step(g, True)
+            return carry
+
+        def plain_step(g, carry):
+            step(g, False)
+            return carry
+
+        step(own, True)
+        lax.fori_loop(low, middle, masked_step, 0)
+        lax.fori_loop(middle, own, plain_step, 0)
+        result = a_s[...] / t_s[...]
+        for h in range(heads):
+            o_ref[h * HEAD_DIM : (h + 1) * HEAD_DIM] = result[:, h * size : (h + 1) * size].astype(
+                jnp.bfloat16
+            )
+        l_ref[0] = m_s[...] + jnp.log(t_s[...])
+
+    return pl.pallas_call(
+        kernel,
+        grid_spec=pltpu.PrefetchScalarGridSpec(
+            num_scalar_prefetch=1,
+            grid=(8,),
+            in_specs=[
+                pl.BlockSpec((1, 1, size), lambda f, info: (f, 0, 0)),
+                pl.BlockSpec((depth, size), lambda f, info: (0, f)),
+                pl.BlockSpec((4, slots, 2 * HEAD_DIM), lambda f, info: (0, 0, 0)),
+            ],
+            out_specs=[
+                pl.BlockSpec((depth, size), lambda f, info: (0, f)),
+                pl.BlockSpec((1, 1, span), lambda f, info: (f, 0, 0)),
+            ],
+            scratch_shapes=[
+                pltpu.VMEM((HEAD_DIM, span), jnp.bfloat16),
+                pltpu.VMEM((1, span), jnp.float32),
+                pltpu.VMEM((1, span), jnp.float32),
+                pltpu.VMEM((HEAD_DIM, span), jnp.float32),
+            ],
+        ),
+        out_shape=[
+            jax.ShapeDtypeStruct((depth, slots), jnp.bfloat16),
+            jax.ShapeDtypeStruct((8, 1, span), jnp.float32),
+        ],
+        compiler_params=pltpu.CompilerParams(vmem_limit_bytes=40 << 20),
+        cost_estimate=pl.CostEstimate(
+            flops=30_000_000_000, bytes_accessed=6_000_000, transcendentals=16_000_000
+        ),
+        name="attend",
+    )(info, begins, queries, pair)
+
+
+def attend_back(info, begins, queries, pair, outputs, grads, totals):
+    depth, slots = queries.shape
+    heads = depth // HEAD_DIM
+    size = slots // 8
+    span = heads * size
+
+    def kernel(
+        info_ref, begin_ref, q_ref, kv_ref, o_ref, g_ref, l_ref, dq_ref, dkv_ref, q_s, g_s, d_s, a_s, w_s
+    ):
+        f = pl.program_id(0)
+        low, middle, own = info_ref[f, 0], info_ref[f, 1], info_ref[f, 2]
+
+        @pl.when(f == 0)
+        def _():
+            w_s[...] = jnp.zeros_like(w_s)
+
+        q_s[...] = head_lanes(q_ref[...], heads)
+        g_s[...] = head_lanes(g_ref[...], heads)
+        out_lanes = head_lanes(o_ref[...], heads).astype(jnp.float32)
+        d_s[...] = jnp.sum(out_lanes * g_s[...].astype(jnp.float32), axis=0, keepdims=True)
+        a_s[...] = jnp.zeros_like(a_s)
+
+        def step(g, masked):
+            block = kv_ref[lax.rem(g, 4), pl.ds(pl.multiple_of(lax.div(g, 4) * size, size), size)]
+            keys, values = block[:, :HEAD_DIM], block[:, HEAD_DIM:]
+            key_cols = keys.astype(jnp.float32).T.astype(jnp.bfloat16)
+            if masked:
+                seen = seen_keys(begin_ref[0], g * size, own * size, (size, size))
+            grad_keys = jnp.zeros((HEAD_DIM, size), jnp.float32)
+            grad_values = jnp.zeros((HEAD_DIM, size), jnp.float32)
+            for h in range(heads):
+                lanes = pl.ds(h * size, size)
+                query, grad = q_s[:, lanes], g_s[:, lanes]
+                raised = jnp.exp(dot_nn(keys, query) - l_ref[0, :, lanes])
+                if masked:
+                    raised = jnp.where(seen, raised, 0.0)
+                grad_probs = dot_nn(values, grad)
+                scores = (raised * (grad_probs - d_s[:, lanes])).astype(jnp.bfloat16)
+                grad_values += outer_cols(grad, raised.astype(jnp.bfloat16))
+                grad_keys += outer_cols(query, scores)
+                a_s[:, lanes] += dot_nn(key_cols, scores)
+            w_s[lax.rem(g, 4), lax.div(g, 4), :HEAD_DIM] += grad_keys
+            w_s[lax.rem(g, 4), lax.div(g, 4), HEAD_DIM:] += grad_values
+
+        def masked_step(g, carry):
+            step(g, True)
+            return carry
+
+        def plain_step(g, carry):
+            step(g, False)
+            return carry
+
+        step(own, True)
+        lax.fori_loop(low, middle, masked_step, 0)
+        lax.fori_loop(middle, own, plain_step, 0)
+        result = a_s[...] * HEAD_DIM ** (-0.5)
+        for h in range(heads):
+            dq_ref[h * HEAD_DIM : (h + 1) * HEAD_DIM] = result[:, h * size : (h + 1) * size]
+
+        @pl.when(f == 7)
+        def _():
+            dkv_ref[...] = w_s[...].astype(jnp.bfloat16)
+
+    return pl.pallas_call(
+        kernel,
+        grid_spec=pltpu.PrefetchScalarGridSpec(
+            num_scalar_prefetch=1,
+            grid=(8,),
+            in_specs=[
+                pl.BlockSpec((1, 1, size), lambda f, info: (f, 0, 0)),
+                pl.BlockSpec((depth, size), lambda f, info: (0, f)),
+                pl.BlockSpec((4, slots, 2 * HEAD_DIM), lambda f, info: (0, 0, 0)),
+                pl.BlockSpec((depth, size), lambda f, info: (0, f)),
+                pl.BlockSpec((depth, size), lambda f, info: (0, f)),
+                pl.BlockSpec((1, 1, span), lambda f, info: (f, 0, 0)),
+            ],
+            out_specs=[
+                pl.BlockSpec((depth, size), lambda f, info: (0, f)),
+                pl.BlockSpec((4, 8, 2 * HEAD_DIM, size), lambda f, info: (0, 0, 0, 0)),
+            ],
+            scratch_shapes=[
+                pltpu.VMEM((HEAD_DIM, span), jnp.bfloat16),
+                pltpu.VMEM((HEAD_DIM, span), jnp.bfloat16),
+                pltpu.VMEM((1, span), jnp.float32),
+                pltpu.VMEM((HEAD_DIM, span), jnp.float32),
+                pltpu.VMEM((4, 8, 2 * HEAD_DIM, size), jnp.float32),
+            ],
+        ),
+        out_shape=[
+            jax.ShapeDtypeStruct((depth, slots), jnp.float32),
+            jax.ShapeDtypeStruct((4, 8, 2 * HEAD_DIM, size), jnp.bfloat16),
+        ],
+        compiler_params=pltpu.CompilerParams(vmem_limit_bytes=40 << 20),
+        cost_estimate=pl.CostEstimate(
+            flops=70_000_000_000, bytes_accessed=10_000_000, transcendentals=16_000_000
+        ),
+        name="attend_back",
+    )(info, begins, queries, pair, outputs, grads, totals)
+
+
+def turn(values, cosine, sine_table):
+    heads = values.shape[0] // HEAD_DIM
+    split = values.reshape(heads, 2, HEAD_DIM // 2, values.shape[1])
+    first, second = split[:, 0], split[:, 1]
+    turned = jnp.stack(
+        [first * cosine - second * sine_table, second * cosine + first * sine_table], axis=1
+    )
+    return turned.reshape(values.shape)
+
+
+def turn_back(values, cosine, sine_table):
+    return turn(values, cosine, -sine_table)
+
+
+def segment_begins(slots, lengths):
+    seq_index = jnp.arange(lengths.shape[0], dtype=jnp.int32)
+    ends = jnp.sum(jnp.where(seq_index[:, None] >= seq_index[None, :], lengths[None, :], 0), axis=1)
+    passed = slots[:, None] >= ends[None, :]
+    begins = jnp.sum(jnp.where(passed, lengths[None, :], 0), axis=1)
+    return begins, slots < ends[-1]
+
+
+def local_plane(
+    tokens,
+    attn_gain,
+    query_weight,
+    key_weight,
+    value_weight,
+    output_weight,
+    mlp_gain,
+    gate_weight,
+    up_weight,
+    down_weight,
+    out_grad,
+    lengths,
+):
+    size, width = tokens.shape
+    f = lax.axis_index("fsdp")
+    t = lax.axis_index("tp")
+    block = query_weight.shape[0]
+    head_rows = query_weight.shape[1] // 2
+    units = gate_weight.shape[1] // 8
+    bf16, f32 = jnp.bfloat16, jnp.float32
+
+    attn_stack = jnp.concatenate(
+        [query_weight.T, key_weight.T, value_weight.T, output_weight], axis=0
+    )
+    attn_all = lax.all_gather(attn_stack, "tp", axis=0, tiled=False)
+    hidden_parts = [w.reshape(8, units, block) for w in (gate_weight.T, up_weight.T, down_weight)]
+
+    def hidden_slices(j, f, sources, targets):
+        if sources is None:
+            return [None] * 3
+        return [(s.at[j], o.at[:, columns(f, block)]) for s, o in zip(sources, targets)]
+
+    gate_part, up_part, down_part = plane_exchange(
+        hidden_parts, [(units, width)] * 3, hidden_slices, 1
+    )
+    gate_rows = lax.all_gather(gate_part, "tp", axis=0, tiled=True)
+    up_rows = lax.all_gather(up_part, "tp", axis=0, tiled=True)
+    down_rows = lax.all_gather(down_part, "tp", axis=0, tiled=True)
+
+    gains = lax.all_gather(jnp.stack([attn_gain, mlp_gain]), "fsdp", axis=0, tiled=False)
+    gains = jnp.moveaxis(gains, 0, 1).reshape(2, width).astype(f32)
+    gain_first, gain_second = gains[0:1], gains[1:2]
+
+    my_slots = (f * 4 + t) * size + jnp.arange(size, dtype=jnp.int32)
+    _, my_valid = segment_begins(my_slots, lengths)
+    valid_rows = my_valid[:, None]
+    chunk_index = jnp.arange(8, dtype=jnp.int32) * 4 + t
+    plane_slots = (chunk_index[:, None] * size + jnp.arange(size, dtype=jnp.int32)[None, :]).reshape(-1)
+    begins, plane_valid = segment_begins(plane_slots, lengths)
+    positions = jnp.where(plane_valid, plane_slots - begins, 0)
+    begins = begins.reshape(8, 1, size)
+    info = jnp.stack(
+        [
+            begins[:, 0, 0] // size,
+            jnp.minimum((begins[:, 0, size - 1] + size - 1) // size, chunk_index),
+            chunk_index,
+        ],
+        axis=1,
+    ).astype(jnp.int32)
+    ladder = jnp.arange(HEAD_DIM // 2).astype(f32)
+    frequency = 10000.0 ** (-2.0 * ladder / HEAD_DIM)
+    angles = positions.astype(f32)[None, :] * frequency[:, None]
+    cosine, sine_table = jnp.cos(angles), jnp.sin(angles)
+
+    tokens_wide = tokens.astype(f32)
+    inverse_first = lax.rsqrt(jnp.mean(tokens_wide * tokens_wide, axis=1, keepdims=True) + epsilon)
+    normed_first = tokens_wide * inverse_first
+    scaled_first = (normed_first * gain_first).astype(bf16)
+    rows_first = plane_gather(scaled_first, 2)
+
+    def attn_slices(j, f, sources, targets):
+        if sources is None:
+            return [None] * 3
+        quarter, side = lax.div(j, 2), lax.rem(j, 2)
+        (source,), (target,) = sources, targets
+        place = columns(f, block)
+        pair_rows = 2 * HEAD_DIM
+        return [
+            (
+                source.at[quarter, pl.ds(pl.multiple_of(side * head_rows, head_rows), head_rows)],
+                target.at[pl.ds(0, head_rows), place],
+            ),
+            (
+                source.at[quarter, pl.ds(2 * head_rows, pair_rows)],
+                target.at[pl.ds(head_rows, pair_rows), place],
+            ),
+            (
+                source.at[
+                    quarter,
+                    pl.ds(
+                        pl.multiple_of(2 * head_rows + pair_rows + side * head_rows, 2 * HEAD_DIM),
+                        head_rows,
+                    ),
+                ],
+                target.at[pl.ds(head_rows + pair_rows, head_rows), place],
+            ),
+        ]
+
+    (attn_rows,) = plane_exchange(
+        [attn_all], [(2 * head_rows + 2 * HEAD_DIM, width)], attn_slices, 3
+    )
+    inner_end = head_rows + 2 * HEAD_DIM
+    inner_rows_w, output_rows = attn_rows[:inner_end], attn_rows[inner_end:]
+    projected = outer_cols(inner_rows_w, rows_first)
+    queries = (turn(projected[:head_rows], cosine, sine_table).astype(bf16) * 0.125).astype(bf16)
+    keys = turn(projected[head_rows : head_rows + HEAD_DIM], cosine, sine_table)
+    pair_local = jnp.concatenate([keys, projected[head_rows + HEAD_DIM :]], axis=0).astype(bf16).T
+    pair = pair_gather(pair_local, 4)
+    attended, totals = attend(info, begins, queries, pair)
+    attn_share = plane_sum(inner_rows(attended, output_rows).astype(bf16), 5)
+    middle = tokens_wide + attn_share
+    inverse_second = lax.rsqrt(jnp.mean(middle * middle, axis=1, keepdims=True) + epsilon)
+    normed_second = middle * inverse_second
+    scaled_second = (normed_second * gain_second).astype(bf16)
+    rows_second = plane_gather(scaled_second, 6)
+
+    gate_proj = outer_cols(gate_rows, rows_second)
+    up_proj = outer_cols(up_rows, rows_second)
+    gate_sigmoid = jax.nn.sigmoid(gate_proj)
+    gate_active = gate_proj * gate_sigmoid
+    hidden = (gate_active * up_proj).astype(bf16)
+    mlp_share = plane_sum(inner_rows(hidden, down_rows).astype(bf16), 7)
+    layer_out = jnp.where(valid_rows, middle + mlp_share, 0.0).astype(bf16)
+
+    grad_rows_own = jnp.where(valid_rows, out_grad.astype(f32), 0.0)
+    grad_rows = plane_gather(grad_rows_own.astype(bf16), 8)
+    grad_down_w = dot_nn(hidden, grad_rows).astype(bf16)
+    grad_hidden = outer_cols(down_rows, grad_rows)
+    grad_up_low = (grad_hidden * gate_active).astype(bf16)
+    grad_gate_low = (
+        grad_hidden * up_proj * gate_sigmoid * (1.0 + gate_proj * (1.0 - gate_sigmoid))
+    ).astype(bf16)
+    grad_gate_w = dot_nn(grad_gate_low, rows_second).astype(bf16)
+    grad_up_w = dot_nn(grad_up_low, rows_second).astype(bf16)
+    grad_second = plane_sum(
+        (inner_rows(grad_gate_low, gate_rows) + inner_rows(grad_up_low, up_rows)).astype(bf16), 9
+    )
+    hidden_grads = [
+        lax.psum_scatter(g, "tp", scatter_dimension=0, tiled=True)
+        for g in (grad_down_w, grad_gate_w, grad_up_w)
+    ]
+    gain_second_part = jnp.sum(grad_second * normed_second, axis=0)
+    grad_middle = grad_rows_own + norm_back(grad_second, gain_second, normed_second, inverse_second)
+    middle_rows = plane_gather(grad_middle.astype(bf16), 10)
+    grad_output_w = dot_nn(attended, middle_rows).astype(bf16)
+    grad_attended = outer_cols(output_rows, middle_rows).astype(bf16)
+    grad_queries, grad_pair_parts = attend_back(
+        info, begins, queries, pair, attended, grad_attended, totals
+    )
+    grad_pair = pair_sum(grad_pair_parts, 11)
+    grad_pair = jnp.moveaxis(grad_pair, 0, 1).reshape(2 * HEAD_DIM, 8 * size)
+    grad_query_low = turn_back(grad_queries, cosine, sine_table).astype(bf16)
+    grad_key_low = turn_back(grad_pair[:HEAD_DIM], cosine, sine_table)
+    first_core = lax.rem(f, 2) == 0
+    grad_single = jnp.where(first_core, grad_key_low, grad_pair[HEAD_DIM:]).astype(bf16)
+    grad_inner = jnp.concatenate([grad_query_low, grad_single], axis=0)
+    single_rows = jnp.where(
+        first_core,
+        attn_rows[head_rows : head_rows + HEAD_DIM],
+        attn_rows[head_rows + HEAD_DIM : inner_end],
+    )
+    single_weights = jnp.concatenate([attn_rows[:head_rows], single_rows], axis=0)
+    grad_first = plane_sum(inner_rows(grad_inner, single_weights).astype(bf16), 12)
+    grad_inner_w = dot_nn(grad_inner, rows_first).astype(bf16)
+    gain_first_part = jnp.sum(grad_first * normed_first, axis=0)
+    tokens_grad = grad_middle + norm_back(grad_first, gain_first, normed_first, inverse_first)
+
+    single_end = head_rows + HEAD_DIM
+    attn_grads = jnp.concatenate([grad_inner_w, grad_output_w], axis=0)
+
+    def attn_back(j, f, sources, targets):
+        if sources is None:
+            return [None]
+        return [(sources[0].at[:, columns(j, block)], targets[0].at[f])]
+
+    (attn_parts,) = plane_exchange(
+        [attn_grads], [(8, single_end + head_rows, block)], attn_back, 13
+    )
+    attn_own = lax.psum_scatter(
+        attn_parts.reshape(4 * 2 * (single_end + head_rows), block),
+        "tp",
+        scatter_dimension=0,
+        tiled=True,
+    ).reshape(2, single_end + head_rows, block)
+
+    def hidden_back(j, f, sources, targets):
+        if sources is None:
+            return [None] * 3
+        return [(s.at[:, columns(j, block)], o.at[f]) for s, o in zip(sources, targets)]
+
+    own_down, own_gate, own_up = plane_exchange(
+        hidden_grads, [(8, units, block)] * 3, hidden_back, 14
+    )
+    gain_sums = lax.psum(jnp.stack([gain_first_part, gain_second_part]), ("fsdp", "tp"))
+    gain_sums = lax.dynamic_slice_in_dim(gain_sums, f * block, block, 1)
+    return (
+        layer_out,
+        tokens_grad,
+        gain_sums[0],
+        attn_own[:, :head_rows].reshape(2 * head_rows, block).T.astype(f32),
+        attn_own[0, head_rows:single_end].T.astype(f32),
+        attn_own[1, head_rows:single_end].T.astype(f32),
+        attn_own[:, single_end:].reshape(2 * head_rows, block).astype(f32),
+        gain_sums[1],
+        own_gate.reshape(8 * units, block).T.astype(f32),
+        own_up.reshape(8 * units, block).T.astype(f32),
+        own_down.reshape(8 * units, block).astype(f32),
+    )
+
+
 def solution(mesh):
+    plane = dict(mesh.shape) == {"fsdp": 8, "tp": 4}
+    body = local_plane if plane else local
     in_specs = (
         P(("fsdp", "tp"), None),
         P("fsdp"),
@@ -374,4 +1133,4 @@
         P("fsdp", "tp"),
         P("tp", "fsdp"),
     )
-    return jax.shard_map(local, mesh=mesh, in_specs=in_specs, out_specs=out_specs, check_vma=False)
+    return jax.shard_map(body, mesh=mesh, in_specs=in_specs, out_specs=out_specs, check_vma=False)

time: 1820 us -> 1060 us (0.58)
  waiting for transfers between devices: 805 us -> 90.1 us
  Pallas kernels: 0 us -> 698 us
  matrix products: 580 us -> 137 us
  other arithmetic: 242 us -> 31.9 us
  local copies, waits for them, and re-layouts: 83.9 us -> 18.9 us
    pallas_call x0 -> x16, Pallas kernels: none -> 698 us  [the longest x4 173 us: plane_sum(): pl.pallas_call(kernel, out_shape=jax.ShapeDtypeStruct((height, width), jn...]
    all_gather x9 -> x4, waiting for transfers between devices: 392 us -> 0.03 us  [the longest x1 0.02 us: local_plane(): up_rows = lax.all_gather(up_part, 'tp', axis=0, tiled=True)]
    reduce_scatter x11 -> x4, waiting for transfers between devices: 398 us -> 88.7 us  [the longest x3 88.7 us: local_plane(): lax.psum_scatter(g, 'tp', scatter_dimension=0, tiled=True)]
    dot_general x29 -> x5, matrix products: 305 us -> 50.3 us  [outer_cols(): lax.dot_general(left, right, (((1,), (1,)), ((), ())), preferred_element_...]
    convert_element_type x24 -> x13, other arithmetic: 170 us -> 12.3 us  [the longest x1 2.92 us: local_plane(): middle_rows = plane_gather(grad_middle.astype(bf16), 10)]
    dot_general x21 -> x5, matrix products: 167 us -> 41.9 us  [dot_nn(): return jnp.dot(left, right, preferred_element_type=jnp.float32)]
    dot_general x21 -> x5, matrix products: 108 us -> 44.9 us  [inner_rows(): lax.dot_general(left, right, (((0,), (0,)), ((), ())), preferred_element_...]
    reduce_sum x17 -> x6, other arithmetic: 56.5 us -> 2.64 us  [the longest x1 1.14 us: local_plane(): gain_second_part = jnp.sum(grad_second * normed_second, axis=0)]
  transfers between devices with their start and end apart: 28 -> 8, of which waited for: 18 -> 2; matrix products, arithmetic and copies ran while one was open for 45% -> 10% of each run, Pallas kernels for 0% -> 35%
where the time goes in v1:
time: 1060 us; the launch traced here: 1040 us
  Pallas kernels  698 us (66%)
  matrix products  137 us (13%)
  waiting for transfers between devices  90.1 us (8%)
  blocking collectives  52.7 us (5%)
  other arithmetic  31.9 us (3%)
  local copies, waits for them, and re-layouts  18.9 us (2%)
  between operations  15.4 us (1%)
    pallas_call x4, Pallas kernels, plane_sum(): pl.pallas_call(kernel, out_shape=jax.ShapeDtypeStruct((height, width), jn...  173 us
    pallas_call x4, Pallas kernels, plane_gather(): pl.pallas_call(kernel, out_shape=jax.ShapeDtypeStruct((8 * height, width)...  157 us
    pallas_call x4, Pallas kernels, plane_exchange(): pl.pallas_call(kernel, out_shape=[jax.ShapeDtypeStruct(shape, jnp.bfloat1...  117 us
    reduce_scatter x3, waiting for transfers between devices, local_plane(): lax.psum_scatter(g, 'tp', scatter_dimension=0, tiled=True)  88.7 us
    pallas_call x1, Pallas kernels, pair_sum(): pl.pallas_call(kernel, out_shape=jax.ShapeDtypeStruct((chunks, height, wi...  80.9 us
    pallas_call x1, Pallas kernels, attend_back(): pl.pallas_call(kernel, grid_spec=pltpu.PrefetchScalarGridSpec(num_scalar_...  67.1 us
    pallas_call x1, Pallas kernels, attend(): pl.pallas_call(kernel, grid_spec=pltpu.PrefetchScalarGridSpec(num_scalar_...  66.1 us
    dot_general x5, matrix products, outer_cols(): lax.dot_general(left, right, (((1,), (1,)), ((), ())), preferred_element_...  50.3 us
  transfers between devices with their start and end apart: 8, of which 2 were waited for; matrix products, arithmetic and copies ran while one was open for 10% of the time, Pallas kernels for 35%

profile of v1, /device:TPU:0, one launch (start us, length us, event | category | flops | bytes accessed | tf_op | source)
XLA Modules:
  0.0 1044.2 jit_solution(13227256296135786185)
XLA Ops:
  8.4 1.8 pad_maximum_fusion.5
  12.6 29.3 %plane_exchange_1.1 = (bf16[176,2048]{1,0:T(8,128)(2,1)}, bf16[176,2048]{1,0:T(8,128)(2,1)}, bf16[176,2048]{1,0:T(8,128)(2,1)}) custom-call(bf16[8,176,256]{2,1,0:T(8,128)(2,1)} %bitcast.118, bf16[8,176,256]{2,1,0:T(8,128)(2,1)} %bitcast.119, bf16[8,176,256]{2,1,0:T(8,128)(2,1)} %bitcast.131), custom_call_target="tpu_custom_call" | custom-call | tf_op jit(solution)/shard_map/plane_exchange_1/pallas_call | solution.py:552
  44.3 8.9 all-gather.2
  55.1 39.3 %plane_gather_2.1 = bf16[2048,2048]{1,0:T(8,128)(2,1)} custom-call(bf16[256,2048]{1,0:T(8,128)(2,1)} %fusion.5.x_ref), custom_call_target="tpu_custom_call" | custom-call | tf_op jit(solution)/shard_map/plane_gather_2/pallas_call | solution.py:436
  97.1 39.4 %plane_gather_8.1 = bf16[2048,2048]{1,0:T(8,128)(2,1)} custom-call(bf16[256,2048]{1,0:T(8,128)(2,1)} %fusion.12.x_ref), custom_call_target="tpu_custom_call" | custom-call | tf_op jit(solution)/shard_map/plane_gather_8/pallas_call | solution.py:436
  136.6 2.0 fusion.36
  138.7 31.4 %plane_exchange_3.1 = bf16[640,2048]{1,0:T(8,128)(2,1)} custom-call(bf16[4,1152,256]{2,1,0:T(8,128)(2,1)} %bitcast.120), custom_call_target="tpu_custom_call" | custom-call | tf_op jit(solution)/shard_map/plane_exchange_3/pallas_call | solution.py:552
  170.1 6.4 fusion.13
  176.5 1.5 slice.128
  180.9 35.8 %pair_gather_4.1.kv_ref = bf16[4,2048,128]{2,1,0:T(8,128)(2,1)} custom-call(bf16[2048,128]{1,0:T(8,128)(2,1)} %maximum_bitcast_fusion.x_ref), custom_call_target="tpu_custom_call" | custom-call | tf_op jit(solution)/shard_map/pair_gather_4/pallas_call | solution.py:603
  216.8 2.0 subtract_convert_fusion.1
  219.0 66.1 %attend.1 = (bf16[256,2048]{1,0:T(8,128)(2,1)S(1)}, f32[8,1,1024]{2,1,0:T(1,128)S(1)}) custom-call(s32[8,3]{1,0:T(8,128)S(1)} %pad_add_fusion.info_ref, s32[8,1,256]{2,1,0:T(1,128)S(1)} %bitcast.112, bf16[256,2048]{1,0:T(8,128)(2,1)S(1)} %bitcast.109, bf16[4,2048,128]{2,1,0:T(8,128)(2,1)S(1)} %copy-done), custom_call_target="tpu_custom_call" | custom-call | flops 30000001024 | bytes 6000000 | tf_op jit(solution)/shard_map/attend/pallas_call | solution.py:740
  285.2 5.6 convolution_convert_fusion.2.p_ref
  290.9 43.4 %plane_sum_5.1 = f32[256,2048]{1,0:T(8,128)S(1)} custom-call(bf16[2048,2048]{1,0:T(8,128)(2,1)} %convolution_convert_fusion.2.p_ref), custom_call_target="tpu_custom_call" | custom-call | tf_op jit(solution)/shard_map/plane_sum_5/pallas_call | solution.py:508
  334.7 1.3 copy-done.5
  337.2 39.4 %plane_gather_6.1 = bf16[2048,2048]{1,0:T(8,128)(2,1)} custom-call(bf16[256,2048]{1,0:T(8,128)(2,1)} %multiply_convert_fusion.3.x_ref), custom_call_target="tpu_custom_call" | custom-call | tf_op jit(solution)/shard_map/plane_gather_6/pallas_call | solution.py:436
  376.7 11.4 %fusion.52 = f32[704,2048]{1,0:T(8,128)} fusion(bf16[704,2048]{1,0:T(8,128)(2,1)} %all-gather.10.cloned.1.call-done, bf16[2048,2048]{1,0:T(8,128)(2,1)} %plane_gather_6.1), kind=kOutput, calls=%fused_computation.132 | convolution fusion | flops 5905580032 | bytes 17039360 | tf_op jit(solution)/shard_map/dot_general | solution.py:63
  388.1 11.1 %fusion.51 = f32[704,2048]{1,0:T(8,128)} fusion(bf16[704,2048]{1,0:T(8,128)(2,1)} %all-gather.8.cloned.1.call-done, bf16[2048,2048]{1,0:T(8,128)(2,1)} %plane_gather_6.1), kind=kOutput, calls=%fused_computation.131 | convolution fusion | flops 5905580032 | bytes 17039360 | tf_op jit(solution)/shard_map/dot_general | solution.py:63
  399.2 15.3 %multiply_convert_fusion = (bf16[704,2048]{1,0:T(8,128)(2,1)S(1)}, bf16[704,2048]{1,0:T(8,128)(2,1)S(1)}, bf16[704,2048]{1,0:T(8,128)(2,1)}) fusion(f32[704,2048]{1,0:T(8,128)} %fusion.51, f32[704,2048]{1,0:T(8,128)} %fusion.52, bf16[704,2048]{1,0:T(8,128)(2,1)} %all-gather.12.cloned.1.call-done, bf16[2048,2048]{1,0:T(8,128)(2,1)} %plane_gather_8.1), kind=kOutput, calls=%fused_computation.4 | convolution fusion | flops 5927206912 | bytes 31457280 | tf_op jit(solution)/shard_map/dot_general | solution.py:63
  414.5 10.8 %fusion.53 = f32[2048,2048]{1,0:T(8,128)} fusion(bf16[704,2048]{1,0:T(8,128)(2,1)S(1)} %get-tuple-element.40, bf16[704,2048]{1,0:T(8,128)(2,1)S(1)} %copy-done.35), kind=kOutput, calls=%fused_computation.133 | convolution fusion | flops 5905580032 | bytes 22544384 | tf_op jit(solution)/shard_map/dot_general | solution.py:57
  425.3 12.4 %add_convert_fusion.p_ref = bf16[2048,2048]{1,0:T(8,128)(2,1)} fusion(f32[2048,2048]{1,0:T(8,128)} %fusion.53, bf16[704,2048]{1,0:T(8,128)(2,1)S(1)} %get-tuple-element.39, bf16[704,2048]{1,0:T(8,128)(2,1)S(1)} %copy-done.33), kind=kOutput, calls=%fused_computation | convolution fusion | flops 5913968640 | bytes 30932992 | tf_op jit(solution)/shard_map/dot_general | solution.py:57
  437.7 43.4 %plane_sum_9.1 = f32[256,2048]{1,0:T(8,128)S(1)} custom-call(bf16[2048,2048]{1,0:T(8,128)(2,1)} %add_convert_fusion.p_ref), custom_call_target="tpu_custom_call" | custom-call | tf_op jit(solution)/shard_map/plane_sum_9/pallas_call | solution.py:508
  482.9 9.2 convolution_convert_fusion.1.p_ref
  492.1 42.8 %plane_sum_7.1 = f32[256,2048]{1,0:T(8,128)S(1)} custom-call(bf16[2048,2048]{1,0:T(8,128)(2,1)} %convolution_convert_fusion.1.p_ref), custom_call_target="tpu_custom_call" | custom-call | tf_op jit(solution)/shard_map/plane_sum_7/pallas_call | solution.py:508
  535.0 2.9 fusion.46
  537.9 39.1 %plane_gather_10.1 = bf16[2048,2048]{1,0:T(8,128)(2,1)} custom-call(bf16[256,2048]{1,0:T(8,128)(2,1)} %get-tuple-element.35.x_ref), custom_call_target="tpu_custom_call" | custom-call | tf_op jit(solution)/shard_map/plane_gather_10/pallas_call | solution.py:436
  577.0 6.2 convolution_convert_fusion.8.g_ref
  583.3 67.1 %attend_back.1 = (f32[256,2048]{1,0:T(8,128)S(1)}, bf16[4,8,128,256]{3,2,1,0:T(8,128)(2,1)S(1)}) custom-call(s32[8,3]{1,0:T(8,128)S(1)} %pad_add_fusion.info_ref, s32[8,1,256]{2,1,0:T(1,128)S(1)} %bitcast.113, bf16[256,2048]{1,0:T(8,128)(2,1)S(1)} %bitcast.110, bf16[4,2048,128]{2,1,0:T(8,128)(2,1)S(1)} %copy-done, ...), custom_call_target="tpu_custom_call" | custom-call | flops 70000001024 | bytes 10000000 | tf_op jit(solution)/shard_map/attend_back/pallas_call | solution.py:836
  650.4 80.9 %pair_sum_11.1 = f32[8,128,256]{2,1,0:T(8,128)S(1)} custom-call(bf16[4,8,128,256]{3,2,1,0:T(8,128)(2,1)S(1)} %get-tuple-element.27.p_ref), custom_call_target="tpu_custom_call" | custom-call | tf_op jit(solution)/shard_map/pair_sum_11/pallas_call | solution.py:656
  732.0 3.3 convolution_convert_fusion.7
  739.5 6.6 convolution_convert_fusion.6
  746.0 1.7 pad_maximum_fusion.refs_0_
  747.7 28.7 %plane_exchange_13.1 = bf16[8,576,256]{2,1,0:T(8,128)(2,1)} custom-call(bf16[576,2048]{1,0:T(8,128)(2,1)} %pad_maximum_fusion.refs_0_), custom_call_target="tpu_custom_call" | custom-call | tf_op jit(solution)/shard_map/plane_exchange_13/pallas_call | solution.py:552
  776.5 10.6 %convolution_convert_fusion.3 = bf16[704,2048]{1,0:T(8,128)(2,1)} fusion(bf16[704,2048]{1,0:T(8,128)(2,1)} %copy-done.39, bf16[2048,2048]{1,0:T(8,128)(2,1)} %plane_gather_6.1), kind=kOutput, calls=%fused_computation.9 | convolution fusion | flops 5907021824 | bytes 14155776 | tf_op jit(solution)/shard_map/dot_general | solution.py:674
  787.2 10.6 %convolution_convert_fusion.4 = bf16[704,2048]{1,0:T(8,128)(2,1)} fusion(bf16[704,2048]{1,0:T(8,128)(2,1)} %copy-done.38, bf16[2048,2048]{1,0:T(8,128)(2,1)} %plane_gather_6.1), kind=kOutput, calls=%fused_computation.10 | convolution fusion | flops 5907021824 | bytes 14155776 | tf_op jit(solution)/shard_map/dot_general | solution.py:674
  797.8 10.9 %convolution_convert_fusion.5 = bf16[704,2048]{1,0:T(8,128)(2,1)} fusion(bf16[704,2048]{1,0:T(8,128)(2,1)} %get-tuple-element.41, bf16[2048,2048]{1,0:T(8,128)(2,1)} %plane_gather_8.1), kind=kOutput, calls=%fused_computation.11 | convolution fusion | flops 5907021824 | bytes 14155776 | tf_op jit(solution)/shard_map/dot_general | solution.py:674
  808.8 1.8 copy-done.11
  811.1 6.8 convolution_convert_fusion.p_ref
  818.0 43.5 %plane_sum_12.1 = f32[256,2048]{1,0:T(8,128)S(1)} custom-call(bf16[2048,2048]{1,0:T(8,128)(2,1)} %convolution_convert_fusion.p_ref), custom_call_target="tpu_custom_call" | custom-call | tf_op jit(solution)/shard_map/plane_sum_12/pallas_call | solution.py:508
  862.3 43.8 %psum.7 = f32[2,2048]{1,0:T(2,128)S(1)} all-reduce(f32[2,2048]{1,0:T(2,128)S(1)} %pad_maximum_fusion.8), channel_id=1, replica_groups=mesh['fsdp'=8,'tp'=4] {'fsdp','tp'}, use_global_device_ids=true, to_apply=%region_8.9 | all-reduce | flops 4096 | bytes 32768 | tf_op jit(solution)/shard_map/psum | solution.py:1089
  906.7 3.5 fusion.9
  912.3 1.4 convert_bitcast_fusion
  914.6 30.4 %reduce-scatter.9.cloned.1.call-done.refs_1_ = bf16[176,2048]{1,0:T(8,128)(2,1)} async-done(((bf16[704,2048]{1,0:T(8,128)(2,1)}), bf16[176,2048]{1,0:T(8,128)(2,1)}) %reduce-scatter.9.cloned.1.call-update) | async-done | bytes 720912 | tf_op jit(solution)/shard_map/reduce_scatter | solution.py:1034
  944.9 58.4 %reduce-scatter.7.cloned.1.call-done.refs_0_ = bf16[176,2048]{1,0:T(8,128)(2,1)} async-done(((bf16[704,2048]{1,0:T(8,128)(2,1)}), bf16[176,2048]{1,0:T(8,128)(2,1)}) %reduce-scatter.7.cloned.1.call-update) | async-done | bytes 720912 | tf_op jit(solution)/shard_map/reduce_scatter | solution.py:1034
  1003.3 27.8 %plane_exchange_14.1 = (bf16[8,176,256]{2,1,0:T(8,128)(2,1)}, bf16[8,176,256]{2,1,0:T(8,128)(2,1)}, bf16[8,176,256]{2,1,0:T(8,128)(2,1)}) custom-call(bf16[176,2048]{1,0:T(8,128)(2,1)} %reduce-scatter.7.cloned.1.call-done.refs_0_, bf16[176,2048]{1,0:T(8,128)(2,1)} %reduce-scatter.9.cloned.1.call-done.refs_1_, ...), custom_call_target="tpu_custom_call" | custom-call | tf_op jit(solution)/shard_map/plane_exchange_14/pallas_call | solution.py:552
  1031.1 1.3 bitcast_convert_fusion.2
  1032.4 1.5 copy.93
  1034.1 1.5 copy.94
  (168 shorter events, 28.2 us)
Async XLA Ops:
  7.2 3.1 copy-start.19
  7.2 4.3 copy-start.20
  7.2 131.5 %all-gather.14.cloned.1.call-start = ((), (), s32[]{:S(2)}) async-start(), calls=%async_computation.11 | async-start | bytes 2949120 | tf_op jit(solution)/shard_map/all_gather | solution.py:920
  10.3 366.4 %all-gather.10.cloned.1.call-start = ((), (), s32[]{:S(2)}) async-start(), calls=%async_computation.5 | async-start | bytes 3604480 | tf_op jit(solution)/shard_map/all_gather | solution.py:932
  11.5 32.0 %copy-start.32 = (s32[2]{0:T(128)S(1)}, s32[2]{0:T(128)}, u32[]{:S(2)}) copy-start(s32[2]{0:T(128)} %param.23) | copy-start | bytes 28
  11.5 32.8 %copy-start.36 = (bf16[256]{0:T(256)(128)(2,1)S(1)}, bf16[256]{0:T(256)(128)(2,1)}, u32[]{:S(2)}) copy-start(bf16[256]{0:T(256)(128)(2,1)} %param.13) | copy-start | bytes 1540
  11.5 32.8 %copy-start.37 = (bf16[256]{0:T(256)(128)(2,1)S(1)}, bf16[256]{0:T(256)(128)(2,1)}, u32[]{:S(2)}) copy-start(bf16[256]{0:T(256)(128)(2,1)} %param.18) | copy-start | bytes 1540
  11.5 41.8 %copy-start.7 = (bf16[256,2048]{1,0:T(8,128)(2,1)S(1)}, bf16[256,2048]{1,0:T(8,128)(2,1)}, u32[]{:S(2)}) copy-start(bf16[256,2048]{1,0:T(8,128)(2,1)} %param.12) | copy-start | bytes 3145732
  42.0 346.1 %all-gather.8.cloned.1.call-start = ((), (), s32[]{:S(2)}) async-start(), calls=%async_computation.4 | async-start | bytes 3604480 | tf_op jit(solution)/shard_map/all_gather | solution.py:931
  42.7 356.4 %all-gather.12.cloned.1.call-start = ((), (), s32[]{:S(2)}) async-start(), calls=%async_computation.6 | async-start | bytes 3604480 | tf_op jit(solution)/shard_map/all_gather | solution.py:933
  43.3 866.9 %reduce-scatter.5.cloned.1.call-start = ((), (), s32[]{:S(2)}) async-start(), calls=%async_computation.7 | async-start | bytes 2949120 | tf_op jit(solution)/shard_map/reduce_scatter | solution.py:1074
  43.4 134.7 %copy-start.30 = (f32[32]{0:T(128)}, f32[32]{0:T(128)S(1)}, u32[]{:S(2)}) copy-start(f32[32]{0:T(128)S(1)} %multiply_power_fusion) | copy-start | bytes 388
  53.6 40.9 %copy-start.28 = (f32[256]{0:T(256)}, f32[256]{0:T(256)S(1)}, u32[]{:S(2)}) copy-start(f32[256]{0:T(256)S(1)} %add_rsqrt_fusion.1) | copy-start | bytes 3076
  55.1 40.8 %copy-start.12 = (bf16[256,2048]{1,0:T(8,128)(2,1)S(1)}, bf16[256,2048]{1,0:T(8,128)(2,1)}, u32[]{:S(2)}) copy-start(bf16[256,2048]{1,0:T(8,128)(2,1)} %param.22) | copy-start | bytes 3145732
  95.1 82.9 %copy-start.23 = (f32[2048]{0:T(1024)}, f32[2048]{0:T(1024)S(1)}, u32[]{:S(2)}) copy-start(f32[2048]{0:T(1024)S(1)} %select_convert_fusion.1) | copy-start | bytes 24580
  138.6 78.2 %copy-start.14 = (f32[32,2048]{1,0:T(8,128)}, f32[32,2048]{1,0:T(8,128)S(1)}, u32[]{:S(2)}) copy-start(f32[32,2048]{1,0:T(8,128)S(1)} %get-tuple-element.61) | copy-start | bytes 786436
  216.8 2.3 copy-start
  218.9 66.3 %copy-start.3 = (bf16[4,2,32,2048]{3,2,1,0:T(8,128)(2,1)}, bf16[4,2,32,2048]{3,2,1,0:T(8,128)(2,1)S(1)}, u32[]{:S(2)}) copy-start(bf16[4,2,32,2048]{3,2,1,0:T(8,128)(2,1)S(1)} %maximum_multiply_fusion) | copy-start | bytes 3145732
  219.0 66.2 %copy-start.10 = (bf16[640,2048]{1,0:T(8,128)(2,1)S(1)}, bf16[640,2048]{1,0:T(8,128)(2,1)}, u32[]{:S(2)}) copy-start(bf16[640,2048]{1,0:T(8,128)(2,1)} %plane_exchange_3.1) | copy-start | bytes 7864324
  290.8 43.4 %copy-start.8 = (bf16[256,2048]{1,0:T(8,128)(2,1)S(1)}, bf16[256,2048]{1,0:T(8,128)(2,1)}, u32[]{:S(2)}) copy-start(bf16[256,2048]{1,0:T(8,128)(2,1)} %param.12) | copy-start | bytes 3145732
  399.2 15.3 %copy-start.35 = (bf16[704,2048]{1,0:T(8,128)(2,1)S(1)}, bf16[704,2048]{1,0:T(8,128)(2,1)}, u32[]{:S(2)}) copy-start(bf16[704,2048]{1,0:T(8,128)(2,1)} %all-gather.8.cloned.1.call-done) | copy-start | bytes 8650756
  414.4 10.8 %copy-start.38 = (bf16[704,2048]{1,0:T(8,128)(2,1)}, bf16[704,2048]{1,0:T(8,128)(2,1)S(1)}, u32[]{:S(2)}) copy-start(bf16[704,2048]{1,0:T(8,128)(2,1)S(1)} %get-tuple-element.40) | copy-start | bytes 8650756
  414.4 10.8 %copy-start.39 = (bf16[704,2048]{1,0:T(8,128)(2,1)}, bf16[704,2048]{1,0:T(8,128)(2,1)S(1)}, u32[]{:S(2)}) copy-start(bf16[704,2048]{1,0:T(8,128)(2,1)S(1)} %get-tuple-element.39) | copy-start | bytes 8650756
  414.5 10.8 %copy-start.33 = (bf16[704,2048]{1,0:T(8,128)(2,1)S(1)}, bf16[704,2048]{1,0:T(8,128)(2,1)}, u32[]{:S(2)}) copy-start(bf16[704,2048]{1,0:T(8,128)(2,1)} %all-gather.10.cloned.1.call-done) | copy-start | bytes 8650756
  437.7 43.4 %copy-start.6 = (f32[256,2048]{1,0:T(8,128)S(1)}, f32[256,2048]{1,0:T(8,128)}, u32[]{:S(2)}) copy-start(f32[256,2048]{1,0:T(8,128)} %copy-done.5) | copy-start | bytes 6291460
  437.7 44.5 %copy-start.40 = (bf16[704,2048]{1,0:T(8,128)(2,1)S(1)}, bf16[704,2048]{1,0:T(8,128)(2,1)}, u32[]{:S(2)}) copy-start(bf16[704,2048]{1,0:T(8,128)(2,1)} %get-tuple-element.41) | copy-start | bytes 8650756
  481.1 1.8 copy-start.34
  492.1 42.8 %copy-start.13 = (bf16[256,2048]{1,0:T(8,128)(2,1)S(1)}, bf16[256,2048]{1,0:T(8,128)(2,1)}, u32[]{:S(2)}) copy-start(bf16[256,2048]{1,0:T(8,128)(2,1)} %param.22) | copy-start | bytes 3145732
  577.0 6.2 copy-start.4
  577.0 155.0 %slice-start.1 = ((s8[8388608]{0:T(1024)(128)(4,1)}), s8[4194304]{0:T(1024)(128)(4,1)S(1)}, s32[]{:S(2)}) async-start(s8[8388608]{0:T(1024)(128)(4,1)} %bitcast.115), calls=%async_computation.13 | async-start | bytes 8388608
  583.3 148.8 %slice-start.2 = ((s8[8388608]{0:T(1024)(128)(4,1)}), s8[4194304]{0:T(1024)(128)(4,1)S(1)}, s32[]{:S(2)}) async-start(s8[8388608]{0:T(1024)(128)(4,1)} %bitcast.115), calls=%async_computation.14 | async-start | bytes 8388608
  650.3 85.0 %copy-start.1 = (f32[256,2048]{1,0:T(8,128)}, f32[256,2048]{1,0:T(8,128)S(1)}, u32[]{:S(2)}) copy-start(f32[256,2048]{1,0:T(8,128)S(1)} %get-tuple-element.26) | copy-start | bytes 6291460
  732.0 3.8 copy-start.24
  732.0 3.8 copy-start.31
  735.4 2.6 copy-start.15
  735.7 2.3 copy-start.2
  739.3 6.7 copy-start.16
  739.4 6.6 copy-start.18
  776.5 138.1 %reduce-scatter.11.cloned.1.call-start = ((), (), s32[]{:S(2)}) async-start(), calls=%async_computation.10 | async-start | bytes 3604480 | tf_op jit(solution)/shard_map/reduce_scatter | solution.py:1034
  787.1 157.8 %reduce-scatter.9.cloned.1.call-start = ((), (), s32[]{:S(2)}) async-start(), calls=%async_computation.9 | async-start | bytes 3604480 | tf_op jit(solution)/shard_map/reduce_scatter | solution.py:1034
  797.8 205.5 %reduce-scatter.7.cloned.1.call-start = ((), (), s32[]{:S(2)}) async-start(), calls=%async_computation.8 | async-start | bytes 3604480 | tf_op jit(solution)/shard_map/reduce_scatter | solution.py:1034
  808.7 1.9 copy-start.11
  808.8 2.3 slice-start
  808.8 2.4 copy-start.17
  818.0 43.5 %copy-start.9 = (bf16[256,2048]{1,0:T(8,128)(2,1)S(1)}, bf16[256,2048]{1,0:T(8,128)(2,1)}, u32[]{:S(2)}) copy-start(bf16[256,2048]{1,0:T(8,128)(2,1)} %param.12) | copy-start | bytes 3145732
  818.0 43.5 %copy-start.26 = (f32[1,8,256]{2,0,1:T(1,128)S(1)}, f32[1,8,256]{2,0,1:T(1,128)}, u32[]{:S(2)}) copy-start(f32[1,8,256]{2,0,1:T(1,128)} %copy-done.25) | copy-start | bytes 24580
  818.0 43.5 %copy-start.29 = (f32[256]{0:T(256)S(1)}, f32[256]{0:T(256)}, u32[]{:S(2)}) copy-start(f32[256]{0:T(256)} %copy-done.28) | copy-start | bytes 3076
  1031.1 2.8 copy-start.22
  (4 other events, 4.3 us)
Sparse Core Ops, SparseCore 0:
  10.4 53.1 all-gather.13
  65.2 57.9 all-gather.9
  124.8 57.8 all-gather.7
  184.1 71.4 all-gather.11
  776.6 51.6 reduce-scatter.4
  830.4 55.7 reduce-scatter.10
  888.6 56.3 reduce-scatter.8
  947.2 56.0 reduce-scatter.6

commit v2 on v0

--- a/solution.py
+++ b/solution.py
@@ -1,6 +1,8 @@
 import jax
 import jax.numpy as jnp
 from jax import lax
+from jax.experimental import pallas as pl
+from jax.experimental.pallas import tpu as pltpu
 from jax.sharding import PartitionSpec as P
 
 HEAD_DIM = 64
@@ -19,7 +21,7 @@
 def stream_layout(slots, lengths):
     seq_count = lengths.shape[0]
     seq_index = jnp.arange(seq_count, dtype=jnp.int32)
-    ends = jnp.cumsum(lengths)
+    ends = jnp.sum(jnp.where(seq_index[:, None] >= seq_index[None, :], lengths[None, :], 0), axis=1)
     starts = ends - lengths
     segment = jnp.sum((slots[:, None] >= ends[None, :]).astype(jnp.int32), axis=1)
     start_of = jnp.sum(
@@ -346,7 +348,1376 @@
     )
 
 
+MESH = pl.DeviceIdType.MESH
+CORE, ALONG_X, ALONG_Y = 1, 2, 4
+PARTS = 4
+VMEM_MOST = 60 << 20
+
+
+def greet(partners):
+    barrier = pltpu.get_barrier_semaphore()
+    for partner in partners:
+        pl.semaphore_signal(barrier, inc=1, device_id=partner, device_id_type=MESH)
+    pl.semaphore_wait(barrier, len(partners))
+
+
+def remote(source, target, sent, arrived, partner):
+    return pltpu.make_async_remote_copy(
+        src_ref=source,
+        dst_ref=target,
+        send_sem=sent,
+        recv_sem=arrived,
+        device_id=partner,
+        device_id_type=MESH,
+    )
+
+
+def comm_params(number, vmem=None):
+    return pltpu.CompilerParams(
+        collective_id=number, has_side_effects=True, vmem_limit_bytes=vmem
+    )
+
+
+def lasting(microseconds):
+    return pl.CostEstimate(
+        flops=int(microseconds * 1.1e9), bytes_accessed=1_000_000, transcendentals=0
+    )
+
+
+ANYWHERE = pl.BlockSpec(memory_space=pl.ANY)
+IN_VMEM = pl.BlockSpec(memory_space=pltpu.VMEM)
+
+
+def columns(index, width):
+    return pl.ds(pl.multiple_of(index * width, width), width)
+
+
+class PlaneGather:
+    def __init__(self, store, sent, arrived):
+        self.f, self.t = lax.axis_index("fsdp"), lax.axis_index("tp")
+        self.store, self.sent, self.arrived = store, sent, arrived
+        self.piece = store.shape[1] // PARTS
+        self.near = [(self.f ^ k, self.t) for k in (CORE, ALONG_X, ALONG_Y)]
+        self.copies, self.on = [], {}
+
+    def send(self, owner, j, way, slot):
+        place = self.store.at[owner, pl.ds(j * self.piece, self.piece)]
+        c = remote(
+            place, place, self.sent.at[slot, j], self.arrived.at[slot, j], self.near[way]
+        )
+        c.start()
+        self.copies.append(c)
+        self.on[slot, j] = c
+
+    def begin(self):
+        for k in range(PARTS):
+            self.send(self.f, k, 1, 1)
+            self.send(self.f, (k + PARTS // 2) % PARTS, 2, 2)
+        for k in range(PARTS):
+            self.send(self.f, k, 0, 0)
+
+    def arrive(self, slot, j):
+        self.on[slot, j].wait_recv()
+
+    def advance(self, k):
+        jx, jy = k, (k + PARTS // 2) % PARTS
+        self.arrive(1, jx)
+        if jx < PARTS // 2:
+            self.send(self.f ^ ALONG_X, jx, 2, 6)
+        self.send(self.f ^ ALONG_X, jx, 0, 3)
+        self.arrive(2, jy)
+        if jy >= PARTS // 2:
+            self.send(self.f ^ ALONG_Y, jy, 1, 6)
+        self.send(self.f ^ ALONG_Y, jy, 0, 4)
+
+    def far(self):
+        for k in range(PARTS // 2):
+            for j in (k, k + PARTS // 2):
+                self.arrive(6, j)
+                self.send(self.f ^ ALONG_X ^ ALONG_Y, j, 0, 5)
+
+    def wait_core(self, *slots):
+        for slot in slots:
+            for j in range(PARTS):
+                self.arrive(slot, j)
+
+    def finish(self):
+        for c in self.copies:
+            c.wait_send()
+
+
+GATHER_SEMAPHORES = [pltpu.SemaphoreType.DMA((7, PARTS)), pltpu.SemaphoreType.DMA((7, PARTS))]
+
+
+class PlaneSum:
+    masks = (ALONG_X ^ ALONG_Y, ALONG_X, ALONG_Y, 0)
+
+    def __init__(self, stage, other, held, from_x, from_y, last, sent, arrived):
+        self.f, self.t = lax.axis_index("fsdp"), lax.axis_index("tp")
+        self.stage, self.other, self.held = stage, other, held
+        self.from_x, self.from_y, self.last = from_x, from_y, last
+        self.sent, self.arrived = sent, arrived
+        self.near = [(self.f ^ k, self.t) for k in (CORE, ALONG_X, ALONG_Y)]
+        self.copies, self.on = [], {}
+        half = held.shape[1] // 2
+        self.top, self.low = pl.ds(0, half), pl.ds(half, half)
+
+    def send(self, source, target, slot, way):
+        c = remote(source, target, self.sent.at[slot], self.arrived.at[slot], self.near[way])
+        c.start()
+        self.copies.append(c)
+        self.on[slot] = c
+
+    def begin(self, write_part, after=None):
+        for i, mask in enumerate(self.masks):
+            if i >= 2:
+                self.on[i - 2].wait_send()
+                self.copies = [c for c in self.copies if c is not self.on[i - 2]]
+            write_part(self.f ^ CORE ^ mask, self.stage.at[i % 2])
+            self.send(self.stage.at[i % 2], self.other.at[i], i, 0)
+            write_part(self.f ^ mask, self.held.at[i])
+            if after is not None:
+                after(i)
+            self.on[i].wait_recv()
+            self.held[i] = (
+                self.held[i].astype(jnp.float32) + self.other[i].astype(jnp.float32)
+            ).astype(jnp.bfloat16)
+            if i == 0:
+                self.send(self.held.at[0, self.top], self.from_x.at[0], 4, 1)
+                self.send(self.held.at[0, self.low], self.from_y.at[0], 5, 2)
+            if i == 1:
+                self.send(self.held.at[1, self.top], self.from_x.at[1], 6, 1)
+            if i == 2:
+                self.send(self.held.at[2, self.low], self.from_y.at[1], 7, 2)
+
+    def turn(self):
+        self.on[4].wait_recv()
+        self.held[2, self.top] = (
+            self.held[2, self.top].astype(jnp.float32) + self.from_x[0].astype(jnp.float32)
+        ).astype(jnp.bfloat16)
+        self.send(self.held.at[2, self.top], self.last.at[0], 8, 2)
+        self.on[5].wait_recv()
+        self.held[1, self.low] = (
+            self.held[1, self.low].astype(jnp.float32) + self.from_y[0].astype(jnp.float32)
+        ).astype(jnp.bfloat16)
+        self.send(self.held.at[1, self.low], self.last.at[1], 9, 1)
+
+    def end(self, total):
+        for rows, first, second, take in (
+            (self.top, 6, 8, lambda: self.from_x[1]),
+            (self.low, 7, 9, lambda: self.from_y[1]),
+        ):
+            self.on[first].wait_recv()
+            part = self.held[3, rows].astype(jnp.float32) + take().astype(jnp.float32)
+            self.on[second].wait_recv()
+            total[rows] = part + self.last[second - 8].astype(jnp.float32)
+
+    def finish(self):
+        for c in self.copies:
+            c.wait_send()
+
+
+def sum_scratch(height, width):
+    chunks = [pltpu.VMEM((n, height, width), jnp.bfloat16) for n in (2, 4, 4)]
+    return chunks + [pltpu.VMEM((2, height // 2, width), jnp.bfloat16)] * 3 + [pltpu.SemaphoreType.DMA((10,)), pltpu.SemaphoreType.DMA((10,))]
+
+
+NARROW = 512
+
+
+def chunk_part(pairs, size):
+    def write_part(owner, ref):
+        lanes = columns(owner, size)
+        lefts = [left[:, lanes] for left, _ in pairs]
+
+        def step(n, carry):
+            wide = columns(n, NARROW)
+            total = inner_rows(lefts[0], pairs[0][1][:, wide])
+            for left, (_, right) in zip(lefts[1:], pairs[1:]):
+                total += inner_rows(left, right[:, wide])
+            ref[:, wide] = total.astype(jnp.bfloat16)
+            return carry
+
+        lax.fori_loop(0, ref.shape[1] // NARROW, step, 0)
+
+    return write_part
+
+
+def plane_greet():
+    f, t = lax.axis_index("fsdp"), lax.axis_index("tp")
+    greet([(f ^ k, t) for k in (CORE, ALONG_X, ALONG_Y)])
+
+
+def forward_output(attended, output_rows, tokens, gain, grads, number):
+    size, width = tokens.shape
+    f32, bf16 = jnp.float32, jnp.bfloat16
+
+    def kernel(
+        o_ref, w_ref, x_ref, gain_ref, dy_ref,
+        middle_ref, row_ref, dys_ref,
+        stage, other, held, from_x, from_y, last, sum_sent, sum_arrived,
+        dys, dys_sent, dys_arrived, keep_sem,
+    ):
+        f = lax.axis_index("fsdp")
+        dys[f] = dy_ref[...]
+        plane_greet()
+        gather_dys = PlaneGather(dys, dys_sent, dys_arrived)
+        total = PlaneSum(stage, other, held, from_x, from_y, last, sum_sent, sum_arrived)
+        total.begin(chunk_part([(o_ref, w_ref)], size))
+        gather_dys.begin()
+        total.turn()
+        for k in range(PARTS):
+            gather_dys.advance(k)
+        total.end(middle_ref)
+        middle = x_ref[...].astype(f32) + middle_ref[...]
+        middle_ref[...] = middle
+        inverse = lax.rsqrt(jnp.mean(middle * middle, axis=1, keepdims=True) + epsilon)
+        row_ref[...] = (middle * inverse * gain_ref[...]).astype(bf16)
+        gather_dys.wait_core(0, 3, 4)
+        gather_dys.far()
+        gather_dys.wait_core(5)
+        keep = pltpu.make_async_copy(dys, dys_ref, keep_sem)
+        keep.start()
+        keep.wait()
+        total.finish()
+        gather_dys.finish()
+
+    return pl.pallas_call(
+        kernel,
+        out_shape=[
+            jax.ShapeDtypeStruct((size, width), f32),
+            jax.ShapeDtypeStruct((size, width), bf16),
+            jax.ShapeDtypeStruct((8, size, width), bf16),
+        ],
+        in_specs=[IN_VMEM] * 5,
+        out_specs=[IN_VMEM, IN_VMEM, ANYWHERE],
+        scratch_shapes=sum_scratch(size, width)
+        + [pltpu.VMEM((8, size, width), bf16)]
+        + GATHER_SEMAPHORES
+        + [pltpu.SemaphoreType.DMA],
+        compiler_params=comm_params(number, 50 << 20),
+        cost_estimate=lasting(75),
+        name="forward_output",
+    )(attended, output_rows, tokens, gain, grads)
+
+
+def forward_hidden(row, dys, gate_rows, up_rows, down_rows, number):
+    size, width = row.shape
+    units = gate_rows.shape[0]
+    f32, bf16 = jnp.float32, jnp.bfloat16
+
+    def kernel(
+        row_ref, dys_hbm, gate_hbm, up_hbm, down_hbm,
+        rows_ref, hidden_ref, dgate_ref, dup_ref,
+        rows, rows_sent, rows_arrived, dys, gate_w, up_w, down_w, load_sem, dh, out, out_sem, keep_sem,
+    ):
+        f = lax.axis_index("fsdp")
+        loads = [
+            pltpu.make_async_copy(source, target, load_sem.at[i])
+            for i, (source, target) in enumerate(
+                ((down_hbm, down_w), (dys_hbm, dys), (gate_hbm, gate_w), (up_hbm, up_w))
+            )
+        ]
+        for load in loads:
+            load.start()
+        rows[f] = row_ref[...]
+        plane_greet()
+        gather_rows = PlaneGather(rows, rows_sent, rows_arrived)
+        gather_rows.begin()
+        loads[0].wait()
+        loads[1].wait()
+
+        def grad_chunk(i, carry):
+            dh[i] = outer_cols(down_w[...], dys[i])
+            return carry
+
+        for k in range(PARTS):
+            lax.fori_loop(2 * k, 2 * k + 2, grad_chunk, 0)
+            gather_rows.advance(k)
+        loads[2].wait()
+        loads[3].wait()
+
+        def out_copies(slot, owner):
+            return [
+                pltpu.make_async_copy(
+                    out.at[slot, n], target.at[:, columns(owner, size)], out_sem.at[slot, n]
+                )
+                for n, target in enumerate((hidden_ref, dgate_ref, dup_ref))
+            ]
+
+        def chunk(i, carry):
+            owner = f ^ i
+            slot = lax.rem(i, 2)
+
+            @pl.when(i >= 2)
+            def _():
+                for c in out_copies(slot, owner):
+                    c.wait()
+
+            gate = outer_cols(gate_w[...], rows[owner])
+            up = outer_cols(up_w[...], rows[owner])
+            sigmoid = jax.nn.sigmoid(gate)
+            active = gate * sigmoid
+            grad = dh[owner]
+            out[slot, 0] = (active * up).astype(bf16)
+            out[slot, 1] = (grad * up * sigmoid * (1.0 + gate * (1.0 - sigmoid))).astype(bf16)
+            out[slot, 2] = (grad * active).astype(bf16)
+            for c in out_copies(slot, owner):
+                c.start()
+            return carry
+
+        gather_rows.wait_core(0)
+        lax.fori_loop(0, 2, chunk, 0)
+        gather_rows.wait_core(3, 4)
+        lax.fori_loop(2, 4, chunk, 0)
+        gather_rows.far()
+        lax.fori_loop(4, 6, chunk, 0)
+        gather_rows.wait_core(5)
+        keep = pltpu.make_async_copy(rows, rows_ref, keep_sem)
+        keep.start()
+        lax.fori_loop(6, 8, chunk, 0)
+        for i in (6, 7):
+            for c in out_copies(i % 2, f ^ i):
+                c.wait()
+        keep.wait()
+        gather_rows.finish()
+
+    store = pltpu.VMEM((8, size, width), bf16)
+    weights = pltpu.VMEM((units, width), bf16)
+    return pl.pallas_call(
+        kernel,
+        out_shape=[jax.ShapeDtypeStruct((8, size, width), bf16)]
+        + [jax.ShapeDtypeStruct((units, 8 * size), bf16)] * 3,
+        in_specs=[IN_VMEM] + [ANYWHERE] * 4,
+        out_specs=[ANYWHERE] * 4,
+        scratch_shapes=[store]
+        + GATHER_SEMAPHORES
+        + [store]
+        + [weights] * 3
+        + [
+            pltpu.SemaphoreType.DMA((4,)),
+            pltpu.VMEM((8, units, size), f32),
+            pltpu.VMEM((2, 3, units, size), bf16),
+            pltpu.SemaphoreType.DMA((2, 3)),
+            pltpu.SemaphoreType.DMA,
+        ],
+        compiler_params=comm_params(number, 50 << 20),
+        cost_estimate=lasting(55),
+        name="forward_hidden",
+    )(row, dys, gate_rows, up_rows, down_rows)
+
+
+def backward_middle(
+    dgate, dup, hidden, gate_rows, up_rows, rows, dys, output_rows, attended, middle, grads, gain, number
+):
+    size, width = middle.shape
+    units = gate_rows.shape[0]
+    depth = output_rows.shape[0]
+    blocks = width // size
+    f32, bf16 = jnp.float32, jnp.bfloat16
+    early = 5
+
+    def kernel(
+        dgate_hbm, dup_hbm, hidden_hbm, gate_hbm, up_hbm, rows_hbm, dys_hbm,
+        w_ref, o_ref, middle_ref, dy_ref, gain_ref,
+        grad_ref, gain_grad_ref, grad_o_ref, do_ref, units_ref,
+        stage, other, held, from_x, from_y, last, sum_sent, sum_arrived,
+        store, store_sent, store_arrived,
+        dgate_v, dup_v, hidden_v, gate_w, up_w, load_sem,
+        tall, tall_sem, out, out_sem, o_sum,
+    ):
+        f = lax.axis_index("fsdp")
+        loads = [
+            pltpu.make_async_copy(source, target, load_sem.at[i])
+            for i, (source, target) in enumerate(
+                (
+                    (dgate_hbm, dgate_v),
+                    (gate_hbm, gate_w),
+                    (dup_hbm, dup_v),
+                    (up_hbm, up_w),
+                    (hidden_hbm, hidden_v),
+                )
+            )
+        ]
+        for load in loads:
+            load.start()
+
+        def tall_loads(n, slot):
+            place = columns(n, size)
+            return [
+                pltpu.make_async_copy(
+                    source.at[:, :, place], tall.at[slot, i], tall_sem.at[slot, i]
+                )
+                for i, source in enumerate((dys_hbm, rows_hbm))
+            ]
+
+        for c in tall_loads(0, 0):
+            c.start()
+        plane_greet()
+        total = PlaneSum(stage, other, held, from_x, from_y, last, sum_sent, sum_arrived)
+        gather = PlaneGather(store, store_sent, store_arrived)
+        for load in loads[:4]:
+            load.wait()
+        total.begin(chunk_part([(dgate_v, gate_w), (dup_v, up_w)], size))
+        total.turn()
+        loads[4].wait()
+
+        def out_copies(n, slot):
+            return [
+                pltpu.make_async_copy(
+                    out.at[slot, i], units_ref.at[:, i, :, columns(n, size)], out_sem.at[slot, i]
+                )
+                for i in range(3)
+            ]
+
+        def block(n, carry):
+            slot = lax.rem(n, 2)
+
+            @pl.when(n + 1 < blocks)
+            def _():
+                for c in tall_loads(n + 1, 1 - slot):
+                    c.start()
+
+            for c in tall_loads(n, slot):
+                c.wait()
+
+            @pl.when(n >= 2)
+            def _():
+                for c in out_copies(n, slot):
+                    c.wait()
+
+            dy_cols = tall[slot, 0].reshape(8 * size, size)
+            row_cols = tall[slot, 1].reshape(8 * size, size)
+            out[slot, 0] = dot_nn(hidden_v[...], dy_cols).astype(bf16).reshape(4, units // 4, size)
+            out[slot, 1] = dot_nn(dgate_v[...], row_cols).astype(bf16).reshape(4, units // 4, size)
+            out[slot, 2] = dot_nn(dup_v[...], row_cols).astype(bf16).reshape(4, units // 4, size)
+            for c in out_copies(n, slot):
+                c.start()
+            return carry
+
+        lax.fori_loop(0, early, block, 0)
+        total.end(grad_ref)
+        middle = middle_ref[...]
+        inverse = lax.rsqrt(jnp.mean(middle * middle, axis=1, keepdims=True) + epsilon)
+        normed = middle * inverse
+        grad = grad_ref[...]
+        gain_grad_ref[...] = jnp.sum(grad * normed, axis=0, keepdims=True)
+        grad = dy_ref[...].astype(f32) + norm_back(grad, gain_ref[...], normed, inverse)
+        grad_ref[...] = grad
+        store[f] = grad.astype(bf16)
+        gather.begin()
+        gather.advance(0)
+        lax.fori_loop(early, early + 1, block, 0)
+        gather.advance(1)
+        lax.fori_loop(early + 1, early + 2, block, 0)
+        gather.advance(2)
+        lax.fori_loop(early + 2, blocks, block, 0)
+        gather.advance(3)
+
+        def chunk(i, carry):
+            owner = f ^ i
+            lanes = columns(owner, size)
+            do_ref[:, lanes] = outer_cols(w_ref[...], store[owner]).astype(bf16)
+            o_sum[...] += dot_nn(o_ref[:, lanes], store[owner])
+            return carry
+
+        o_sum[...] = jnp.zeros_like(o_sum)
+        gather.wait_core(0)
+        lax.fori_loop(0, 2, chunk, 0)
+        gather.wait_core(3, 4)
+        lax.fori_loop(2, 6, chunk, 0)
+        gather.far()
+        gather.wait_core(5)
+        lax.fori_loop(6, 8, chunk, 0)
+        grad_o_ref[...] = o_sum[...].astype(bf16)
+        for n in (blocks - 2, blocks - 1):
+            for c in out_copies(n, n % 2):
+                c.wait()
+        total.finish()
+        gather.finish()
+
+    weights = pltpu.VMEM((units, width), bf16)
+    return pl.pallas_call(
+        kernel,
+        out_shape=[
+            jax.ShapeDtypeStruct((size, width), f32),
+            jax.ShapeDtypeStruct((1, width), f32),
+            jax.ShapeDtypeStruct((depth, width), bf16),
+            jax.ShapeDtypeStruct((depth, 8 * size), bf16),
+        ]
+        + [jax.ShapeDtypeStruct((4, 3, units // 4, width), bf16)],
+        in_specs=[ANYWHERE] * 7 + [IN_VMEM] * 5,
+        out_specs=[IN_VMEM] * 4 + [ANYWHERE],
+        scratch_shapes=sum_scratch(size, width)
+        + [pltpu.VMEM((8, size, width), bf16)]
+        + GATHER_SEMAPHORES
+        + [weights] * 5
+        + [
+            pltpu.SemaphoreType.DMA((5,)),
+            pltpu.VMEM((2, 2, 8, size, size), bf16),
+            pltpu.SemaphoreType.DMA((2, 2)),
+            pltpu.VMEM((2, 3, 4, units // 4, size), bf16),
+            pltpu.SemaphoreType.DMA((2, 3)),
+            pltpu.VMEM((depth, width), f32),
+        ],
+        compiler_params=comm_params(number, VMEM_MOST),
+        cost_estimate=lasting(92),
+        name="backward_middle",
+    )(dgate, dup, hidden, gate_rows, up_rows, rows, dys, output_rows, attended, middle, grads, gain)
+
+
+def everyone(f, t):
+    return [(f ^ k, t) for k in range(1, 8)] + [(f, lax.rem(t + k, 4)) for k in (1, 2, 3)]
+
+
+def first_exchange(parts, inner, gains, number):
+    _, units, block = parts[0].shape
+    count = len(parts)
+    far_first = (6, 7, 2, 4, 3, 5, 1)
+
+    def kernel(*refs):
+        sources, (inner_ref, gains_ref) = refs[:count], refs[count : count + 2]
+        targets, (inner_all, gains_all) = refs[count + 2 : 2 * count + 2], refs[2 * count + 2 : 2 * count + 4]
+        sent, arrived, z_sent, z_arrived, kept_sem = refs[2 * count + 4 :]
+        f, t = lax.axis_index("fsdp"), lax.axis_index("tp")
+        place = columns(f, block)
+        kept = [
+            pltpu.make_async_copy(s.at[f], o.at[:, place], kept_sem.at[i])
+            for i, (s, o) in enumerate(zip(sources, targets))
+        ] + [pltpu.make_async_copy(inner_ref, inner_all.at[t], kept_sem.at[count])]
+        for c in kept:
+            c.start()
+        gains_all[f] = gains_ref[...]
+        greet(everyone(f, t))
+        copies = []
+        for k in (2, 1, 3):
+            copies.append(
+                remote(inner_ref, inner_all.at[t], z_sent.at[k], z_arrived.at[k], (f, lax.rem(t + k, 4)))
+            )
+        for k in far_first:
+            copies.append(
+                remote(gains_ref, gains_all.at[f], sent.at[k, count], arrived.at[k, count], (f ^ k, t))
+            )
+        for i, (s, o) in enumerate(zip(sources, targets)):
+            for k in far_first:
+                copies.append(
+                    remote(s.at[f ^ k], o.at[:, place], sent.at[k, i], arrived.at[k, i], (f ^ k, t))
+                )
+        for c in copies:
+            c.start()
+        for c in kept + copies:
+            c.wait()
+
+    return pl.pallas_call(
+        kernel,
+        out_shape=[jax.ShapeDtypeStruct((units, 8 * block), jnp.bfloat16)] * count
+        + [
+            jax.ShapeDtypeStruct((4, *inner.shape), inner.dtype),
+            jax.ShapeDtypeStruct((8, *gains.shape), gains.dtype),
+        ],
+        in_specs=[ANYWHERE] * (count + 1) + [IN_VMEM],
+        out_specs=[ANYWHERE] * (count + 1) + [IN_VMEM],
+        scratch_shapes=[
+            pltpu.SemaphoreType.DMA((8, count + 1)),
+            pltpu.SemaphoreType.DMA((8, count + 1)),
+            pltpu.SemaphoreType.DMA((4,)),
+            pltpu.SemaphoreType.DMA((4,)),
+            pltpu.SemaphoreType.DMA((count + 1,)),
+        ],
+        compiler_params=comm_params(number),
+        cost_estimate=lasting(32),
+        name="first_exchange",
+    )(*parts, inner, gains)
+
+
+def turn_heads(values, cosine, sine_table):
+    half = HEAD_DIM // 2
+    turned = []
+    for h in range(values.shape[0] // HEAD_DIM):
+        first = values[h * HEAD_DIM : h * HEAD_DIM + half]
+        second = values[h * HEAD_DIM + half : (h + 1) * HEAD_DIM]
+        turned.append(first * cosine - second * sine_table)
+        turned.append(second * cosine + first * sine_table)
+    return jnp.concatenate(turned, axis=0)
+
+
+def first_rows(tokens, gains, inner_all, output_own, cosine, sine_table, number):
+    size, width = tokens.shape
+    block = width // 8
+    quarter_rows = output_own.shape[0]
+    depth = quarter_rows // 2
+    pair_rows = 2 * HEAD_DIM
+    f32, bf16 = jnp.float32, jnp.bfloat16
+
+    def kernel(
+        x_ref, gains_ref, inner_ref, own_ref, cos_ref, sin_ref,
+        rows_ref, q_ref, pair_ref, w_ref, wo_ref, wo_all,
+        rows, rows_sent, rows_arrived, pair_v,
+        w_sent, w_arrived, o_sent, o_arrived, z_sent, z_arrived, p_sent, p_arrived, on_sent, on_arrived, kept_sem,
+    ):
+        f, t = lax.axis_index("fsdp"), lax.axis_index("tp")
+        place = columns(f, block)
+        far_first = (6, 7, 2, 4, 3, 5, 1)
+
+        def inner_slices(j):
+            quarter, side = lax.div(j, 2), lax.rem(j, 2)
+            return [
+                (
+                    inner_ref.at[quarter, pl.ds(pl.multiple_of(side * depth, depth), depth)],
+                    w_ref.at[pl.ds(0, depth), place],
+                ),
+                (
+                    inner_ref.at[quarter, pl.ds(2 * depth, pair_rows)],
+                    w_ref.at[pl.ds(depth, pair_rows), place],
+                ),
+            ]
+
+        def output_slice(j):
+            quarter, side = lax.div(j, 2), lax.rem(j, 2)
+            return (
+                wo_all.at[quarter, pl.ds(pl.multiple_of(side * depth, depth), depth)],
+                wo_ref.at[:, place],
+            )
+
+        kept = [
+            pltpu.make_async_copy(s, o, kept_sem.at[i]) for i, (s, o) in enumerate(inner_slices(f))
+        ]
+        kept.append(pltpu.make_async_copy(own_ref, wo_all.at[t], kept_sem.at[2]))
+        for c in kept:
+            c.start()
+        greet(everyone(f, t))
+        copies, along_z = [], []
+        for k in (2, 1, 3):
+            c = remote(own_ref, wo_all.at[t], z_sent.at[k], z_arrived.at[k], (f, lax.rem(t + k, 4)))
+            c.start()
+            along_z.append(c)
+        weights = []
+        for k in far_first:
+            for i, (s, o) in enumerate(inner_slices(f ^ k)):
+                c = remote(s, o, w_sent.at[k, i], w_arrived.at[k, i], (f ^ k, t))
+                c.start()
+                weights.append(c)
+        gain = jnp.concatenate([gains_ref[j, 0:1] for j in range(8)], axis=1)
+        wide = x_ref[...].astype(f32)
+        inverse = lax.rsqrt(jnp.mean(wide * wide, axis=1, keepdims=True) + epsilon)
+        rows[f] = (wide * inverse * gain).astype(bf16)
+        gather = PlaneGather(rows, rows_sent, rows_arrived)
+        gather.begin()
+        for k in range(PARTS):
+            gather.advance(k)
+        for c in kept[:2]:
+            c.wait()
+        for c in weights:
+            c.wait_recv()
+
+        def chunk(i, carry):
+            owner = f ^ i
+            lanes = columns(owner, size)
+            projected = outer_cols(w_ref[...], rows[owner])
+            cosine, sine = cos_ref[:, lanes], sin_ref[:, lanes]
+            queries = turn_heads(projected[:depth], cosine, sine).astype(bf16)
+            q_ref[:, lanes] = (queries.astype(f32) * HEAD_DIM ** (-0.5)).astype(bf16)
+            keys = turn_heads(projected[depth : depth + HEAD_DIM], cosine, sine)
+            pair = jnp.concatenate([keys, projected[depth + HEAD_DIM :]], axis=0)
+            pair_v[owner] = pair.T.astype(bf16)
+            return carry
+
+        spread = []
+
+        def spread_pair(i):
+            for k in (2, 1, 3):
+                c = remote(
+                    pair_v.at[f ^ i],
+                    pair_ref.at[t, f ^ i],
+                    p_sent.at[i // 2, k],
+                    p_arrived.at[i // 2, k],
+                    (f, lax.rem(t + k, 4)),
+                )
+                c.start()
+                spread.append((i, k, c))
+
+        gather.wait_core(0)
+        lax.fori_loop(0, 2, chunk, 0)
+        spread_pair(0)
+        gather.wait_core(3, 4)
+        lax.fori_loop(2, 6, chunk, 0)
+        spread_pair(2)
+        spread_pair(4)
+        gather.far()
+        gather.wait_core(5)
+        lax.fori_loop(6, 8, chunk, 0)
+        spread_pair(6)
+        own_pair = pltpu.make_async_copy(pair_v, pair_ref.at[t], kept_sem.at[3])
+        own_pair.start()
+        keep_rows = pltpu.make_async_copy(rows, rows_ref, kept_sem.at[4])
+        keep_rows.start()
+        kept[2].wait()
+        for c in along_z:
+            c.wait_recv()
+        for k in far_first:
+            s, o = output_slice(f ^ k)
+            c = remote(s, o, o_sent.at[k], o_arrived.at[k], (f ^ k, t))
+            c.start()
+            copies.append(c)
+        s, o = output_slice(f)
+        keep_output = pltpu.make_async_copy(s, o, kept_sem.at[5])
+        keep_output.start()
+        passed = []
+        for i, k, c in spread:
+            c.wait_recv()
+            spot = pair_ref.at[lax.rem(t + 4 - k, 4), f ^ i]
+            d = remote(spot, spot, on_sent.at[i // 2, k], on_arrived.at[i // 2, k], (f ^ CORE, t))
+            d.start()
+            passed.append(d)
+        for c in passed + copies:
+            c.wait()
+        for c in weights + along_z + [c for _, _, c in spread]:
+            c.wait_send()
+        gather.finish()
+        own_pair.wait()
+        keep_rows.wait()
+        keep_output.wait()
+
+    dma = pltpu.SemaphoreType.DMA
+    return pl.pallas_call(
+        kernel,
+        out_shape=[
+            jax.ShapeDtypeStruct((8, size, width), bf16),
+            jax.ShapeDtypeStruct((depth, 8 * size), bf16),
+            jax.ShapeDtypeStruct((4, 8, size, pair_rows), bf16),
+            jax.ShapeDtypeStruct((depth + pair_rows, width), bf16),
+            jax.ShapeDtypeStruct((depth, width), bf16),
+            jax.ShapeDtypeStruct((4, quarter_rows, block), bf16),
+        ],
+        in_specs=[IN_VMEM, IN_VMEM, ANYWHERE, ANYWHERE, IN_VMEM, IN_VMEM],
+        out_specs=[ANYWHERE, IN_VMEM, ANYWHERE, IN_VMEM, ANYWHERE, ANYWHERE],
+        scratch_shapes=[pltpu.VMEM((8, size, width), bf16)]
+        + GATHER_SEMAPHORES
+        + [
+            pltpu.VMEM((8, size, pair_rows), bf16),
+            dma((8, 2)),
+            dma((8, 2)),
+            dma((8,)),
+            dma((8,)),
+            dma((4,)),
+            dma((4,)),
+            dma((4, 4)),
+            dma((4, 4)),
+            dma((4, 4)),
+            dma((4, 4)),
+            dma((6,)),
+        ],
+        compiler_params=comm_params(number, 40 << 20),
+        cost_estimate=lasting(85),
+        name="first_rows",
+    )(tokens, gains, inner_all, output_own, cosine, sine_table)[:5]
+
+
+def backward_pairs(pair_parts, hidden, down_rows, middle, valid, grad_output, number):
+    size, width = middle.shape
+    units = hidden.shape[0]
+    depth = grad_output.shape[0]
+    _, chunks, height, _ = pair_parts.shape
+    half = chunks // 2
+    f32, bf16 = jnp.float32, jnp.bfloat16
+
+    def kernel(
+        p_ref, hidden_hbm, down_hbm, middle_ref, valid_ref, g_ref,
+        pair_ref, out_ref, spread_ref,
+        stage, other, held, from_x, from_y, last, sum_sent, sum_arrived,
+        hidden_v, down_w, load_sem, ra, s, rz, sent, arrived, g_sent, g_arrived, share,
+    ):
+        f, t = lax.axis_index("fsdp"), lax.axis_index("tp")
+        loads = [
+            pltpu.make_async_copy(hidden_hbm, hidden_v, load_sem.at[0]),
+            pltpu.make_async_copy(down_hbm, down_w, load_sem.at[1]),
+            pltpu.make_async_copy(g_ref.at[:, columns(f, size)], spread_ref.at[f], load_sem.at[2]),
+        ]
+        for c in loads:
+            c.start()
+        side = lax.rem(f, 2)
+        mine, theirs = pl.ds(side * half, half), pl.ds((1 - side) * half, half)
+        core = (f ^ CORE, t)
+        greet(everyone(f, t))
+        first = []
+        for k in (2, 1, 3, 0):
+            plane = lax.rem(t + k, 4)
+            c = remote(p_ref.at[plane, theirs], ra.at[k], sent.at[k], arrived.at[k], core)
+            c.start()
+            first.append((k, c))
+        out = []
+        for k, c in first:
+            c.wait_recv()
+            plane = lax.rem(t + k, 4)
+            both = p_ref[plane, mine].astype(f32) + ra[k].astype(f32)
+            if k:
+                s[k] = both.astype(bf16)
+                d = remote(s.at[k], rz.at[k], sent.at[3 + k], arrived.at[3 + k], (f, plane))
+                d.start()
+                out.append((k, d))
+            else:
+                pair_ref[mine] = both
+        for c in loads[:2]:
+            c.wait()
+        total = PlaneSum(stage, other, held, from_x, from_y, last, sum_sent, sum_arrived)
+        total.begin(chunk_part([(hidden_v, down_w)], size))
+        spread = []
+        for k in (6, 7, 2, 4, 3, 5, 1):
+            c = remote(
+                g_ref.at[:, columns(f ^ k, size)],
+                spread_ref.at[f],
+                g_sent.at[k],
+                g_arrived.at[k],
+                (f ^ k, t),
+            )
+            c.start()
+            spread.append(c)
+        total.turn()
+        for k, d in out:
+            d.wait_recv()
+            pair_ref[mine] += rz[k].astype(f32)
+        back = remote(pair_ref.at[mine], pair_ref.at[mine], sent.at[7], arrived.at[7], core)
+        back.start()
+        total.end(share)
+        out_ref[...] = jnp.where(valid_ref[...] > 0, middle_ref[...] + share[...], 0.0).astype(bf16)
+        back.wait()
+        for c in spread:
+            c.wait()
+        loads[2].wait()
+        for k, c in first + out:
+            c.wait_send()
+        total.finish()
+
+    dma = pltpu.SemaphoreType.DMA
+    return pl.pallas_call(
+        kernel,
+        out_shape=[
+            jax.ShapeDtypeStruct((chunks, height, size), f32),
+            jax.ShapeDtypeStruct((size, width), bf16),
+            jax.ShapeDtypeStruct((8, depth, size), bf16),
+        ],
+        in_specs=[IN_VMEM, ANYWHERE, ANYWHERE, IN_VMEM, IN_VMEM, ANYWHERE],
+        out_specs=[IN_VMEM, IN_VMEM, ANYWHERE],
+        scratch_shapes=sum_scratch(size, width)
+        + [pltpu.VMEM((units, 8 * size), bf16), pltpu.VMEM((units, width), bf16), dma((3,))]
+        + [pltpu.VMEM((4, half, height, size), bf16)] * 3
+        + [dma((8,)), dma((8,)), dma((8,)), dma((8,)), pltpu.VMEM((size, width), f32)],
+        compiler_params=comm_params(number, VMEM_MOST),
+        cost_estimate=lasting(50),
+        name="backward_pairs",
+    )(pair_parts, hidden, down_rows, middle, valid, grad_output)
+
+
+def backward_first(grad_inner, weights, rows, tokens, grad_middle, gain, number):
+    size, width = tokens.shape
+    depth = grad_inner.shape[0]
+    block = width // 8
+    f32, bf16 = jnp.float32, jnp.bfloat16
+
+    def kernel(
+        g_ref, w_ref, rows_hbm, x_ref, middle_ref, gain_ref,
+        tokens_grad_ref, gain_grad_ref, spread_ref,
+        stage, other, held, from_x, from_y, last, sum_sent, sum_arrived,
+        rows_v, load_sem, w_grad, sent, arrived,
+    ):
+        f, t = lax.axis_index("fsdp"), lax.axis_index("tp")
+        load = pltpu.make_async_copy(rows_hbm, rows_v, load_sem.at[0])
+        load.start()
+        greet([(f ^ k, t) for k in range(1, 8)])
+        total = PlaneSum(stage, other, held, from_x, from_y, last, sum_sent, sum_arrived)
+        total.begin(chunk_part([(g_ref, w_ref)], size))
+        load.wait()
+        spread = []
+
+        def weight_grad(k):
+            j = f ^ k
+            right = rows_v[:, :, columns(j, block)].reshape(8 * size, block)
+            w_grad[k] = dot_nn(g_ref[...], right).astype(bf16)
+            if k:
+                c = remote(w_grad.at[k], spread_ref.at[f], sent.at[k], arrived.at[k], (j, t))
+                c.start()
+                spread.append(c)
+
+        for k in (6, 7, 2, 4):
+            weight_grad(k)
+        total.turn()
+        for k in (3, 5, 1, 0):
+            weight_grad(k)
+        keep = pltpu.make_async_copy(w_grad.at[0], spread_ref.at[f], load_sem.at[1])
+        keep.start()
+        wide = x_ref[...].astype(f32)
+        inverse = lax.rsqrt(jnp.mean(wide * wide, axis=1, keepdims=True) + epsilon)
+        normed = wide * inverse
+        total.end(tokens_grad_ref)
+        grad = tokens_grad_ref[...]
+        gain_grad_ref[...] = jnp.sum(grad * normed, axis=0, keepdims=True)
+        tokens_grad_ref[...] = middle_ref[...] + norm_back(grad, gain_ref[...], normed, inverse)
+        for c in spread:
+            c.wait()
+        keep.wait()
+        total.finish()
+
+    dma = pltpu.SemaphoreType.DMA
+    return pl.pallas_call(
+        kernel,
+        out_shape=[
+            jax.ShapeDtypeStruct((size, width), f32),
+            jax.ShapeDtypeStruct((1, width), f32),
+            jax.ShapeDtypeStruct((8, depth, block), bf16),
+        ],
+        in_specs=[IN_VMEM, IN_VMEM, ANYWHERE, IN_VMEM, IN_VMEM, IN_VMEM],
+        out_specs=[IN_VMEM, IN_VMEM, ANYWHERE],
+        scratch_shapes=sum_scratch(size, width)
+        + [
+            pltpu.VMEM((8, size, width), bf16),
+            dma((2,)),
+            pltpu.VMEM((8, depth, block), bf16),
+            dma((8,)),
+            dma((8,)),
+        ],
+        compiler_params=comm_params(number, VMEM_MOST),
+        cost_estimate=lasting(60),
+        name="backward_first",
+    )(grad_inner, weights, rows, tokens, grad_middle, gain)
+
+
+def last_exchange(hidden_grads, gain_parts, number):
+    count, units, width = hidden_grads.shape
+    block = width // 8
+    f32, bf16 = jnp.float32, jnp.bfloat16
+    far_first = (6, 7, 2, 4, 3, 5, 1)
+
+    def kernel(
+        source, gains_ref, target, sums_ref, taken, planes, sent, arrived, z_sent, z_arrived, kept_sem
+    ):
+        f, t = lax.axis_index("fsdp"), lax.axis_index("tp")
+        keep = pltpu.make_async_copy(source.at[:, :, columns(f, block)], target.at[f], kept_sem)
+        keep.start()
+        greet(everyone(f, t))
+        gains = []
+        for k in far_first:
+            c = remote(
+                gains_ref.at[f ^ k], taken.at[k], sent.at[k, 0], arrived.at[k, 0], (f ^ k, t)
+            )
+            c.start()
+            gains.append(c)
+        copies = []
+        for k in far_first:
+            c = remote(
+                source.at[:, :, columns(f ^ k, block)],
+                target.at[f],
+                sent.at[k, 1],
+                arrived.at[k, 1],
+                (f ^ k, t),
+            )
+            c.start()
+            copies.append(c)
+        total = gains_ref[f]
+        for k, c in zip(far_first, gains):
+            c.wait_recv()
+            total += taken[k]
+        planes[0] = total
+        along_z = []
+        for k in (1, 2, 3):
+            c = remote(planes.at[0], planes.at[k], z_sent.at[k], z_arrived.at[k], (f, lax.rem(t + k, 4)))
+            c.start()
+            along_z.append(c)
+        for c in along_z:
+            c.wait_recv()
+        sums = planes[lax.rem(t, 4)]
+        for plane in (1, 2, 3):
+            sums += planes[lax.rem(t + 4 - plane, 4)]
+        sums_ref[...] = sums
+        for c in [keep] + copies:
+            c.wait()
+        for c in gains + along_z:
+            c.wait_send()
+
+    dma = pltpu.SemaphoreType.DMA
+    return pl.pallas_call(
+        kernel,
+        out_shape=[
+            jax.ShapeDtypeStruct((8, count, units, block), bf16),
+            jax.ShapeDtypeStruct(gain_parts.shape[1:], f32),
+        ],
+        in_specs=[ANYWHERE, IN_VMEM],
+        out_specs=[ANYWHERE, IN_VMEM],
+        scratch_shapes=[
+            pltpu.VMEM(gain_parts.shape, f32),
+            pltpu.VMEM((4, *gain_parts.shape[1:]), f32),
+            dma((8, 2)),
+            dma((8, 2)),
+            dma((4,)),
+            dma((4,)),
+            dma,
+        ],
+        compiler_params=comm_params(number),
+        cost_estimate=lasting(28),
+        name="last_exchange",
+    )(hidden_grads, gain_parts)
+
+
+def dot_nn(left, right):
+    return jnp.dot(left, right, preferred_element_type=jnp.float32)
+
+
+def seen_keys(begin_row, first_key, first_query, shape):
+    key_slot = first_key + lax.broadcasted_iota(jnp.int32, shape, 0)
+    query_slot = first_query + lax.broadcasted_iota(jnp.int32, (1, shape[1]), 1)
+    return (key_slot <= query_slot) & (key_slot >= begin_row)
+
+
+def head_lanes(block, heads):
+    return jnp.concatenate([block[h * HEAD_DIM : (h + 1) * HEAD_DIM] for h in range(heads)], axis=1)
+
+
+def attend(info, begins, queries, pair):
+    depth, slots = queries.shape
+    heads = depth // HEAD_DIM
+    size = slots // 8
+    span = heads * size
+
+    def kernel(info_ref, begin_ref, q_ref, kv_ref, o_ref, l_ref, q_s, m_s, t_s, a_s):
+        f = pl.program_id(0)
+        low, middle, own = info_ref[f, 0], info_ref[f, 1], info_ref[f, 2]
+        q_s[...] = head_lanes(q_ref[...], heads)
+        m_s[...] = jnp.full_like(m_s, -1e30)
+        t_s[...] = jnp.zeros_like(t_s)
+        a_s[...] = jnp.zeros_like(a_s)
+
+        def step(g, masked):
+            block = kv_ref[lax.rem(g, 4), lax.div(g, 4)]
+            keys, values = block[:, :HEAD_DIM], block[:, HEAD_DIM:]
+            value_cols = values.astype(jnp.float32).T.astype(jnp.bfloat16)
+            if masked:
+                seen = seen_keys(begin_ref[0], g * size, own * size, (size, size))
+            for h in range(heads):
+                lanes = pl.ds(h * size, size)
+                scores = dot_nn(keys, q_s[:, lanes])
+                if masked:
+                    scores = jnp.where(seen, scores, -1e30)
+                largest = m_s[:, lanes]
+                higher = jnp.maximum(largest, jnp.max(scores, axis=0, keepdims=True))
+                raised = jnp.exp(scores - higher)
+                fade = jnp.exp(largest - higher)
+                m_s[:, lanes] = higher
+                t_s[:, lanes] = t_s[:, lanes] * fade + jnp.sum(raised, axis=0, keepdims=True)
+                a_s[:, lanes] = a_s[:, lanes] * fade + dot_nn(
+                    value_cols, raised.astype(jnp.bfloat16)
+                )
+
+        def masked_step(g, carry):
+            step(g, True)
+            return carry
+
+        def plain_step(g, carry):
+            step(g, False)
+            return carry
+
+        step(own, True)
+        lax.fori_loop(low, middle, masked_step, 0)
+        lax.fori_loop(middle, own, plain_step, 0)
+        result = a_s[...] / t_s[...]
+        for h in range(heads):
+            o_ref[h * HEAD_DIM : (h + 1) * HEAD_DIM] = result[:, h * size : (h + 1) * size].astype(
+                jnp.bfloat16
+            )
+        l_ref[0] = m_s[...] + jnp.log(t_s[...])
+
+    return pl.pallas_call(
+        kernel,
+        grid_spec=pltpu.PrefetchScalarGridSpec(
+            num_scalar_prefetch=1,
+            grid=(8,),
+            in_specs=[
+                pl.BlockSpec((1, 1, size), lambda f, info: (f, 0, 0)),
+                pl.BlockSpec((depth, size), lambda f, info: (0, f)),
+                pl.BlockSpec((4, 8, size, 2 * HEAD_DIM), lambda f, info: (0, 0, 0, 0)),
+            ],
+            out_specs=[
+                pl.BlockSpec((depth, size), lambda f, info: (0, f)),
+                pl.BlockSpec((1, 1, span), lambda f, info: (f, 0, 0)),
+            ],
+            scratch_shapes=[
+                pltpu.VMEM((HEAD_DIM, span), jnp.bfloat16),
+                pltpu.VMEM((1, span), jnp.float32),
+                pltpu.VMEM((1, span), jnp.float32),
+                pltpu.VMEM((HEAD_DIM, span), jnp.float32),
+            ],
+        ),
+        out_shape=[
+            jax.ShapeDtypeStruct((depth, slots), jnp.bfloat16),
+            jax.ShapeDtypeStruct((8, 1, span), jnp.float32),
+        ],
+        compiler_params=pltpu.CompilerParams(vmem_limit_bytes=40 << 20),
+        cost_estimate=lasting(75),
+        name="attend",
+    )(info, begins, queries, pair)
+
+
+def attend_back(info, begins, queries, pair, outputs, grads, totals):
+    depth, slots = queries.shape
+    heads = depth // HEAD_DIM
+    size = slots // 8
+    span = heads * size
+
+    def kernel(
+        info_ref, begin_ref, q_ref, kv_ref, o_ref, g_ref, l_ref, dq_ref, dkv_ref, q_s, g_s, d_s, a_s, w_s
+    ):
+        f = pl.program_id(0)
+        low, middle, own = info_ref[f, 0], info_ref[f, 1], info_ref[f, 2]
+
+        @pl.when(f == 0)
+        def _():
+            w_s[...] = jnp.zeros_like(w_s)
+
+        q_s[...] = head_lanes(q_ref[...], heads)
+        g_s[...] = head_lanes(g_ref[...], heads)
+        out_lanes = head_lanes(o_ref[...], heads).astype(jnp.float32)
+        d_s[...] = jnp.sum(out_lanes * g_s[...].astype(jnp.float32), axis=0, keepdims=True)
+        a_s[...] = jnp.zeros_like(a_s)
+
+        def step(g, masked):
+            block = kv_ref[lax.rem(g, 4), lax.div(g, 4)]
+            keys, values = block[:, :HEAD_DIM], block[:, HEAD_DIM:]
+            key_cols = keys.astype(jnp.float32).T.astype(jnp.bfloat16)
+            if masked:
+                seen = seen_keys(begin_ref[0], g * size, own * size, (size, size))
+            grad_keys = jnp.zeros((HEAD_DIM, size), jnp.float32)
+            grad_values = jnp.zeros((HEAD_DIM, size), jnp.float32)
+            for h in range(heads):
+                lanes = pl.ds(h * size, size)
+                query, grad = q_s[:, lanes], g_s[:, lanes]
+                raised = jnp.exp(dot_nn(keys, query) - l_ref[0, :, lanes])
+                if masked:
+                    raised = jnp.where(seen, raised, 0.0)
+                grad_probs = dot_nn(values, grad)
+                scores = (raised * (grad_probs - d_s[:, lanes])).astype(jnp.bfloat16)
+                grad_values += outer_cols(grad, raised.astype(jnp.bfloat16))
+                grad_keys += outer_cols(query, scores)
+                a_s[:, lanes] += dot_nn(key_cols, scores)
+            w_s[lax.rem(g, 4), lax.div(g, 4), :HEAD_DIM] += grad_keys
+            w_s[lax.rem(g, 4), lax.div(g, 4), HEAD_DIM:] += grad_values
+
+        def masked_step(g, carry):
+            step(g, True)
+            return carry
+
+        def plain_step(g, carry):
+            step(g, False)
+            return carry
+
+        step(own, True)
+        lax.fori_loop(low, middle, masked_step, 0)
+        lax.fori_loop(middle, own, plain_step, 0)
+        result = a_s[...] * HEAD_DIM ** (-0.5)
+        for h in range(heads):
+            dq_ref[h * HEAD_DIM : (h + 1) * HEAD_DIM] = result[:, h * size : (h + 1) * size]
+
+        @pl.when(f == 7)
+        def _():
+            dkv_ref[...] = w_s[...].astype(jnp.bfloat16)
+
+    return pl.pallas_call(
+        kernel,
+        grid_spec=pltpu.PrefetchScalarGridSpec(
+            num_scalar_prefetch=1,
+            grid=(8,),
+            in_specs=[
+                pl.BlockSpec((1, 1, size), lambda f, info: (f, 0, 0)),
+                pl.BlockSpec((depth, size), lambda f, info: (0, f)),
+                pl.BlockSpec((4, 8, size, 2 * HEAD_DIM), lambda f, info: (0, 0, 0, 0)),
+                pl.BlockSpec((depth, size), lambda f, info: (0, f)),
+                pl.BlockSpec((depth, size), lambda f, info: (0, f)),
+                pl.BlockSpec((1, 1, span), lambda f, info: (f, 0, 0)),
+            ],
+            out_specs=[
+                pl.BlockSpec((depth, size), lambda f, info: (0, f)),
+                pl.BlockSpec((4, 8, 2 * HEAD_DIM, size), lambda f, info: (0, 0, 0, 0)),
+            ],
+            scratch_shapes=[
+                pltpu.VMEM((HEAD_DIM, span), jnp.bfloat16),
+                pltpu.VMEM((HEAD_DIM, span), jnp.bfloat16),
+                pltpu.VMEM((1, span), jnp.float32),
+                pltpu.VMEM((HEAD_DIM, span), jnp.float32),
+                pltpu.VMEM((4, 8, 2 * HEAD_DIM, size), jnp.float32),
+            ],
+        ),
+        out_shape=[
+            jax.ShapeDtypeStruct((depth, slots), jnp.float32),
+            jax.ShapeDtypeStruct((4, 8, 2 * HEAD_DIM, size), jnp.bfloat16),
+        ],
+        compiler_params=pltpu.CompilerParams(vmem_limit_bytes=40 << 20),
+        cost_estimate=lasting(80),
+        name="attend_back",
+    )(info, begins, queries, pair, outputs, grads, totals)
+
+
+def turn(values, cosine, sine_table):
+    heads = values.shape[0] // HEAD_DIM
+    split = values.reshape(heads, 2, HEAD_DIM // 2, values.shape[1])
+    first, second = split[:, 0], split[:, 1]
+    turned = jnp.stack(
+        [first * cosine - second * sine_table, second * cosine + first * sine_table], axis=1
+    )
+    return turned.reshape(values.shape)
+
+
+def turn_back(values, cosine, sine_table):
+    return turn(values, cosine, -sine_table)
+
+
+def segment_begins(slots, lengths):
+    seq_index = jnp.arange(lengths.shape[0], dtype=jnp.int32)
+    ends = jnp.sum(jnp.where(seq_index[:, None] >= seq_index[None, :], lengths[None, :], 0), axis=1)
+    passed = slots[:, None] >= ends[None, :]
+    begins = jnp.sum(jnp.where(passed, lengths[None, :], 0), axis=1)
+    return begins, slots < ends[-1]
+
+
+def local_plane(
+    tokens,
+    attn_gain,
+    query_weight,
+    key_weight,
+    value_weight,
+    output_weight,
+    mlp_gain,
+    gate_weight,
+    up_weight,
+    down_weight,
+    out_grad,
+    lengths,
+):
+    size, width = tokens.shape
+    f = lax.axis_index("fsdp")
+    t = lax.axis_index("tp")
+    block = query_weight.shape[0]
+    head_rows = query_weight.shape[1] // 2
+    units = gate_weight.shape[1] // 8
+    bf16, f32 = jnp.bfloat16, jnp.float32
+
+    inner_own = jnp.concatenate([query_weight.T, key_weight.T, value_weight.T], axis=0)
+    hidden_parts = [w.reshape(8, units, block) for w in (down_weight, gate_weight.T, up_weight.T)]
+    gains_own = jnp.stack([attn_gain, mlp_gain]).astype(f32)
+    down_part, gate_part, up_part, inner_all, gains_all = first_exchange(
+        hidden_parts, inner_own, gains_own, 1
+    )
+    down_rows = lax.all_gather(down_part, "tp", axis=0, tiled=True)
+    gate_rows = lax.all_gather(gate_part, "tp", axis=0, tiled=True)
+    up_rows = lax.all_gather(up_part, "tp", axis=0, tiled=True)
+    gains = jnp.moveaxis(gains_all, 0, 1).reshape(2, width)
+    gain_first, gain_second = gains[0:1], gains[1:2]
+
+    my_slots = (f * 4 + t) * size + jnp.arange(size, dtype=jnp.int32)
+    _, my_valid = segment_begins(my_slots, lengths)
+    valid_rows = my_valid[:, None]
+    chunk_index = jnp.arange(8, dtype=jnp.int32) * 4 + t
+    plane_slots = (chunk_index[:, None] * size + jnp.arange(size, dtype=jnp.int32)[None, :]).reshape(-1)
+    begins, plane_valid = segment_begins(plane_slots, lengths)
+    positions = jnp.where(plane_valid, plane_slots - begins, 0)
+    begins = begins.reshape(8, 1, size)
+    info = jnp.stack(
+        [
+            begins[:, 0, 0] // size,
+            jnp.minimum((begins[:, 0, size - 1] + size - 1) // size, chunk_index),
+            chunk_index,
+        ],
+        axis=1,
+    ).astype(jnp.int32)
+    ladder = jnp.arange(HEAD_DIM // 2).astype(f32)
+    frequency = 10000.0 ** (-2.0 * ladder / HEAD_DIM)
+    angles = positions.astype(f32)[None, :] * frequency[:, None]
+    cosine, sine_table = jnp.cos(angles), jnp.sin(angles)
+
+    rows_first, queries, pair, inner_rows_w, output_rows = first_rows(
+        tokens, gains_all, inner_all, output_weight, cosine, sine_table, 2
+    )
+    attended, totals = attend(info, begins, queries, pair)
+    grad_rows_own = jnp.where(valid_rows, out_grad, jnp.zeros_like(out_grad))
+    middle, row_second, grad_rows = forward_output(
+        attended, output_rows, tokens, gain_second, grad_rows_own, 4
+    )
+    rows_second, hidden, grad_gate_low, grad_up_low = forward_hidden(
+        row_second, grad_rows, gate_rows, up_rows, down_rows, 5
+    )
+    (
+        grad_middle,
+        gain_second_part,
+        grad_output_w,
+        grad_attended,
+        hidden_grads,
+    ) = backward_middle(
+        grad_gate_low,
+        grad_up_low,
+        hidden,
+        gate_rows,
+        up_rows,
+        rows_second,
+        grad_rows,
+        output_rows,
+        attended,
+        middle,
+        grad_rows_own,
+        gain_second,
+        6,
+    )
+    hidden_grads = lax.psum_scatter(
+        hidden_grads.reshape(12 * units, width), "tp", scatter_dimension=0, tiled=True
+    )
+    grad_queries, grad_pair_parts = attend_back(
+        info, begins, queries, pair, attended, grad_attended, totals
+    )
+    grad_pair, layer_out, output_parts = backward_pairs(
+        grad_pair_parts, hidden, down_rows, middle, valid_rows.astype(f32), grad_output_w, 7
+    )
+    grad_pair = jnp.moveaxis(grad_pair, 0, 1).reshape(2 * HEAD_DIM, 8 * size)
+    grad_query_low = turn_back(grad_queries, cosine, sine_table).astype(bf16)
+    grad_key_low = turn_back(grad_pair[:HEAD_DIM], cosine, sine_table)
+    first_core = lax.rem(f, 2) == 0
+    grad_single = jnp.where(first_core, grad_key_low, grad_pair[HEAD_DIM:]).astype(bf16)
+    grad_inner = jnp.concatenate([grad_query_low, grad_single], axis=0)
+    single_rows = jnp.where(
+        first_core,
+        inner_rows_w[head_rows : head_rows + HEAD_DIM],
+        inner_rows_w[head_rows + HEAD_DIM :],
+    )
+    single_weights = jnp.concatenate([inner_rows_w[:head_rows], single_rows], axis=0)
+    tokens_grad, gain_first_part, inner_parts = backward_first(
+        grad_inner, single_weights, rows_first, tokens, grad_middle, gain_first, 8
+    )
+
+    def along_z(parts):
+        rows = parts.shape[1]
+        flat = parts.reshape(8 * rows, block)
+        return lax.psum_scatter(flat, "tp", scatter_dimension=0, tiled=True).reshape(2, rows, block)
+
+    output_parts, hidden_grads = lax.optimization_barrier((output_parts, hidden_grads))
+    output_own = along_z(output_parts)
+    inner_parts, output_own = lax.optimization_barrier((inner_parts, output_own))
+    inner_grads = along_z(inner_parts)
+    gain_parts = jnp.concatenate([gain_first_part, gain_second_part], axis=0)
+    gain_parts = jnp.moveaxis(gain_parts.reshape(2, 8, block), 1, 0)
+    hidden_own, gain_sums = last_exchange(hidden_grads.reshape(3, units, width), gain_parts, 9)
+    own_down, own_gate, own_up = (hidden_own[:, n].reshape(8 * units, block) for n in range(3))
+    return (
+        layer_out,
+        tokens_grad,
+        gain_sums[0],
+        inner_grads[:, :head_rows].reshape(2 * head_rows, block).T.astype(f32),
+        inner_grads[0, head_rows:].T.astype(f32),
+        inner_grads[1, head_rows:].T.astype(f32),
+        output_own.reshape(2 * head_rows, block).astype(f32),
+        gain_sums[1],
+        own_gate.T.astype(f32),
+        own_up.T.astype(f32),
+        own_down.astype(f32),
+    )
+
+
 def solution(mesh):
+    plane = dict(mesh.shape) == {"fsdp": 8, "tp": 4}
+    body = local_plane if plane else local
     in_specs = (
         P(("fsdp", "tp"), None),
         P("fsdp"),
@@ -374,4 +1745,4 @@
         P("fsdp", "tp"),
         P("tp", "fsdp"),
     )
-    return jax.shard_map(local, mesh=mesh, in_specs=in_specs, out_specs=out_specs, check_vma=False)
+    return jax.shard_map(body, mesh=mesh, in_specs=in_specs, out_specs=out_specs, check_vma=False)

time: 1820 us -> 766 us (0.42)
  waiting for transfers between devices: 805 us -> 1.43 us
  Pallas kernels: 0 us -> 698 us
  matrix products: 580 us -> 0 us
  other arithmetic: 242 us -> 16.6 us
  blocking collectives: 66.9 us -> 0 us
  local copies, waits for them, and re-layouts: 83.9 us -> 26 us
  starting transfers between devices: 18.5 us -> 0.24 us
    pallas_call x0 -> x10, Pallas kernels: none -> 698 us  [the longest x1 117 us: backward_pairs(): pl.pallas_call(kernel, out_shape=[jax.ShapeDtypeStruct((chunks, height, s...]
    dot_general x71 -> x0, matrix products: 580 us -> none  [the longest x29 305 us: outer_cols(): lax.dot_general(left, right, (((1,), (1,)), ((), ())), preferred_element_...]
    reduce_scatter x11 -> x3, waiting for transfers between devices: 398 us -> 0.01 us  [the longest x2 0.01 us: along_z(): lax.psum_scatter(flat, 'tp', scatter_dimension=0, tiled=True)]
    all_gather x9 -> x3, waiting for transfers between devices: 392 us -> 0.01 us  [the longest x1 0.01 us: local_plane(): gate_rows = lax.all_gather(gate_part, 'tp', axis=0, tiled=True)]
    convert_element_type x24 -> x10, other arithmetic: 170 us -> 6.64 us  [the longest x1 1.47 us: local_plane(): valid_rows.astype(f32)]
    reduce_sum x17 -> x2, other arithmetic: 56.5 us -> 0.21 us  [the longest x1 0.12 us: segment_begins(): jnp.sum(jnp.where(seq_index[:, None] >= seq_index[None, :], lengths[None,...]
    all_gather x4 -> x0, blocking collectives: 41.1 us -> none  [the longest x1 11.2 us: local(): lax.all_gather(key_weight, 'fsdp', axis=0, tiled=True)]
    while x48 -> x0, local copies, waits for them, and re-layouts: 37.3 us -> none
  transfers between devices with their start and end apart: 28 -> 6, of which waited for: 18 -> 0; matrix products, arithmetic and copies ran while one was open for 45% -> 3% of each run, Pallas kernels for 0% -> 70%
where the time goes in v2:
time: 766 us; the launch traced here: 757 us
  Pallas kernels  698 us (91%)
  local copies, waits for them, and re-layouts  26 us (3%)
  other arithmetic  16.6 us (2%)
  between operations  15.2 us (2%)
    pallas_call x1, Pallas kernels, backward_pairs(): pl.pallas_call(kernel, out_shape=[jax.ShapeDtypeStruct((chunks, height, s...  117 us
    pallas_call x1, Pallas kernels, first_rows(): pl.pallas_call(kernel, out_shape=[jax.ShapeDtypeStruct((8, size, width),...  98.8 us
    pallas_call x1, Pallas kernels, backward_middle(): pl.pallas_call(kernel, out_shape=[jax.ShapeDtypeStruct((size, width), f32...  89.9 us
    pallas_call x1, Pallas kernels, forward_output(): pl.pallas_call(kernel, out_shape=[jax.ShapeDtypeStruct((size, width), f32...  82.9 us
    pallas_call x1, Pallas kernels, attend_back(): pl.pallas_call(kernel, grid_spec=pltpu.PrefetchScalarGridSpec(num_scalar_...  71.5 us
    pallas_call x1, Pallas kernels, attend(): pl.pallas_call(kernel, grid_spec=pltpu.PrefetchScalarGridSpec(num_scalar_...  70.9 us
    pallas_call x1, Pallas kernels, backward_first(): pl.pallas_call(kernel, out_shape=[jax.ShapeDtypeStruct((size, width), f32...  60.4 us
    pallas_call x1, Pallas kernels, forward_hidden(): pl.pallas_call(kernel, out_shape=[jax.ShapeDtypeStruct((8, size, width),...  46.1 us
  transfers between devices with their start and end apart: 6, of which 0 were waited for; matrix products, arithmetic and copies ran while one was open for 3% of the time, Pallas kernels for 70%

profile of v2, /device:TPU:0, one launch (start us, length us, event | category | flops | bytes accessed | tf_op | source)
XLA Modules:
  0.0 757.4 jit_solution(615437681381468015)
XLA Ops:
  7.3 0.7 stack.27
  8.0 0.7 stack.28
  8.6 1.1 copy.80
  9.7 2.2 copy.78
  12.0 1.1 copy.79
  13.1 0.6 maximum_convert_fusion.refs_4_
  13.7 0.7 pad_maximum_fusion.4.refs_3_
  14.4 31.7 %first_exchange.1 = (bf16[176,2048]{1,0:T(8,128)(2,1)}, bf16[176,2048]{1,0:T(8,128)(2,1)}, bf16[176,2048]{1,0:T(8,128)(2,1)}, bf16[4,640,256]{2,1,0:T(8,128)(2,1)}, f32[8,2,256]{2,1,0:T(2,128)}) custom-call(bf16[8,176,256]{2,1,0:T(8,128)(2,1)} %bitcast.107, bf16[8,176,256]{2,1,0:T(8,128)(2,1)} %bitcast.88, bf16[8,176,256]{2,1,0:T(8,128)(2,1)} %bitcast.89, ...), custom_call_target="tpu_custom_call" | custom-call | flops 35200000000 | bytes 1000000 | tf_op jit(solution)/shard_map/first_exchange/pallas_call | solution.py:911
  46.2 0.7 all-gather.6.cloned.1.call-update
  47.0 0.7 all-gather.8.cloned.1.call-update
  47.9 0.6 slice.79
  48.6 0.7 add_compare_fusion.1
  49.3 0.7 select_convert_fusion
  50.1 0.6 fusion.18
  50.7 1.7 fusion.9
  52.5 1.1 broadcast_select_fusion.dy_ref
  53.7 1.3 copy-done.10
  55.0 98.8 %first_rows.1 = (bf16[8,256,2048]{2,1,0:T(8,128)(2,1)}, bf16[256,2048]{1,0:T(8,128)(2,1)S(1)}, bf16[4,8,256,128]{3,2,1,0:T(8,128)(2,1)S(1)}, bf16[384,2048]{1,0:...) custom-call(bf16[256,2048]{1,0:T(8,128)(2,1)S(1)} %copy-done.8, ...), custom_call_target="tpu_custom_call" | custom-call | flops 93499998208 | bytes 1000000 | tf_op jit(solution)/shard_map/first_rows/pallas_call | solution.py:1082
  153.8 70.9 %attend.1 = (bf16[256,2048]{1,0:T(8,128)(2,1)S(1)}, f32[8,1,1024]{2,1,0:T(1,128)S(1)}) custom-call(s32[8,3]{1,0:T(8,128)S(1)} %pad_add_fusion.info_ref, s32[8,1,256]{2,1,0:T(1,128)S(1)} %bitcast.73, bf16[256,2048]{1,0:T(8,128)(2,1)S(1)} %get-tuple-element.51.q_ref, bf16[4,8,256,128]{3,2,1,0:T(8,128)(2,1)S(1)} %get-tuple-element.52.kv_ref), custom_call_target="tpu_custom_call" | custom-call | flops 82500001792 | bytes 1000000 | tf_op jit(solution)/shard_map/attend/pallas_call | solution.py:1427
  224.8 82.9 %forward_output.1 = (f32[256,2048]{1,0:T(8,128)}, bf16[256,2048]{1,0:T(8,128)(2,1)S(1)}, bf16[8,256,2048]{2,1,0:T(8,128)(2,1)}) custom-call(bf16[256,2048]{1,0:T(8,128)(2,1)S(1)} %get-tuple-element.53.o_ref, bf16[256,2048]{1,0:T(8,128)(2,1)S(1)} %get-tuple-element.54.w_ref, bf16[256,2048]{1,0:T(8,128)(2,1)} %x_ref.5, f32[1,2048]{1,0:T(1,128)S(1)} %bitcast.76, ...), custom_call_target="tpu_custom_call" | custom-call | flops 82500001792 | bytes 1000000 | tf_op jit(solution)/shard_map/forward_output/pallas_call | solution.py:585
  307.7 1.0 copy-done.15
  308.7 46.1 %forward_hidden.1 = (bf16[8,256,2048]{2,1,0:T(8,128)(2,1)}, bf16[704,2048]{1,0:T(8,128)(2,1)S(1)}, bf16[704,2048]{1,0:T(8,128)(2,1)}, bf16[704,2048]{1,0:T(8,128)(2,1)}) custom-call(bf16[256,2048]{1,0:T(8,128)(2,1)S(1)} %get-tuple-element.55.row_ref, bf16[8,256,2048]{2,1,0:T(8,128)(2,1)} %get-tuple-element.56.dys_hbm, ...), custom_call_target="tpu_custom_call" | custom-call | flops 60500000768 | bytes 1000000 | tf_op jit(solution)/shard_map/forward_hidden/pallas_call | solution.py:687
  354.8 1.5 copy-done.11
  356.3 89.9 %backward_middle.1 = (f32[256,2048]{1,0:T(8,128)}, f32[1,2048]{1,0:T(1,128)}, bf16[256,2048]{1,0:T(8,128)(2,1)}, bf16[256,2048]{1,0:T(8,128)(2,1)}, bf16[4,3,176,2048]{3,2,1,0:T(8,128)(2,1)}) custom-call(bf16[704,2048]{1,0:T(8,128)(2,1)} %get-tuple-element.60.dgate_hbm, bf16[704,2048]{1,0:T(8,128)(2,1)} %get-tuple-element.61.dup_hbm, ...), custom_call_target="tpu_custom_call" | custom-call | flops 101200003072 | bytes 1000000 | tf_op jit(solution)/shard_map/backward_middle/pallas_call | solution.py:840
  446.5 1.5 fusion.8.valid_ref
  448.0 1.1 pad_maximum_fusion.1.w_ref
  449.2 71.5 %attend_back.1 = (f32[256,2048]{1,0:T(8,128)S(1)}, bf16[4,8,128,256]{3,2,1,0:T(8,128)(2,1)S(1)}) custom-call(s32[8,3]{1,0:T(8,128)S(1)} %copy-done.7, s32[8,1,256]{2,1,0:T(1,128)S(1)} %bitcast.74, bf16[256,2048]{1,0:T(8,128)(2,1)S(1)} %copy-done.19, bf16[4,8,256,128]{3,2,1,0:T(8,128)(2,1)S(1)} %copy-done.14, bf16[256,2048]{1,0:T(8,128)(2,1)S(1)} %copy-done.16, ...), custom_call_target="tpu_custom_call" | custom-call | flops 88000004096 | bytes 1000000 | tf_op jit(solution)/shard_map/attend_back/pallas_call | solution.py:1521
  520.7 1.3 copy-done.12
  522.1 116.5 %backward_pairs.1 = (f32[8,128,256]{2,1,0:T(8,128)}, bf16[256,2048]{1,0:T(8,128)(2,1)}, bf16[8,256,256]{2,1,0:T(8,128)(2,1)}) custom-call(bf16[4,8,128,256]{3,2,1,0:T(8,128)(2,1)} %copy-done.12, bf16[704,2048]{1,0:T(8,128)(2,1)} %copy-done.11, bf16[704,2048]{1,0:T(8,128)(2,1)} %all-gather.8.cloned.1.call-done.down_hbm, ...), custom_call_target="tpu_custom_call" | custom-call | flops 54999998464 | bytes 1000000 | tf_op jit(solution)/shard_map/backward_pairs/pallas_call | solution.py:1192
  638.6 1.1 slice.107
  639.7 0.3 copy.82
  640.1 1.1 slice_bitcast_fusion
  641.3 1.2 fusion.3
  643.0 1.1 pad_maximum_fusion.g_ref
  644.2 60.4 %backward_first.1 = (f32[256,2048]{1,0:T(8,128)}, f32[1,2048]{1,0:T(1,128)}, bf16[8,320,256]{2,1,0:T(8,128)(2,1)}) custom-call(bf16[320,2048]{1,0:T(8,128)(2,1)} %pad_maximum_fusion.g_ref, bf16[320,2048]{1,0:T(8,128)(2,1)} %pad_maximum_fusion.1.w_ref, bf16[8,256,2048]{2,1,0:T(8,128)(2,1)} %get-tuple-element.73.rows_hbm, bf16[256,2048]{1,0:T(8,128)(2,1)} %x_ref.5, ...), custom_call_target="tpu_custom_call" | custom-call | flops 65999998976 | bytes 1000000 | tf_op jit(solution)/shard_map/backward_first/pallas_call | solution.py:1261
  704.7 1.3 pad_maximum_fusion.5
  706.1 29.2 %last_exchange.1 = (bf16[8,3,176,256]{3,2,1,0:T(8,128)(2,1)}, f32[2,256]{1,0:T(2,128)}) custom-call(bf16[3,176,2048]{2,1,0:T(8,128)(2,1)} %bitcast.106, f32[8,2,256]{2,1,0:T(2,128)} %bitcast.100), custom_call_target="tpu_custom_call" | custom-call | flops 30799998976 | bytes 1000000 | tf_op jit(solution)/shard_map/last_exchange/pallas_call | solution.py:1337
  735.2 1.7 fusion.17
  737.1 1.5 copy.86
  738.8 1.5 copy.85
  740.4 0.6 fusion.20
  740.9 1.3 bitcast_convert_fusion
  742.2 0.8 bitcast_convert_fusion.3
  743.0 1.4 convert_bitcast_fusion
  744.5 1.0 slice.112
  745.5 1.0 copy.84
  746.5 2.3 copy.91
  748.8 1.3 copy.92
  (103 shorter events, 2.0 us)
Async XLA Ops:
  7.2 4.8 copy-start.24
  7.2 6.5 copy-start.28
  7.2 6.5 copy-start.29
  7.2 301.4 %all-gather.4.cloned.1.call-start = ((), (), s32[]{:S(2)}) async-start(), calls=%async_computation.3 | async-start | bytes 3604480 | tf_op jit(solution)/shard_map/all_gather | solution.py:1607
  46.1 1.6 copy-start.34
  46.1 4.0 copy-start.4
  46.1 6.3 copy-start.23
  46.2 262.5 %all-gather.6.cloned.1.call-start = ((), (), s32[]{:S(2)}) async-start(), calls=%async_computation.4 | async-start | bytes 3604480 | tf_op jit(solution)/shard_map/all_gather | solution.py:1608
  46.2 7.5 copy-start.8
  46.2 7.5 copy-start.9
  46.9 261.7 %all-gather.8.cloned.1.call-start = ((), (), s32[]{:S(2)}) async-start(), calls=%async_computation.5 | async-start | bytes 3604480 | tf_op jit(solution)/shard_map/all_gather | solution.py:1606
  47.6 596.5 %reduce-scatter.4.cloned.1.call-start = ((), (), s32[]{:S(2)}) async-start(), calls=%async_computation.6 | async-start | bytes 10813440 | tf_op jit(solution)/shard_map/reduce_scatter | solution.py:1665
  47.7 5.9 copy-start.32
  48.6 105.2 %copy-start.2 = (s32[2048]{0:T(1024)}, s32[2048]{0:T(1024)S(1)}, u32[]{:S(2)}) copy-start(s32[2048]{0:T(1024)S(1)} %fusion.10) | copy-start | bytes 24580
  50.0 3.7 copy-start.26
  50.7 174.0 %copy-start.5 = (f32[1,8,256]{2,0,1:T(1,128)}, f32[1,8,256]{2,0,1:T(1,128)S(1)}, u32[]{:S(2)}) copy-start(f32[1,8,256]{2,0,1:T(1,128)S(1)} %get-tuple-element.97) | copy-start | bytes 24580
  52.5 101.3 %copy-start = (f32[32,2048]{1,0:T(8,128)}, f32[32,2048]{1,0:T(8,128)S(1)}, u32[]{:S(2)}) copy-start(f32[32,2048]{1,0:T(8,128)S(1)} %get-tuple-element.100.cos_ref) | copy-start | bytes 786436
  53.6 100.2 %copy-start.6 = (s32[8,3]{1,0:T(8,128)}, s32[8,3]{1,0:T(8,128)S(1)}, u32[]{:S(2)}) copy-start(s32[8,3]{1,0:T(8,128)S(1)} %pad_add_fusion.info_ref) | copy-start | bytes 292
  53.7 1.3 copy-start.10
  153.8 70.9 %copy-start.13 = (bf16[4,8,256,128]{3,2,1,0:T(8,128)(2,1)}, bf16[4,8,256,128]{3,2,1,0:T(8,128)(2,1)S(1)}, u32[]{:S(2)}) copy-start(bf16[4,8,256,128]{3,2,1,0:T(8,128)(2,1)S(1)} %get-tuple-element.52.kv_ref) | copy-start | bytes 6291460
  153.8 70.9 %copy-start.18 = (bf16[256,2048]{1,0:T(8,128)(2,1)}, bf16[256,2048]{1,0:T(8,128)(2,1)S(1)}, u32[]{:S(2)}) copy-start(bf16[256,2048]{1,0:T(8,128)(2,1)S(1)} %get-tuple-element.51.q_ref) | copy-start | bytes 3145732
  153.8 70.9 %copy-start.17 = (bf16[256,2048]{1,0:T(8,128)(2,1)}, bf16[256,2048]{1,0:T(8,128)(2,1)S(1)}, u32[]{:S(2)}) copy-start(bf16[256,2048]{1,0:T(8,128)(2,1)S(1)} %get-tuple-element.54.w_ref) | copy-start | bytes 3145732
  307.7 1.0 copy-start.15
  354.8 1.6 copy-start.11
  446.3 259.7 %reduce-scatter.6.cloned.1.call-start = ((), (), s32[]{:S(2)}) async-start(), calls=%async_computation.7 | async-start | bytes 1310720 | tf_op jit(solution)/shard_map/reduce_scatter | solution.py:1693
  446.4 2.8 copy-start.19
  446.4 2.8 copy-start.20
  446.5 2.7 copy-start.3
  446.5 2.7 copy-start.7
  446.5 2.7 copy-start.14
  446.5 2.7 copy-start.16
  520.7 1.3 copy-start.12
  638.6 2.7 copy-start.27
  638.6 2.7 copy-start.33
  639.7 2.8 copy-start.1
  640.1 2.4 copy-start.22
  644.2 98.9 %reduce-scatter.8.cloned.1.call-start = ((), (), s32[]{:S(2)}) async-start(), calls=%async_computation.8 | async-start | bytes 1638400 | tf_op jit(solution)/shard_map/reduce_scatter | solution.py:1693
  644.2 60.5 %copy-start.30 = (f32[1,2048]{1,0:T(1,128)S(1)}, f32[1,2048]{1,0:T(1,128)}, u32[]{:S(2)}) copy-start(f32[1,2048]{1,0:T(1,128)} %get-tuple-element.80) | copy-start | bytes 24580
  738.7 1.7 copy-start.31
  738.8 3.4 copy-start.25
  745.4 3.4 copy-start.21
Sparse Core Ops, SparseCore 0:
  46.3 107.5 all-gather.3
  155.4 57.9 all-gather.5
  215.0 57.7 all-gather.7
  446.4 192.9 reduce-scatter.3
  644.3 28.9 reduce-scatter.5
  706.2 29.9 reduce-scatter.7

commit v3 on v2

--- a/solution.py
+++ b/solution.py
@@ -548,57 +548,39 @@
     greet([(f ^ k, t) for k in (CORE, ALONG_X, ALONG_Y)])
 
 
-def forward_output(attended, output_rows, tokens, gain, grads, number):
+def forward_output(attended, output_rows, tokens, gain, number):
     size, width = tokens.shape
     f32, bf16 = jnp.float32, jnp.bfloat16
 
     def kernel(
-        o_ref, w_ref, x_ref, gain_ref, dy_ref,
-        middle_ref, row_ref, dys_ref,
+        o_ref, w_ref, x_ref, gain_ref,
+        middle_ref, row_ref,
         stage, other, held, from_x, from_y, last, sum_sent, sum_arrived,
-        dys, dys_sent, dys_arrived, keep_sem,
     ):
-        f = lax.axis_index("fsdp")
-        dys[f] = dy_ref[...]
         plane_greet()
-        gather_dys = PlaneGather(dys, dys_sent, dys_arrived)
         total = PlaneSum(stage, other, held, from_x, from_y, last, sum_sent, sum_arrived)
         total.begin(chunk_part([(o_ref, w_ref)], size))
-        gather_dys.begin()
         total.turn()
-        for k in range(PARTS):
-            gather_dys.advance(k)
         total.end(middle_ref)
         middle = x_ref[...].astype(f32) + middle_ref[...]
         middle_ref[...] = middle
         inverse = lax.rsqrt(jnp.mean(middle * middle, axis=1, keepdims=True) + epsilon)
         row_ref[...] = (middle * inverse * gain_ref[...]).astype(bf16)
-        gather_dys.wait_core(0, 3, 4)
-        gather_dys.far()
-        gather_dys.wait_core(5)
-        keep = pltpu.make_async_copy(dys, dys_ref, keep_sem)
-        keep.start()
-        keep.wait()
         total.finish()
-        gather_dys.finish()
 
     return pl.pallas_call(
         kernel,
         out_shape=[
             jax.ShapeDtypeStruct((size, width), f32),
             jax.ShapeDtypeStruct((size, width), bf16),
-            jax.ShapeDtypeStruct((8, size, width), bf16),
         ],
-        in_specs=[IN_VMEM] * 5,
-        out_specs=[IN_VMEM, IN_VMEM, ANYWHERE],
-        scratch_shapes=sum_scratch(size, width)
-        + [pltpu.VMEM((8, size, width), bf16)]
-        + GATHER_SEMAPHORES
-        + [pltpu.SemaphoreType.DMA],
-        compiler_params=comm_params(number, 50 << 20),
-        cost_estimate=lasting(75),
+        in_specs=[IN_VMEM] * 4,
+        out_specs=[IN_VMEM] * 2,
+        scratch_shapes=sum_scratch(size, width),
+        compiler_params=comm_params(number, 40 << 20),
+        cost_estimate=lasting(45),
         name="forward_output",
-    )(attended, output_rows, tokens, gain, grads)
+    )(attended, output_rows, tokens, gain)
 
 
 def forward_hidden(row, dys, gate_rows, up_rows, down_rows, number):
@@ -608,8 +590,8 @@
 
     def kernel(
         row_ref, dys_hbm, gate_hbm, up_hbm, down_hbm,
-        rows_ref, hidden_ref, dgate_ref, dup_ref,
-        rows, rows_sent, rows_arrived, dys, gate_w, up_w, down_w, load_sem, dh, out, out_sem, keep_sem,
+        rows_ref, hidden_ref, dgate_ref, dup_ref, down_grad_ref,
+        rows, rows_sent, rows_arrived, dys, gate_w, up_w, down_w, load_sem, dh, out, out_sem, keep_sem, down_grad,
     ):
         f = lax.axis_index("fsdp")
         loads = [
@@ -659,13 +641,16 @@
             sigmoid = jax.nn.sigmoid(gate)
             active = gate * sigmoid
             grad = dh[owner]
-            out[slot, 0] = (active * up).astype(bf16)
+            hidden = (active * up).astype(bf16)
+            out[slot, 0] = hidden
+            down_grad[...] += dot_nn(hidden, dys[owner])
             out[slot, 1] = (grad * up * sigmoid * (1.0 + gate * (1.0 - sigmoid))).astype(bf16)
             out[slot, 2] = (grad * active).astype(bf16)
             for c in out_copies(slot, owner):
                 c.start()
             return carry
 
+        down_grad[...] = jnp.zeros_like(down_grad)
         gather_rows.wait_core(0)
         lax.fori_loop(0, 2, chunk, 0)
         gather_rows.wait_core(3, 4)
@@ -676,6 +661,7 @@
         keep = pltpu.make_async_copy(rows, rows_ref, keep_sem)
         keep.start()
         lax.fori_loop(6, 8, chunk, 0)
+        down_grad_ref[...] = down_grad[...].astype(bf16)
         for i in (6, 7):
             for c in out_copies(i % 2, f ^ i):
                 c.wait()
@@ -687,9 +673,10 @@
     return pl.pallas_call(
         kernel,
         out_shape=[jax.ShapeDtypeStruct((8, size, width), bf16)]
-        + [jax.ShapeDtypeStruct((units, 8 * size), bf16)] * 3,
+        + [jax.ShapeDtypeStruct((units, 8 * size), bf16)] * 3
+        + [jax.ShapeDtypeStruct((units, width), bf16)],
         in_specs=[IN_VMEM] + [ANYWHERE] * 4,
-        out_specs=[ANYWHERE] * 4,
+        out_specs=[ANYWHERE] * 4 + [IN_VMEM],
         scratch_shapes=[store]
         + GATHER_SEMAPHORES
         + [store]
@@ -700,15 +687,16 @@
             pltpu.VMEM((2, 3, units, size), bf16),
             pltpu.SemaphoreType.DMA((2, 3)),
             pltpu.SemaphoreType.DMA,
+            pltpu.VMEM((units, width), f32),
         ],
-        compiler_params=comm_params(number, 50 << 20),
-        cost_estimate=lasting(55),
+        compiler_params=comm_params(number, 56 << 20),
+        cost_estimate=lasting(50),
         name="forward_hidden",
     )(row, dys, gate_rows, up_rows, down_rows)
 
 
 def backward_middle(
-    dgate, dup, hidden, gate_rows, up_rows, rows, dys, output_rows, attended, middle, grads, gain, number
+    dgate, dup, gate_rows, up_rows, rows, output_rows, attended, middle, grads, gain, number
 ):
     size, width = middle.shape
     units = gate_rows.shape[0]
@@ -718,12 +706,12 @@
     early = 5
 
     def kernel(
-        dgate_hbm, dup_hbm, hidden_hbm, gate_hbm, up_hbm, rows_hbm, dys_hbm,
+        dgate_hbm, dup_hbm, gate_hbm, up_hbm, rows_hbm,
         w_ref, o_ref, middle_ref, dy_ref, gain_ref,
         grad_ref, gain_grad_ref, grad_o_ref, do_ref, units_ref,
         stage, other, held, from_x, from_y, last, sum_sent, sum_arrived,
         store, store_sent, store_arrived,
-        dgate_v, dup_v, hidden_v, gate_w, up_w, load_sem,
+        dgate_v, dup_v, gate_w, up_w, load_sem,
         tall, tall_sem, out, out_sem, o_sum,
     ):
         f = lax.axis_index("fsdp")
@@ -735,39 +723,32 @@
                     (gate_hbm, gate_w),
                     (dup_hbm, dup_v),
                     (up_hbm, up_w),
-                    (hidden_hbm, hidden_v),
                 )
             )
         ]
         for load in loads:
             load.start()
 
-        def tall_loads(n, slot):
-            place = columns(n, size)
-            return [
-                pltpu.make_async_copy(
-                    source.at[:, :, place], tall.at[slot, i], tall_sem.at[slot, i]
-                )
-                for i, source in enumerate((dys_hbm, rows_hbm))
-            ]
-
-        for c in tall_loads(0, 0):
-            c.start()
+        def tall_load(n, slot):
+            return pltpu.make_async_copy(
+                rows_hbm.at[:, :, columns(n, size)], tall.at[slot], tall_sem.at[slot]
+            )
+
+        tall_load(0, 0).start()
         plane_greet()
         total = PlaneSum(stage, other, held, from_x, from_y, last, sum_sent, sum_arrived)
         gather = PlaneGather(store, store_sent, store_arrived)
-        for load in loads[:4]:
+        for load in loads:
             load.wait()
         total.begin(chunk_part([(dgate_v, gate_w), (dup_v, up_w)], size))
         total.turn()
-        loads[4].wait()
 
         def out_copies(n, slot):
             return [
                 pltpu.make_async_copy(
                     out.at[slot, i], units_ref.at[:, i, :, columns(n, size)], out_sem.at[slot, i]
                 )
-                for i in range(3)
+                for i in range(2)
             ]
 
         def block(n, carry):
@@ -775,22 +756,18 @@
 
             @pl.when(n + 1 < blocks)
             def _():
-                for c in tall_loads(n + 1, 1 - slot):
-                    c.start()
-
-            for c in tall_loads(n, slot):
-                c.wait()
+                tall_load(n + 1, 1 - slot).start()
+
+            tall_load(n, slot).wait()
 
             @pl.when(n >= 2)
             def _():
                 for c in out_copies(n, slot):
                     c.wait()
 
-            dy_cols = tall[slot, 0].reshape(8 * size, size)
-            row_cols = tall[slot, 1].reshape(8 * size, size)
-            out[slot, 0] = dot_nn(hidden_v[...], dy_cols).astype(bf16).reshape(4, units // 4, size)
-            out[slot, 1] = dot_nn(dgate_v[...], row_cols).astype(bf16).reshape(4, units // 4, size)
-            out[slot, 2] = dot_nn(dup_v[...], row_cols).astype(bf16).reshape(4, units // 4, size)
+            row_cols = tall[slot].reshape(8 * size, size)
+            for i, left in enumerate((dgate_v, dup_v)):
+                out[slot, i] = dot_nn(left[...], row_cols).astype(bf16).reshape(4, units // 4, size)
             for c in out_copies(n, slot):
                 c.start()
             return carry
@@ -845,25 +822,89 @@
             jax.ShapeDtypeStruct((depth, width), bf16),
             jax.ShapeDtypeStruct((depth, 8 * size), bf16),
         ]
-        + [jax.ShapeDtypeStruct((4, 3, units // 4, width), bf16)],
-        in_specs=[ANYWHERE] * 7 + [IN_VMEM] * 5,
+        + [jax.ShapeDtypeStruct((4, 2, units // 4, width), bf16)],
+        in_specs=[ANYWHERE] * 5 + [IN_VMEM] * 5,
         out_specs=[IN_VMEM] * 4 + [ANYWHERE],
         scratch_shapes=sum_scratch(size, width)
         + [pltpu.VMEM((8, size, width), bf16)]
         + GATHER_SEMAPHORES
-        + [weights] * 5
+        + [weights] * 4
         + [
-            pltpu.SemaphoreType.DMA((5,)),
-            pltpu.VMEM((2, 2, 8, size, size), bf16),
+            pltpu.SemaphoreType.DMA((4,)),
+            pltpu.VMEM((2, 8, size, size), bf16),
+            pltpu.SemaphoreType.DMA((2,)),
+            pltpu.VMEM((2, 2, 4, units // 4, size), bf16),
             pltpu.SemaphoreType.DMA((2, 2)),
-            pltpu.VMEM((2, 3, 4, units // 4, size), bf16),
-            pltpu.SemaphoreType.DMA((2, 3)),
             pltpu.VMEM((depth, width), f32),
         ],
         compiler_params=comm_params(number, VMEM_MOST),
         cost_estimate=lasting(92),
         name="backward_middle",
-    )(dgate, dup, hidden, gate_rows, up_rows, rows, dys, output_rows, attended, middle, grads, gain)
+    )(dgate, dup, gate_rows, up_rows, rows, output_rows, attended, middle, grads, gain)
+
+
+class LineGather:
+    def __init__(self, own, store, sent, arrived):
+        self.f, self.t = lax.axis_index("fsdp"), lax.axis_index("tp")
+        self.own, self.store, self.sent, self.arrived = own, store, sent, arrived
+
+    def copy(self, way, hop):
+        step = 1 if way == 0 else -1
+        place = self.store.at[self.t - step * (hop - 1)]
+        source = self.own if hop == 1 else place
+        return remote(
+            source, place, self.sent.at[way, hop], self.arrived.at[way, hop], (self.f, self.t + step)
+        )
+
+    def goes(self, way, hop):
+        if way == 0:
+            return (self.t < 3) & (self.t >= hop - 1)
+        return (self.t > 0) & (self.t <= 4 - hop)
+
+    def came(self, way, hop):
+        return self.t >= hop if way == 0 else self.t <= 3 - hop
+
+    def send(self, hop):
+        for way in (0, 1):
+            pl.when(self.goes(way, hop))(lambda way=way: self.copy(way, hop).start())
+
+    def begin(self):
+        self.send(1)
+
+    def take(self, hop):
+        for way in (0, 1):
+
+            @pl.when(self.came(way, hop))
+            def _(way=way):
+                spot = self.store.at[self.t - hop if way == 0 else self.t + hop]
+                remote(
+                    spot, spot, self.sent.at[way, hop], self.arrived.at[way, hop], (self.f, self.t)
+                ).wait_recv()
+
+        if hop < 3:
+            self.send(hop + 1)
+
+    def finish(self):
+        for hop in (1, 2, 3):
+            for way in (0, 1):
+                pl.when(self.goes(way, hop))(lambda way=way, hop=hop: self.copy(way, hop).wait_send())
+
+
+LINE_SEMAPHORES = [pltpu.SemaphoreType.DMA((2, 4)), pltpu.SemaphoreType.DMA((2, 4))]
+
+
+def line_greet(f, t):
+    barrier = pltpu.get_barrier_semaphore()
+    for k in range(1, 8):
+        pl.semaphore_signal(barrier, inc=1, device_id=(f ^ k, t), device_id_type=MESH)
+    for there, step in ((t < 3, 1), (t > 0, -1)):
+
+        @pl.when(there)
+        def _(step=step):
+            pl.semaphore_signal(barrier, inc=1, device_id=(f, t + step), device_id_type=MESH)
+
+    ends = (t == 0).astype(jnp.int32) + (t == 3).astype(jnp.int32)
+    pl.semaphore_wait(barrier, 9 - ends)
 
 
 def everyone(f, t):
@@ -888,12 +929,10 @@
         for c in kept:
             c.start()
         gains_all[f] = gains_ref[...]
-        greet(everyone(f, t))
+        line_greet(f, t)
+        line = LineGather(inner_ref, inner_all, z_sent, z_arrived)
+        line.begin()
         copies = []
-        for k in (2, 1, 3):
-            copies.append(
-                remote(inner_ref, inner_all.at[t], z_sent.at[k], z_arrived.at[k], (f, lax.rem(t + k, 4)))
-            )
         for k in far_first:
             copies.append(
                 remote(gains_ref, gains_all.at[f], sent.at[k, count], arrived.at[k, count], (f ^ k, t))
@@ -905,8 +944,11 @@
                 )
         for c in copies:
             c.start()
+        for hop in (1, 2, 3):
+            line.take(hop)
         for c in kept + copies:
             c.wait()
+        line.finish()
 
     return pl.pallas_call(
         kernel,
@@ -920,8 +962,7 @@
         scratch_shapes=[
             pltpu.SemaphoreType.DMA((8, count + 1)),
             pltpu.SemaphoreType.DMA((8, count + 1)),
-            pltpu.SemaphoreType.DMA((4,)),
-            pltpu.SemaphoreType.DMA((4,)),
+            *LINE_SEMAPHORES,
             pltpu.SemaphoreType.DMA((count + 1,)),
         ],
         compiler_params=comm_params(number),
@@ -941,7 +982,7 @@
     return jnp.concatenate(turned, axis=0)
 
 
-def first_rows(tokens, gains, inner_all, output_own, cosine, sine_table, number):
+def first_rows(tokens, gains, inner_all, output_own, cosine, sine_table, grads, number):
     size, width = tokens.shape
     block = width // 8
     quarter_rows = output_own.shape[0]
@@ -950,10 +991,11 @@
     f32, bf16 = jnp.float32, jnp.bfloat16
 
     def kernel(
-        x_ref, gains_ref, inner_ref, own_ref, cos_ref, sin_ref,
-        rows_ref, q_ref, pair_ref, w_ref, wo_ref, wo_all,
-        rows, rows_sent, rows_arrived, pair_v,
-        w_sent, w_arrived, o_sent, o_arrived, z_sent, z_arrived, p_sent, p_arrived, on_sent, on_arrived, kept_sem,
+        x_ref, gains_ref, inner_ref, own_ref, cos_ref, sin_ref, dy_ref,
+        rows_ref, q_ref, pair_ref, w_ref, wo_ref, wo_all, dys_ref,
+        rows, rows_sent, rows_arrived, dys, dys_sent, dys_arrived, pair_v,
+        w_sent, w_arrived, o_sent, o_arrived, z_sent, z_arrived,
+        p_sent, p_arrived, on_sent, on_arrived, kept_sem,
     ):
         f, t = lax.axis_index("fsdp"), lax.axis_index("tp")
         place = columns(f, block)
@@ -986,12 +1028,9 @@
         for c in kept:
             c.start()
         greet(everyone(f, t))
-        copies, along_z = [], []
-        for k in (2, 1, 3):
-            c = remote(own_ref, wo_all.at[t], z_sent.at[k], z_arrived.at[k], (f, lax.rem(t + k, 4)))
-            c.start()
-            along_z.append(c)
-        weights = []
+        line_output = LineGather(own_ref, wo_all, z_sent, z_arrived)
+        line_output.begin()
+        copies, weights = [], []
         for k in far_first:
             for i, (s, o) in enumerate(inner_slices(f ^ k)):
                 c = remote(s, o, w_sent.at[k, i], w_arrived.at[k, i], (f ^ k, t))
@@ -1003,12 +1042,16 @@
         rows[f] = (wide * inverse * gain).astype(bf16)
         gather = PlaneGather(rows, rows_sent, rows_arrived)
         gather.begin()
+        dys[f] = dy_ref[...]
         for k in range(PARTS):
             gather.advance(k)
+        gather_dys = PlaneGather(dys, dys_sent, dys_arrived)
+        gather_dys.begin()
         for c in kept[:2]:
             c.wait()
         for c in weights:
             c.wait_recv()
+        line_output.take(1)
 
         def chunk(i, carry):
             owner = f ^ i
@@ -1043,6 +1086,7 @@
         lax.fori_loop(2, 6, chunk, 0)
         spread_pair(2)
         spread_pair(4)
+        line_output.take(2)
         gather.far()
         gather.wait_core(5)
         lax.fori_loop(6, 8, chunk, 0)
@@ -1052,8 +1096,7 @@
         keep_rows = pltpu.make_async_copy(rows, rows_ref, kept_sem.at[4])
         keep_rows.start()
         kept[2].wait()
-        for c in along_z:
-            c.wait_recv()
+        line_output.take(3)
         for k in far_first:
             s, o = output_slice(f ^ k)
             c = remote(s, o, o_sent.at[k], o_arrived.at[k], (f ^ k, t))
@@ -1062,6 +1105,8 @@
         s, o = output_slice(f)
         keep_output = pltpu.make_async_copy(s, o, kept_sem.at[5])
         keep_output.start()
+        for k in range(PARTS):
+            gather_dys.advance(k)
         passed = []
         for i, k, c in spread:
             c.wait_recv()
@@ -1069,14 +1114,22 @@
             d = remote(spot, spot, on_sent.at[i // 2, k], on_arrived.at[i // 2, k], (f ^ CORE, t))
             d.start()
             passed.append(d)
+        gather_dys.wait_core(0, 3, 4)
+        gather_dys.far()
+        gather_dys.wait_core(5)
+        keep_dys = pltpu.make_async_copy(dys, dys_ref, kept_sem.at[6])
+        keep_dys.start()
         for c in passed + copies:
             c.wait()
-        for c in weights + along_z + [c for _, _, c in spread]:
+        for c in weights + [c for _, _, c in spread]:
             c.wait_send()
+        line_output.finish()
         gather.finish()
+        gather_dys.finish()
         own_pair.wait()
         keep_rows.wait()
         keep_output.wait()
+        keep_dys.wait()
 
     dma = pltpu.SemaphoreType.DMA
     return pl.pallas_call(
@@ -1088,10 +1141,13 @@
             jax.ShapeDtypeStruct((depth + pair_rows, width), bf16),
             jax.ShapeDtypeStruct((depth, width), bf16),
             jax.ShapeDtypeStruct((4, quarter_rows, block), bf16),
+            jax.ShapeDtypeStruct((8, size, width), bf16),
         ],
-        in_specs=[IN_VMEM, IN_VMEM, ANYWHERE, ANYWHERE, IN_VMEM, IN_VMEM],
-        out_specs=[ANYWHERE, IN_VMEM, ANYWHERE, IN_VMEM, ANYWHERE, ANYWHERE],
+        in_specs=[IN_VMEM, IN_VMEM, ANYWHERE, ANYWHERE, IN_VMEM, IN_VMEM, IN_VMEM],
+        out_specs=[ANYWHERE, IN_VMEM, ANYWHERE, IN_VMEM, ANYWHERE, ANYWHERE, ANYWHERE],
         scratch_shapes=[pltpu.VMEM((8, size, width), bf16)]
+        + GATHER_SEMAPHORES
+        + [pltpu.VMEM((8, size, width), bf16)]
         + GATHER_SEMAPHORES
         + [
             pltpu.VMEM((8, size, pair_rows), bf16),
@@ -1099,18 +1155,17 @@
             dma((8, 2)),
             dma((8,)),
             dma((8,)),
-            dma((4,)),
-            dma((4,)),
+            *LINE_SEMAPHORES,
             dma((4, 4)),
             dma((4, 4)),
             dma((4, 4)),
             dma((4, 4)),
-            dma((6,)),
+            dma((7,)),
         ],
         compiler_params=comm_params(number, 40 << 20),
-        cost_estimate=lasting(85),
+        cost_estimate=lasting(100),
         name="first_rows",
-    )(tokens, gains, inner_all, output_own, cosine, sine_table)[:5]
+    )(tokens, gains, inner_all, output_own, cosine, sine_table, grads)
 
 
 def backward_pairs(pair_parts, hidden, down_rows, middle, valid, grad_output, number):
@@ -1281,18 +1336,24 @@
     )(grad_inner, weights, rows, tokens, grad_middle, gain)
 
 
-def last_exchange(hidden_grads, gain_parts, number):
-    count, units, width = hidden_grads.shape
+def last_exchange(down_grads, hidden_grads, gain_parts, number):
+    _, units, width = hidden_grads.shape
+    arrays = (down_grads, hidden_grads)
     block = width // 8
     f32, bf16 = jnp.float32, jnp.bfloat16
     far_first = (6, 7, 2, 4, 3, 5, 1)
 
     def kernel(
-        source, gains_ref, target, sums_ref, taken, planes, sent, arrived, z_sent, z_arrived, kept_sem
+        source_0, source_1, gains_ref, target_0, target_1, sums_ref, taken, planes, sent, arrived, z_sent, z_arrived, kept_sem
     ):
         f, t = lax.axis_index("fsdp"), lax.axis_index("tp")
-        keep = pltpu.make_async_copy(source.at[:, :, columns(f, block)], target.at[f], kept_sem)
-        keep.start()
+        ways = ((source_0, target_0), (source_1, target_1))
+        kept = [
+            pltpu.make_async_copy(s.at[:, :, columns(f, block)], o.at[f], kept_sem.at[i])
+            for i, (s, o) in enumerate(ways)
+        ]
+        for c in kept:
+            c.start()
         greet(everyone(f, t))
         gains = []
         for k in far_first:
@@ -1302,16 +1363,17 @@
             c.start()
             gains.append(c)
         copies = []
-        for k in far_first:
-            c = remote(
-                source.at[:, :, columns(f ^ k, block)],
-                target.at[f],
-                sent.at[k, 1],
-                arrived.at[k, 1],
-                (f ^ k, t),
-            )
-            c.start()
-            copies.append(c)
+        for i, (s, o) in enumerate(ways):
+            for k in far_first:
+                c = remote(
+                    s.at[:, :, columns(f ^ k, block)],
+                    o.at[f],
+                    sent.at[k, 1 + i],
+                    arrived.at[k, 1 + i],
+                    (f ^ k, t),
+                )
+                c.start()
+                copies.append(c)
         total = gains_ref[f]
         for k, c in zip(far_first, gains):
             c.wait_recv()
@@ -1328,7 +1390,7 @@
         for plane in (1, 2, 3):
             sums += planes[lax.rem(t + 4 - plane, 4)]
         sums_ref[...] = sums
-        for c in [keep] + copies:
+        for c in kept + copies:
             c.wait()
         for c in gains + along_z:
             c.wait_send()
@@ -1337,24 +1399,24 @@
     return pl.pallas_call(
         kernel,
         out_shape=[
-            jax.ShapeDtypeStruct((8, count, units, block), bf16),
+            *(jax.ShapeDtypeStruct((8, len(x), units, block), bf16) for x in arrays),
             jax.ShapeDtypeStruct(gain_parts.shape[1:], f32),
         ],
-        in_specs=[ANYWHERE, IN_VMEM],
-        out_specs=[ANYWHERE, IN_VMEM],
+        in_specs=[ANYWHERE, ANYWHERE, IN_VMEM],
+        out_specs=[ANYWHERE, ANYWHERE, IN_VMEM],
         scratch_shapes=[
             pltpu.VMEM(gain_parts.shape, f32),
             pltpu.VMEM((4, *gain_parts.shape[1:]), f32),
-            dma((8, 2)),
-            dma((8, 2)),
+            dma((8, 3)),
+            dma((8, 3)),
             dma((4,)),
             dma((4,)),
-            dma,
+            dma((2,)),
         ],
         compiler_params=comm_params(number),
         cost_estimate=lasting(28),
         name="last_exchange",
-    )(hidden_grads, gain_parts)
+    )(down_grads, hidden_grads, gain_parts)
 
 
 def dot_nn(left, right):
@@ -1369,6 +1431,13 @@
 
 def head_lanes(block, heads):
     return jnp.concatenate([block[h * HEAD_DIM : (h + 1) * HEAD_DIM] for h in range(heads)], axis=1)
+
+
+WIDE = 2
+
+def key_block(kv_ref, g, count):
+    blocks = [kv_ref[lax.rem(g + n, 4), lax.div(g + n, 4)] for n in range(count)]
+    return blocks[0] if count == 1 else jnp.concatenate(blocks, axis=0)
 
 
 def attend(info, begins, queries, pair):
@@ -1380,50 +1449,49 @@
     def kernel(info_ref, begin_ref, q_ref, kv_ref, o_ref, l_ref, q_s, m_s, t_s, a_s):
         f = pl.program_id(0)
         low, middle, own = info_ref[f, 0], info_ref[f, 1], info_ref[f, 2]
+        middle = middle + lax.rem(own - middle, WIDE)
         q_s[...] = head_lanes(q_ref[...], heads)
         m_s[...] = jnp.full_like(m_s, -1e30)
         t_s[...] = jnp.zeros_like(t_s)
         a_s[...] = jnp.zeros_like(a_s)
 
-        def step(g, masked):
-            block = kv_ref[lax.rem(g, 4), lax.div(g, 4)]
+        def step(g, count, masked):
+            block = key_block(kv_ref, g, count)
             keys, values = block[:, :HEAD_DIM], block[:, HEAD_DIM:]
             value_cols = values.astype(jnp.float32).T.astype(jnp.bfloat16)
             if masked:
                 seen = seen_keys(begin_ref[0], g * size, own * size, (size, size))
-            for h in range(heads):
-                lanes = pl.ds(h * size, size)
-                scores = dot_nn(keys, q_s[:, lanes])
-                if masked:
-                    scores = jnp.where(seen, scores, -1e30)
-                largest = m_s[:, lanes]
-                higher = jnp.maximum(largest, jnp.max(scores, axis=0, keepdims=True))
-                raised = jnp.exp(scores - higher)
-                fade = jnp.exp(largest - higher)
-                m_s[:, lanes] = higher
-                t_s[:, lanes] = t_s[:, lanes] * fade + jnp.sum(raised, axis=0, keepdims=True)
-                a_s[:, lanes] = a_s[:, lanes] * fade + dot_nn(
-                    value_cols, raised.astype(jnp.bfloat16)
-                )
+                seen = jnp.concatenate([seen] * heads, axis=1)
+            scores = dot_nn(keys, q_s[...])
+            if masked:
+                scores = jnp.where(seen, scores, -1e30)
+            largest = m_s[...]
+            higher = jnp.maximum(largest, jnp.max(scores, axis=0, keepdims=True))
+            raised = jnp.exp(scores - higher)
+            fade = jnp.exp(largest - higher)
+            m_s[...] = higher
+            t_s[...] = t_s[...] * fade + jnp.sum(raised, axis=0, keepdims=True)
+            a_s[...] = a_s[...] * fade + dot_nn(
+                value_cols, raised.astype(jnp.bfloat16)
+            )
 
         def masked_step(g, carry):
-            step(g, True)
+            step(g, 1, True)
             return carry
 
-        def plain_step(g, carry):
-            step(g, False)
+        def plain_step(n, carry):
+            step(middle + n * WIDE, WIDE, False)
             return carry
 
-        step(own, True)
+        step(own, 1, True)
         lax.fori_loop(low, middle, masked_step, 0)
-        lax.fori_loop(middle, own, plain_step, 0)
+        lax.fori_loop(0, lax.div(own - middle, WIDE), plain_step, 0)
         result = a_s[...] / t_s[...]
         for h in range(heads):
             o_ref[h * HEAD_DIM : (h + 1) * HEAD_DIM] = result[:, h * size : (h + 1) * size].astype(
                 jnp.bfloat16
             )
         l_ref[0] = m_s[...] + jnp.log(t_s[...])
-
     return pl.pallas_call(
         kernel,
         grid_spec=pltpu.PrefetchScalarGridSpec(
@@ -1450,7 +1518,7 @@
             jax.ShapeDtypeStruct((8, 1, span), jnp.float32),
         ],
         compiler_params=pltpu.CompilerParams(vmem_limit_bytes=40 << 20),
-        cost_estimate=lasting(75),
+        cost_estimate=lasting(50),
         name="attend",
     )(info, begins, queries, pair)
 
@@ -1466,6 +1534,7 @@
     ):
         f = pl.program_id(0)
         low, middle, own = info_ref[f, 0], info_ref[f, 1], info_ref[f, 2]
+        middle = middle + lax.rem(own - middle, WIDE)
 
         @pl.when(f == 0)
         def _():
@@ -1477,39 +1546,40 @@
         d_s[...] = jnp.sum(out_lanes * g_s[...].astype(jnp.float32), axis=0, keepdims=True)
         a_s[...] = jnp.zeros_like(a_s)
 
-        def step(g, masked):
-            block = kv_ref[lax.rem(g, 4), lax.div(g, 4)]
+        def step(g, count, masked):
+            block = key_block(kv_ref, g, count)
             keys, values = block[:, :HEAD_DIM], block[:, HEAD_DIM:]
             key_cols = keys.astype(jnp.float32).T.astype(jnp.bfloat16)
             if masked:
                 seen = seen_keys(begin_ref[0], g * size, own * size, (size, size))
-            grad_keys = jnp.zeros((HEAD_DIM, size), jnp.float32)
-            grad_values = jnp.zeros((HEAD_DIM, size), jnp.float32)
-            for h in range(heads):
-                lanes = pl.ds(h * size, size)
-                query, grad = q_s[:, lanes], g_s[:, lanes]
-                raised = jnp.exp(dot_nn(keys, query) - l_ref[0, :, lanes])
-                if masked:
-                    raised = jnp.where(seen, raised, 0.0)
-                grad_probs = dot_nn(values, grad)
-                scores = (raised * (grad_probs - d_s[:, lanes])).astype(jnp.bfloat16)
-                grad_values += outer_cols(grad, raised.astype(jnp.bfloat16))
-                grad_keys += outer_cols(query, scores)
-                a_s[:, lanes] += dot_nn(key_cols, scores)
-            w_s[lax.rem(g, 4), lax.div(g, 4), :HEAD_DIM] += grad_keys
-            w_s[lax.rem(g, 4), lax.div(g, 4), HEAD_DIM:] += grad_values
+                seen = jnp.concatenate([seen] * heads, axis=1)
+            grad_keys = jnp.zeros((HEAD_DIM, count * size), jnp.float32)
+            grad_values = jnp.zeros((HEAD_DIM, count * size), jnp.float32)
+            query, grad = q_s[...], g_s[...]
+            raised = jnp.exp(dot_nn(keys, query) - l_ref[0])
+            if masked:
+                raised = jnp.where(seen, raised, 0.0)
+            grad_probs = dot_nn(values, grad)
+            scores = (raised * (grad_probs - d_s[...])).astype(jnp.bfloat16)
+            grad_values += outer_cols(grad, raised.astype(jnp.bfloat16))
+            grad_keys += outer_cols(query, scores)
+            a_s[...] += dot_nn(key_cols, scores)
+            for n in range(count):
+                keep = slice(n * size, (n + 1) * size)
+                w_s[lax.rem(g + n, 4), lax.div(g + n, 4), :HEAD_DIM] += grad_keys[:, keep]
+                w_s[lax.rem(g + n, 4), lax.div(g + n, 4), HEAD_DIM:] += grad_values[:, keep]
 
         def masked_step(g, carry):
-            step(g, True)
+            step(g, 1, True)
             return carry
 
-        def plain_step(g, carry):
-            step(g, False)
+        def plain_step(n, carry):
+            step(middle + n * WIDE, WIDE, False)
             return carry
 
-        step(own, True)
+        step(own, 1, True)
         lax.fori_loop(low, middle, masked_step, 0)
-        lax.fori_loop(middle, own, plain_step, 0)
+        lax.fori_loop(0, lax.div(own - middle, WIDE), plain_step, 0)
         result = a_s[...] * HEAD_DIM ** (-0.5)
         for h in range(heads):
             dq_ref[h * HEAD_DIM : (h + 1) * HEAD_DIM] = result[:, h * size : (h + 1) * size]
@@ -1548,7 +1618,7 @@
             jax.ShapeDtypeStruct((4, 8, 2 * HEAD_DIM, size), jnp.bfloat16),
         ],
         compiler_params=pltpu.CompilerParams(vmem_limit_bytes=40 << 20),
-        cost_estimate=lasting(80),
+        cost_estimate=lasting(65),
         name="attend_back",
     )(info, begins, queries, pair, outputs, grads, totals)
 
@@ -1630,15 +1700,13 @@
     angles = positions.astype(f32)[None, :] * frequency[:, None]
     cosine, sine_table = jnp.cos(angles), jnp.sin(angles)
 
-    rows_first, queries, pair, inner_rows_w, output_rows = first_rows(
-        tokens, gains_all, inner_all, output_weight, cosine, sine_table, 2
+    grad_rows_own = jnp.where(valid_rows, out_grad, jnp.zeros_like(out_grad))
+    rows_first, queries, pair, inner_rows_w, output_rows, _, grad_rows = first_rows(
+        tokens, gains_all, inner_all, output_weight, cosine, sine_table, grad_rows_own, 2
     )
     attended, totals = attend(info, begins, queries, pair)
-    grad_rows_own = jnp.where(valid_rows, out_grad, jnp.zeros_like(out_grad))
-    middle, row_second, grad_rows = forward_output(
-        attended, output_rows, tokens, gain_second, grad_rows_own, 4
-    )
-    rows_second, hidden, grad_gate_low, grad_up_low = forward_hidden(
+    middle, row_second = forward_output(attended, output_rows, tokens, gain_second, 4)
+    rows_second, hidden, grad_gate_low, grad_up_low, down_grads = forward_hidden(
         row_second, grad_rows, gate_rows, up_rows, down_rows, 5
     )
     (
@@ -1650,11 +1718,9 @@
     ) = backward_middle(
         grad_gate_low,
         grad_up_low,
-        hidden,
         gate_rows,
         up_rows,
         rows_second,
-        grad_rows,
         output_rows,
         attended,
         middle,
@@ -1662,8 +1728,10 @@
         gain_second,
         6,
     )
+    down_grads = lax.psum_scatter(down_grads, "tp", scatter_dimension=0, tiled=True)
+    hidden_grads, down_grads = lax.optimization_barrier((hidden_grads, down_grads))
     hidden_grads = lax.psum_scatter(
-        hidden_grads.reshape(12 * units, width), "tp", scatter_dimension=0, tiled=True
+        hidden_grads.reshape(8 * units, width), "tp", scatter_dimension=0, tiled=True
     )
     grad_queries, grad_pair_parts = attend_back(
         info, begins, queries, pair, attended, grad_attended, totals
@@ -1698,8 +1766,10 @@
     inner_grads = along_z(inner_parts)
     gain_parts = jnp.concatenate([gain_first_part, gain_second_part], axis=0)
     gain_parts = jnp.moveaxis(gain_parts.reshape(2, 8, block), 1, 0)
-    hidden_own, gain_sums = last_exchange(hidden_grads.reshape(3, units, width), gain_parts, 9)
-    own_down, own_gate, own_up = (hidden_own[:, n].reshape(8 * units, block) for n in range(3))
+    own_down, hidden_own, gain_sums = last_exchange(
+        down_grads.reshape(1, units, width), hidden_grads.reshape(2, units, width), gain_parts, 9
+    )
+    own_gate, own_up = (hidden_own[:, n].reshape(8 * units, block) for n in range(2))
     return (
         layer_out,
         tokens_grad,
@@ -1711,7 +1781,7 @@
         gain_sums[1],
         own_gate.T.astype(f32),
         own_up.T.astype(f32),
-        own_down.astype(f32),
+        own_down.reshape(8 * units, block).astype(f32),
     )
 
 

time: 766 us -> 665 us (0.87)
  Pallas kernels: 698 us -> 591 us
    pallas_call x1, Pallas kernels: 82.9 us -> 42.9 us  [forward_output(): pl.pallas_call(kernel, out_shape=[jax.ShapeDtypeStruct((size, width), f32...]
    pallas_call x1, Pallas kernels: 70.9 us -> 31.9 us  [attend(): pl.pallas_call(kernel, grid_spec=pltpu.PrefetchScalarGridSpec(num_scalar_...]
    pallas_call x1, Pallas kernels: 71.5 us -> 45.3 us  [attend_back(): pl.pallas_call(kernel, grid_spec=pltpu.PrefetchScalarGridSpec(num_scalar_...]
    pallas_call x1, Pallas kernels: 117 us -> 96 us  [backward_pairs(): pl.pallas_call(kernel, out_shape=[jax.ShapeDtypeStruct((chunks, height, s...]
    pallas_call x1, Pallas kernels: 98.8 us -> 110 us  [first_rows(): pl.pallas_call(kernel, out_shape=[jax.ShapeDtypeStruct((8, size, width),...]
  transfers between devices with their start and end apart: 6 -> 7, of which waited for: 0 -> 0; matrix products, arithmetic and copies ran while one was open for 3% -> 4% of each run, Pallas kernels for 70% -> 77%
where the time goes in v3:
time: 665 us; the launch traced here: 655 us
  Pallas kernels  591 us (89%)
  local copies, waits for them, and re-layouts  29.8 us (4%)
  other arithmetic  17 us (3%)
  between operations  15.2 us (2%)
    pallas_call x1, Pallas kernels, first_rows(): pl.pallas_call(kernel, out_shape=[jax.ShapeDtypeStruct((8, size, width),...  110 us
    pallas_call x1, Pallas kernels, backward_pairs(): pl.pallas_call(kernel, out_shape=[jax.ShapeDtypeStruct((chunks, height, s...  96 us
    pallas_call x1, Pallas kernels, backward_middle(): pl.pallas_call(kernel, out_shape=[jax.ShapeDtypeStruct((size, width), f32...  90.2 us
    pallas_call x1, Pallas kernels, backward_first(): pl.pallas_call(kernel, out_shape=[jax.ShapeDtypeStruct((size, width), f32...  60.6 us
    pallas_call x1, Pallas kernels, forward_hidden(): pl.pallas_call(kernel, out_shape=[jax.ShapeDtypeStruct((8, size, width),...  51.8 us
    pallas_call x1, Pallas kernels, attend_back(): pl.pallas_call(kernel, grid_spec=pltpu.PrefetchScalarGridSpec(num_scalar_...  45.3 us
    pallas_call x1, Pallas kernels, forward_output(): pl.pallas_call(kernel, out_shape=[jax.ShapeDtypeStruct((size, width), f32...  42.9 us
    pallas_call x1, Pallas kernels, first_exchange(): pl.pallas_call(kernel, out_shape=[jax.ShapeDtypeStruct((units, 8 * block)...  34.2 us
  transfers between devices with their start and end apart: 7, of which 0 were waited for; matrix products, arithmetic and copies ran while one was open for 4% of the time, Pallas kernels for 77%

profile of v3, /device:TPU:0, one launch (start us, length us, event | category | flops | bytes accessed | tf_op | source)
XLA Modules:
  0.0 655.0 jit_solution(11688797052449596474)
XLA Ops:
  7.3 0.7 stack.27
  8.0 0.7 stack.28
  8.6 1.1 copy.80
  9.7 2.2 copy.78
  12.0 1.1 copy.79
  13.7 0.7 pad_maximum_fusion.4.refs_3_
  14.4 34.2 %first_exchange.1 = (bf16[176,2048]{1,0:T(8,128)(2,1)}, bf16[176,2048]{1,0:T(8,128)(2,1)}, bf16[176,2048]{1,0:T(8,128)(2,1)}, bf16[4,640,256]{2,1,0:T(8,128)(2,1)}, f32[8,2,256]{2,1,0:T(2,128)}) custom-call(bf16[8,176,256]{2,1,0:T(8,128)(2,1)} %bitcast.108, bf16[8,176,256]{2,1,0:T(8,128)(2,1)} %bitcast.89, bf16[8,176,256]{2,1,0:T(8,128)(2,1)} %bitcast.90, ...), custom_call_target="tpu_custom_call" | custom-call | flops 35200000000 | bytes 1000000 | tf_op jit(solution)/shard_map/first_exchange/pallas_call | solution.py:953
  48.7 0.7 all-gather.6.cloned.1.call-update
  49.5 0.7 all-gather.8.cloned.1.call-update
  50.4 0.6 slice.76
  51.0 0.7 add_compare_fusion.1
  51.6 1.3 fusion.8.valid_ref
  53.1 0.7 select_convert_fusion
  53.9 0.6 fusion.18
  54.6 1.7 fusion.9
  56.3 1.5 broadcast_select_fusion.dy_ref
  57.8 110.3 %first_rows.1 = (bf16[8,256,2048]{2,1,0:T(8,128)(2,1)}, bf16[256,2048]{1,0:T(8,128)(2,1)S(1)}, bf16[4,8,256,128]{3,2,1,0:T(8,128)(2,1)S(1)}, bf16[384,2048]{1,0:...) custom-call(bf16[256,2048]{1,0:T(8,128)(2,1)S(1)} %copy-done.9, ...), custom_call_target="tpu_custom_call" | custom-call | flops 109999996928 | bytes 1000000 | tf_op jit(solution)/shard_map/first_rows/pallas_call | solution.py:1135
  168.3 1.4 pad_maximum_fusion.1.w_ref
  170.2 31.9 %attend.1 = (bf16[256,2048]{1,0:T(8,128)(2,1)S(1)}, f32[8,1,1024]{2,1,0:T(1,128)S(1)}) custom-call(s32[8,3]{1,0:T(8,128)S(1)} %pad_add_fusion.info_ref, s32[8,1,256]{2,1,0:T(1,128)S(1)} %bitcast.74, bf16[256,2048]{1,0:T(8,128)(2,1)S(1)} %get-tuple-element.55.q_ref, bf16[4,8,256,128]{3,2,1,0:T(8,128)(2,1)S(1)} %get-tuple-element.56.kv_ref), custom_call_target="tpu_custom_call" | custom-call | flops 54999998464 | bytes 1000000 | tf_op jit(solution)/shard_map/attend/pallas_call | solution.py:1495
  202.1 42.9 %forward_output.1 = (f32[256,2048]{1,0:T(8,128)S(1)}, bf16[256,2048]{1,0:T(8,128)(2,1)S(1)}) custom-call(bf16[256,2048]{1,0:T(8,128)(2,1)S(1)} %get-tuple-element.57.o_ref, bf16[256,2048]{1,0:T(8,128)(2,1)S(1)} %get-tuple-element.58.w_ref, bf16[256,2048]{1,0:T(8,128)(2,1)S(1)} %copy-done.9, f32[1,2048]{1,0:T(1,128)S(1)} %bitcast.77), custom_call_target="tpu_custom_call" | custom-call | flops 49500000256 | bytes 1000000 | tf_op jit(solution)/shard_map/forward_output/pallas_call | solution.py:571
  245.0 1.3 copy-done.12
  246.3 1.0 copy-done.19
  247.3 51.8 %forward_hidden.1 = (bf16[8,256,2048]{2,1,0:T(8,128)(2,1)}, bf16[704,2048]{1,0:T(8,128)(2,1)}, bf16[704,2048]{1,0:T(8,128)(2,1)}, bf16[704,2048]{1,0:T(8,128)(2,1)}, bf16[704,2048]{1,0:T(8,128)(2,1)}) custom-call(bf16[256,2048]{1,0:T(8,128)(2,1)} %copy-done.19, bf16[8,256,2048]{2,1,0:T(8,128)(2,1)} %get-tuple-element.60.dys_hbm, ...), custom_call_target="tpu_custom_call" | custom-call | flops 54999998464 | bytes 1000000 | tf_op jit(solution)/shard_map/forward_hidden/pallas_call | solution.py:673
  299.1 90.2 %backward_middle.1 = (f32[256,2048]{1,0:T(8,128)}, f32[1,2048]{1,0:T(1,128)}, bf16[256,2048]{1,0:T(8,128)(2,1)}, bf16[256,2048]{1,0:T(8,128)(2,1)}, bf16[4,2,176,2048]{3,2,1,0:T(8,128)(2,1)}) custom-call(bf16[704,2048]{1,0:T(8,128)(2,1)} %get-tuple-element.64.dgate_hbm, bf16[704,2048]{1,0:T(8,128)(2,1)} %get-tuple-element.65.dup_hbm, ...), custom_call_target="tpu_custom_call" | custom-call | flops 101200003072 | bytes 1000000 | tf_op jit(solution)/shard_map/backward_middle/pallas_call | solution.py:817
  389.5 0.6 copy-done.4
  390.6 1.6 copy-done.15
  392.2 1.2 copy-done.21
  393.4 1.2 copy-done.22
  394.7 45.3 %attend_back.1 = (f32[256,2048]{1,0:T(8,128)S(1)}, bf16[4,8,128,256]{3,2,1,0:T(8,128)(2,1)S(1)}) custom-call(s32[8,3]{1,0:T(8,128)S(1)} %copy-done.8, s32[8,1,256]{2,1,0:T(1,128)S(1)} %bitcast.75, bf16[256,2048]{1,0:T(8,128)(2,1)S(1)} %copy-done.21, bf16[4,8,256,128]{3,2,1,0:T(8,128)(2,1)S(1)} %copy-done.15, bf16[256,2048]{1,0:T(8,128)(2,1)S(1)} %copy-done.17, ...), custom_call_target="tpu_custom_call" | custom-call | flops 71499997184 | bytes 1000000 | tf_op jit(solution)/shard_map/attend_back/pallas_call | solution.py:1591
  439.9 1.3 copy-done.13
  441.3 96.0 %backward_pairs.1 = (f32[8,128,256]{2,1,0:T(8,128)}, bf16[256,2048]{1,0:T(8,128)(2,1)}, bf16[8,256,256]{2,1,0:T(8,128)(2,1)}) custom-call(bf16[4,8,128,256]{3,2,1,0:T(8,128)(2,1)} %copy-done.13, bf16[704,2048]{1,0:T(8,128)(2,1)} %get-tuple-element.71.hidden_hbm, bf16[704,2048]{1,0:T(8,128)(2,1)} %all-gather.8.cloned.1.call-done.down_hbm, ...), custom_call_target="tpu_custom_call" | custom-call | flops 54999998464 | bytes 1000000 | tf_op jit(solution)/shard_map/backward_pairs/pallas_call | solution.py:1247
  537.3 1.1 slice.103
  538.8 1.1 slice_bitcast_fusion
  540.0 1.2 fusion.3
  541.7 1.1 pad_maximum_fusion.g_ref
  542.9 60.6 %backward_first.1 = (f32[256,2048]{1,0:T(8,128)}, f32[1,2048]{1,0:T(1,128)}, bf16[8,320,256]{2,1,0:T(8,128)(2,1)}) custom-call(bf16[320,2048]{1,0:T(8,128)(2,1)} %pad_maximum_fusion.g_ref, bf16[320,2048]{1,0:T(8,128)(2,1)} %pad_maximum_fusion.1.w_ref, bf16[8,256,2048]{2,1,0:T(8,128)(2,1)} %get-tuple-element.77.rows_hbm, bf16[256,2048]{1,0:T(8,128)(2,1)} %x_ref.5, ...), custom_call_target="tpu_custom_call" | custom-call | flops 65999998976 | bytes 1000000 | tf_op jit(solution)/shard_map/backward_first/pallas_call | solution.py:1316
  603.5 1.3 pad_maximum_fusion.5
  604.9 28.2 %last_exchange.1 = (bf16[8,1,176,256]{3,2,1,0:T(8,128)(2,1)}, bf16[8,2,176,256]{3,2,1,0:T(8,128)(2,1)}, f32[2,256]{1,0:T(2,128)}) custom-call(bf16[1,176,2048]{2,1,0:T(8,128)(2,1)} %bitcast.109, bf16[2,176,2048]{2,1,0:T(8,128)(2,1)} %bitcast.107, f32[8,2,256]{2,1,0:T(2,128)} %bitcast.101), custom_call_target="tpu_custom_call" | custom-call | flops 30799998976 | bytes 1000000 | tf_op jit(solution)/shard_map/last_exchange/pallas_call | solution.py:1399
  633.1 1.4 fusion.17
  634.6 1.5 copy.86
  636.4 1.5 copy.85
  638.5 1.3 bitcast_convert_fusion
  639.7 0.8 bitcast_convert_fusion.3
  640.6 1.4 convert_bitcast_fusion
  642.0 1.0 slice.108
  643.1 1.0 copy.84
  644.0 2.3 copy.91
  646.4 1.3 copy.92
  (110 shorter events, 4.5 us)
Async XLA Ops:
  7.2 4.8 copy-start.25
  7.2 6.5 copy-start.30
  7.2 6.5 copy-start.31
  7.2 240.1 %all-gather.4.cloned.1.call-start = ((), (), s32[]{:S(2)}) async-start(), calls=%async_computation.4 | async-start | bytes 3604480 | tf_op jit(solution)/shard_map/all_gather | solution.py:1677
  48.6 1.7 copy-start.36
  48.6 5.3 copy-start.5
  48.6 198.7 %all-gather.6.cloned.1.call-start = ((), (), s32[]{:S(2)}) async-start(), calls=%async_computation.5 | async-start | bytes 3604480 | tf_op jit(solution)/shard_map/all_gather | solution.py:1678
  49.4 8.4 %copy-start.9 = (bf16[256,2048]{1,0:T(8,128)(2,1)S(1)}, bf16[256,2048]{1,0:T(8,128)(2,1)}, u32[]{:S(2)}) copy-start(bf16[256,2048]{1,0:T(8,128)(2,1)} %x_ref.5) | copy-start | bytes 3145732
  49.4 8.4 %copy-start.10 = (bf16[512,256]{1,0:T(8,128)(2,1)S(1)}, bf16[512,256]{1,0:T(8,128)(2,1)}, u32[]{:S(2)}) copy-start(bf16[512,256]{1,0:T(8,128)(2,1)} %own_ref.1) | copy-start | bytes 786436
  49.4 8.4 %copy-start.11 = (bf16[4,640,256]{2,1,0:T(8,128)(2,1)S(1)}, bf16[4,640,256]{2,1,0:T(8,128)(2,1)}, u32[]{:S(2)}) copy-start(bf16[4,640,256]{2,1,0:T(8,128)(2,1)} %get-tuple-element.54.inner_ref) | copy-start | bytes 3932164
  49.4 197.9 %all-gather.8.cloned.1.call-start = ((), (), s32[]{:S(2)}) async-start(), calls=%async_computation.6 | async-start | bytes 3604480 | tf_op jit(solution)/shard_map/all_gather | solution.py:1676
  50.2 339.2 %reduce-scatter.5.cloned.1.call-start = ((), (), s32[]{:S(2)}) async-start(), calls=%async_computation.7 | async-start | bytes 3604480 | tf_op jit(solution)/shard_map/reduce_scatter | solution.py:1731
  50.2 117.9 %copy-start.34 = (f32[32]{0:T(128)}, f32[32]{0:T(128)S(1)}, u32[]{:S(2)}) copy-start(f32[32]{0:T(128)S(1)} %multiply_power_fusion) | copy-start | bytes 388
  53.1 116.6 %copy-start.3 = (s32[2048]{0:T(1024)}, s32[2048]{0:T(1024)S(1)}, u32[]{:S(2)}) copy-start(s32[2048]{0:T(1024)S(1)} %fusion.10) | copy-start | bytes 24580
  53.8 0.7 copy-start.28
  54.6 147.5 %copy-start.6 = (f32[1,8,256]{2,0,1:T(1,128)}, f32[1,8,256]{2,0,1:T(1,128)S(1)}, u32[]{:S(2)}) copy-start(f32[1,8,256]{2,0,1:T(1,128)S(1)} %get-tuple-element.104) | copy-start | bytes 24580
  56.3 111.8 %copy-start = (f32[32,2048]{1,0:T(8,128)}, f32[32,2048]{1,0:T(8,128)S(1)}, u32[]{:S(2)}) copy-start(f32[32,2048]{1,0:T(8,128)S(1)} %get-tuple-element.107.cos_ref) | copy-start | bytes 786436
  57.8 110.3 %copy-start.2 = (bf16[256,2048]{1,0:T(8,128)(2,1)}, bf16[256,2048]{1,0:T(8,128)(2,1)S(1)}, u32[]{:S(2)}) copy-start(bf16[256,2048]{1,0:T(8,128)(2,1)S(1)} %broadcast_select_fusion.dy_ref) | copy-start | bytes 3145732
  168.1 1.7 copy-start.14
  168.1 2.0 copy-start.20
  168.1 34.0 %copy-start.18 = (bf16[256,2048]{1,0:T(8,128)(2,1)}, bf16[256,2048]{1,0:T(8,128)(2,1)S(1)}, u32[]{:S(2)}) copy-start(bf16[256,2048]{1,0:T(8,128)(2,1)S(1)} %get-tuple-element.58.w_ref) | copy-start | bytes 3145732
  169.8 32.3 %copy-start.7 = (s32[8,3]{1,0:T(8,128)}, s32[8,3]{1,0:T(8,128)S(1)}, u32[]{:S(2)}) copy-start(s32[8,3]{1,0:T(8,128)S(1)} %pad_add_fusion.info_ref) | copy-start | bytes 292
  202.1 42.9 %copy-start.16 = (bf16[256,2048]{1,0:T(8,128)(2,1)}, bf16[256,2048]{1,0:T(8,128)(2,1)S(1)}, u32[]{:S(2)}) copy-start(bf16[256,2048]{1,0:T(8,128)(2,1)S(1)} %get-tuple-element.57.o_ref) | copy-start | bytes 3145732
  245.0 1.3 copy-start.12
  246.3 1.0 copy-start.19
  299.1 243.7 %reduce-scatter.7.cloned.1.call-start = ((), (), s32[]{:S(2)}) async-start(), calls=%async_computation.8 | async-start | bytes 7208960 | tf_op jit(solution)/shard_map/reduce_scatter | solution.py:1733
  389.4 0.7 copy-start.4
  389.4 0.7 copy-start.8
  389.4 1.2 copy-start.17
  389.4 215.4 %reduce-scatter.9.cloned.1.call-start = ((), (), s32[]{:S(2)}) async-start(), calls=%async_computation.9 | async-start | bytes 1310720 | tf_op jit(solution)/shard_map/reduce_scatter | solution.py:1761
  390.6 1.6 copy-start.15
  392.2 1.2 copy-start.21
  393.4 1.2 copy-start.22
  439.9 1.3 copy-start.13
  537.3 2.7 copy-start.29
  537.3 2.7 copy-start.35
  538.4 2.8 copy-start.1
  538.8 2.4 copy-start.24
  542.8 97.7 %reduce-scatter.11.cloned.1.call-start = ((), (), s32[]{:S(2)}) async-start(), calls=%async_computation.10 | async-start | bytes 1638400 | tf_op jit(solution)/shard_map/reduce_scatter | solution.py:1761
  542.9 60.6 %copy-start.32 = (f32[1,2048]{1,0:T(1,128)S(1)}, f32[1,2048]{1,0:T(1,128)}, u32[]{:S(2)}) copy-start(f32[1,2048]{1,0:T(1,128)} %get-tuple-element.87) | copy-start | bytes 24580
  636.2 1.7 copy-start.33
  636.2 2.3 copy-start.26
  636.3 3.4 copy-start.27
  643.0 3.4 copy-start.23
Sparse Core Ops, SparseCore 0:
  48.8 74.5 all-gather.3
  124.9 61.4 all-gather.5
  187.9 57.7 all-gather.7
  299.2 70.3 reduce-scatter.4
  389.6 134.3 reduce-scatter.6
  543.0 26.4 reduce-scatter.8
  605.0 30.0 reduce-scatter.10

commit v4 on v3

--- a/solution.py
+++ b/solution.py
@@ -548,186 +548,248 @@
     greet([(f ^ k, t) for k in (CORE, ALONG_X, ALONG_Y)])
 
 
-def forward_output(attended, output_rows, tokens, gain, number):
+def forward_output(attended, output_rows, tokens, gain, dys, down_all, number):
     size, width = tokens.shape
+    units = down_all.shape[2]
     f32, bf16 = jnp.float32, jnp.bfloat16
 
     def kernel(
-        o_ref, w_ref, x_ref, gain_ref,
-        middle_ref, row_ref,
+        o_ref, x_ref, gain_ref, w_hbm, dys_hbm, down_hbm,
+        middle_ref, row_ref, dh_ref,
         stage, other, held, from_x, from_y, last, sum_sent, sum_arrived,
+        dys, down_w, dys_sem, load_sem, dh, dh_sem, w, w_sem,
     ):
+        load = pltpu.make_async_copy(dys_hbm, dys, dys_sem)
+        loads = unit_loads(lambda j: down_hbm.at[:, j], down_w, load_sem)
+        output_loads = column_loads(w_hbm, w, w_sem)
+        for c in output_loads + loads + [load]:
+            c.start()
         plane_greet()
+        for c in output_loads:
+            c.wait()
         total = PlaneSum(stage, other, held, from_x, from_y, last, sum_sent, sum_arrived)
-        total.begin(chunk_part([(o_ref, w_ref)], size))
+        total.begin(chunk_part([(o_ref, w)], size))
+        for c in loads + [load]:
+            c.wait()
+
+        def out_copy(i):
+            return pltpu.make_async_copy(dh.at[i], dh_ref.at[i], dh_sem.at[i])
+
+        def grad_chunk(i, carry):
+            dh[i] = outer_cols(as_rows(down_w), dys[i])
+            out_copy(i).start()
+            return carry
+
+        lax.fori_loop(0, 6, grad_chunk, 0)
         total.turn()
+        lax.fori_loop(6, 8, grad_chunk, 0)
         total.end(middle_ref)
         middle = x_ref[...].astype(f32) + middle_ref[...]
         middle_ref[...] = middle
         inverse = lax.rsqrt(jnp.mean(middle * middle, axis=1, keepdims=True) + epsilon)
         row_ref[...] = (middle * inverse * gain_ref[...]).astype(bf16)
+        for i in range(8):
+            out_copy(i).wait()
         total.finish()
 
+    dma = pltpu.SemaphoreType.DMA
+    chunks = (8, 4 * units, size)
     return pl.pallas_call(
         kernel,
         out_shape=[
             jax.ShapeDtypeStruct((size, width), f32),
             jax.ShapeDtypeStruct((size, width), bf16),
+            jax.ShapeDtypeStruct(chunks, f32),
         ],
-        in_specs=[IN_VMEM] * 4,
-        out_specs=[IN_VMEM] * 2,
-        scratch_shapes=sum_scratch(size, width),
-        compiler_params=comm_params(number, 40 << 20),
+        in_specs=[IN_VMEM] * 3 + [ANYWHERE] * 3,
+        out_specs=[IN_VMEM] * 2 + [ANYWHERE],
+        scratch_shapes=sum_scratch(size, width)
+        + [
+            pltpu.VMEM((8, size, width), bf16),
+            pltpu.VMEM((4, units, width), bf16),
+            dma,
+            dma((8,)),
+            pltpu.VMEM(chunks, f32),
+            dma((8,)),
+            pltpu.VMEM((attended.shape[0], width), bf16),
+            dma((8,)),
+        ],
+        compiler_params=comm_params(number, VMEM_MOST),
         cost_estimate=lasting(45),
         name="forward_output",
-    )(attended, output_rows, tokens, gain)
-
-
-def forward_hidden(row, dys, gate_rows, up_rows, down_rows, number):
+    )(attended, tokens, gain, output_rows, dys, down_all)
+
+
+def forward_hidden(row, dys, dh_all, gate_up, number):
     size, width = row.shape
-    units = gate_rows.shape[0]
+    quarter = gate_up.shape[3]
+    units = 4 * quarter
     f32, bf16 = jnp.float32, jnp.bfloat16
 
     def kernel(
-        row_ref, dys_hbm, gate_hbm, up_hbm, down_hbm,
+        row_ref, dys_hbm, dh_hbm, gate_up_hbm,
         rows_ref, hidden_ref, dgate_ref, dup_ref, down_grad_ref,
-        rows, rows_sent, rows_arrived, dys, gate_w, up_w, down_w, load_sem, dh, out, out_sem, keep_sem, down_grad,
+        rows, rows_sent, rows_arrived, dys, gate_w, up_w, load_sem, unit_sem, dh, out, out_sem, keep_sem, down_grad,
     ):
         f = lax.axis_index("fsdp")
         loads = [
             pltpu.make_async_copy(source, target, load_sem.at[i])
-            for i, (source, target) in enumerate(
-                ((down_hbm, down_w), (dys_hbm, dys), (gate_hbm, gate_w), (up_hbm, up_w))
-            )
+            for i, (source, target) in enumerate(((dys_hbm, dys), (dh_hbm, dh)))
         ]
+        for i, w in enumerate((gate_w, up_w)):
+            loads += unit_loads(lambda j, i=i: gate_up_hbm.at[:, j, i], w, unit_sem.at[i])
         for load in loads:
             load.start()
         rows[f] = row_ref[...]
         plane_greet()
         gather_rows = PlaneGather(rows, rows_sent, rows_arrived)
         gather_rows.begin()
-        loads[0].wait()
-        loads[1].wait()
-
-        def grad_chunk(i, carry):
-            dh[i] = outer_cols(down_w[...], dys[i])
-            return carry
-
-        for k in range(PARTS):
-            lax.fori_loop(2 * k, 2 * k + 2, grad_chunk, 0)
-            gather_rows.advance(k)
-        loads[2].wait()
-        loads[3].wait()
-
-        def out_copies(slot, owner):
+        for load in loads:
+            load.wait()
+
+        half = size // 2
+        halves = (slice(0, half), slice(half, size))
+
+        def owners(i, crossed):
+            return f ^ i, f ^ (i ^ ALONG_X ^ ALONG_Y if crossed else i)
+
+        def out_copies(slot, pair):
             return [
                 pltpu.make_async_copy(
-                    out.at[slot, n], target.at[:, columns(owner, size)], out_sem.at[slot, n]
+                    out.at[slot, n, :, lanes],
+                    target.at[
+                        :, pl.ds(pl.multiple_of(owner * size + side * half, half), half)
+                    ],
+                    out_sem.at[slot, n, side],
                 )
                 for n, target in enumerate((hidden_ref, dgate_ref, dup_ref))
+                for side, (owner, lanes) in enumerate(zip(pair, halves))
             ]
 
-        def chunk(i, carry):
-            owner = f ^ i
-            slot = lax.rem(i, 2)
-
-            @pl.when(i >= 2)
-            def _():
-                for c in out_copies(slot, owner):
-                    c.wait()
-
-            gate = outer_cols(gate_w[...], rows[owner])
-            up = outer_cols(up_w[...], rows[owner])
-            sigmoid = jax.nn.sigmoid(gate)
-            active = gate * sigmoid
-            grad = dh[owner]
-            hidden = (active * up).astype(bf16)
-            out[slot, 0] = hidden
-            down_grad[...] += dot_nn(hidden, dys[owner])
-            out[slot, 1] = (grad * up * sigmoid * (1.0 + gate * (1.0 - sigmoid))).astype(bf16)
-            out[slot, 2] = (grad * active).astype(bf16)
-            for c in out_copies(slot, owner):
-                c.start()
-            return carry
+        def unit(crossed):
+            def body(i, carry):
+                pair = owners(i, crossed)
+                slot = lax.rem(i, 2)
+
+                @pl.when(i >= 2)
+                def _():
+                    for c in out_copies(slot, pair):
+                        c.wait()
+
+                right = jnp.concatenate([rows[o, r] for o, r in zip(pair, halves)], axis=0)
+                gate = outer_cols(as_rows(gate_w), right)
+                up = outer_cols(as_rows(up_w), right)
+                sigmoid = jax.nn.sigmoid(gate)
+                active = gate * sigmoid
+                grad = jnp.concatenate([dh[o, :, r] for o, r in zip(pair, halves)], axis=1)
+                hidden = (active * up).astype(bf16)
+                out[slot, 0] = hidden
+                out[slot, 1] = (grad * up * sigmoid * (1.0 + gate * (1.0 - sigmoid))).astype(bf16)
+                out[slot, 2] = (grad * active).astype(bf16)
+                for c in out_copies(slot, pair):
+                    c.start()
+                cotangent = jnp.concatenate([dys[o, r] for o, r in zip(pair, halves)], axis=0)
+                down_grad[...] += dot_nn(hidden, cotangent)
+                return carry
+
+            return body
+
+        def take(*pieces):
+            for slot, j in pieces:
+                gather_rows.arrive(slot, j)
 
         down_grad[...] = jnp.zeros_like(down_grad)
+        gather_rows.advance(0)
+        lax.fori_loop(0, 1, unit(False), 0)
+        gather_rows.advance(1)
         gather_rows.wait_core(0)
-        lax.fori_loop(0, 2, chunk, 0)
-        gather_rows.wait_core(3, 4)
-        lax.fori_loop(2, 4, chunk, 0)
+        lax.fori_loop(1, 2, unit(False), 0)
+        lax.fori_loop(2, 3, unit(True), 0)
+        gather_rows.advance(2)
+        take((3, 0), (3, 1), (4, 2), (4, 3))
+        lax.fori_loop(3, 4, unit(True), 0)
+        gather_rows.advance(3)
+        lax.fori_loop(4, 5, unit(True), 0)
+        take((3, 2), (3, 3), (4, 0), (4, 1))
+        lax.fori_loop(5, 6, unit(True), 0)
         gather_rows.far()
-        lax.fori_loop(4, 6, chunk, 0)
+        lax.fori_loop(6, 7, unit(False), 0)
         gather_rows.wait_core(5)
         keep = pltpu.make_async_copy(rows, rows_ref, keep_sem)
         keep.start()
-        lax.fori_loop(6, 8, chunk, 0)
-        down_grad_ref[...] = down_grad[...].astype(bf16)
+        lax.fori_loop(7, 8, unit(False), 0)
+        for j in range(8):
+            part = down_grad[:, j * size : (j + 1) * size].astype(bf16)
+            down_grad_ref[:, j] = part.reshape(4, quarter, size)
         for i in (6, 7):
-            for c in out_copies(i % 2, f ^ i):
+            for c in out_copies(i % 2, owners(i, False)):
                 c.wait()
         keep.wait()
         gather_rows.finish()
 
     store = pltpu.VMEM((8, size, width), bf16)
-    weights = pltpu.VMEM((units, width), bf16)
+    weights = pltpu.VMEM((4, quarter, width), bf16)
     return pl.pallas_call(
         kernel,
         out_shape=[jax.ShapeDtypeStruct((8, size, width), bf16)]
         + [jax.ShapeDtypeStruct((units, 8 * size), bf16)] * 3
-        + [jax.ShapeDtypeStruct((units, width), bf16)],
-        in_specs=[IN_VMEM] + [ANYWHERE] * 4,
+        + [jax.ShapeDtypeStruct((4, 8, quarter, size), bf16)],
+        in_specs=[IN_VMEM] + [ANYWHERE] * 3,
         out_specs=[ANYWHERE] * 4 + [IN_VMEM],
         scratch_shapes=[store]
         + GATHER_SEMAPHORES
         + [store]
-        + [weights] * 3
+        + [weights] * 2
         + [
-            pltpu.SemaphoreType.DMA((4,)),
+            pltpu.SemaphoreType.DMA((2,)),
+            pltpu.SemaphoreType.DMA((2, 8)),
             pltpu.VMEM((8, units, size), f32),
             pltpu.VMEM((2, 3, units, size), bf16),
-            pltpu.SemaphoreType.DMA((2, 3)),
+            pltpu.SemaphoreType.DMA((2, 3, 2)),
             pltpu.SemaphoreType.DMA,
             pltpu.VMEM((units, width), f32),
         ],
-        compiler_params=comm_params(number, 56 << 20),
+        compiler_params=comm_params(number, VMEM_MOST),
         cost_estimate=lasting(50),
         name="forward_hidden",
-    )(row, dys, gate_rows, up_rows, down_rows)
+    )(row, dys, dh_all, gate_up)
 
 
 def backward_middle(
-    dgate, dup, gate_rows, up_rows, rows, output_rows, attended, middle, grads, gain, number
+    dgate, dup, gate_up, rows, dys, output_rows, attended, middle, gain, number
 ):
     size, width = middle.shape
-    units = gate_rows.shape[0]
-    depth = output_rows.shape[0]
+    quarter = gate_up.shape[3]
+    units = 4 * quarter
+    depth = output_rows.shape[1]
     blocks = width // size
     f32, bf16 = jnp.float32, jnp.bfloat16
     early = 5
 
     def kernel(
-        dgate_hbm, dup_hbm, gate_hbm, up_hbm, rows_hbm,
-        w_ref, o_ref, middle_ref, dy_ref, gain_ref,
-        grad_ref, gain_grad_ref, grad_o_ref, do_ref, units_ref,
+        dgate_hbm, dup_hbm, gate_up_hbm, rows_hbm,
+        dys_hbm, w_hbm, o_ref, middle_ref, gain_ref,
+        grad_ref, gain_grad_ref, grad_o_ref, do_ref, gate_g_ref, up_g_ref,
         stage, other, held, from_x, from_y, last, sum_sent, sum_arrived,
         store, store_sent, store_arrived,
-        dgate_v, dup_v, gate_w, up_w, load_sem,
-        tall, tall_sem, out, out_sem, o_sum,
+        dgate_v, dup_v, gate_w, up_w, load_sem, unit_sem,
+        tall, tall_sem, out, out_sem, o_sum, dy, dy_sem, w_ref, w_sem,
     ):
         f = lax.axis_index("fsdp")
         loads = [
             pltpu.make_async_copy(source, target, load_sem.at[i])
-            for i, (source, target) in enumerate(
-                (
-                    (dgate_hbm, dgate_v),
-                    (gate_hbm, gate_w),
-                    (dup_hbm, dup_v),
-                    (up_hbm, up_w),
-                )
-            )
+            for i, (source, target) in enumerate(((dgate_hbm, dgate_v), (dup_hbm, dup_v)))
         ]
+        for i, w in enumerate((gate_w, up_w)):
+            loads += unit_loads(lambda j, i=i: gate_up_hbm.at[:, j, i], w, unit_sem.at[i])
         for load in loads:
             load.start()
+
+        load_dy = pltpu.make_async_copy(dys_hbm.at[f], dy, dy_sem)
+        load_dy.start()
+        output_loads = column_loads(w_hbm, w_ref, w_sem)
+        for c in output_loads:
+            c.start()
 
         def tall_load(n, slot):
             return pltpu.make_async_copy(
@@ -740,15 +802,15 @@
         gather = PlaneGather(store, store_sent, store_arrived)
         for load in loads:
             load.wait()
-        total.begin(chunk_part([(dgate_v, gate_w), (dup_v, up_w)], size))
+        total.begin(chunk_part([(dgate_v, Rows(gate_w)), (dup_v, Rows(up_w))], size))
         total.turn()
 
         def out_copies(n, slot):
             return [
                 pltpu.make_async_copy(
-                    out.at[slot, i], units_ref.at[:, i, :, columns(n, size)], out_sem.at[slot, i]
+                    out.at[slot, i], target.at[:, n], out_sem.at[slot, i]
                 )
-                for i in range(2)
+                for i, target in enumerate((gate_g_ref, up_g_ref))
             ]
 
         def block(n, carry):
@@ -767,7 +829,7 @@
 
             row_cols = tall[slot].reshape(8 * size, size)
             for i, left in enumerate((dgate_v, dup_v)):
-                out[slot, i] = dot_nn(left[...], row_cols).astype(bf16).reshape(4, units // 4, size)
+                out[slot, i] = dot_nn(left[...], row_cols).astype(bf16).reshape(4, quarter, size)
             for c in out_copies(n, slot):
                 c.start()
             return carry
@@ -779,7 +841,10 @@
         normed = middle * inverse
         grad = grad_ref[...]
         gain_grad_ref[...] = jnp.sum(grad * normed, axis=0, keepdims=True)
-        grad = dy_ref[...].astype(f32) + norm_back(grad, gain_ref[...], normed, inverse)
+        load_dy.wait()
+        for c in output_loads:
+            c.wait()
+        grad = dy[...].astype(f32) + norm_back(grad, gain_ref[...], normed, inverse)
         grad_ref[...] = grad
         store[f] = grad.astype(bf16)
         gather.begin()
@@ -806,41 +871,49 @@
         gather.far()
         gather.wait_core(5)
         lax.fori_loop(6, 8, chunk, 0)
-        grad_o_ref[...] = o_sum[...].astype(bf16)
+        for j in range(8):
+            grad_o_ref[j] = o_sum[:, j * size : (j + 1) * size].astype(bf16)
         for n in (blocks - 2, blocks - 1):
             for c in out_copies(n, n % 2):
                 c.wait()
         total.finish()
         gather.finish()
 
-    weights = pltpu.VMEM((units, width), bf16)
+    tall_units = pltpu.VMEM((units, width), bf16)
+    weights = pltpu.VMEM((4, quarter, width), bf16)
     return pl.pallas_call(
         kernel,
         out_shape=[
             jax.ShapeDtypeStruct((size, width), f32),
             jax.ShapeDtypeStruct((1, width), f32),
-            jax.ShapeDtypeStruct((depth, width), bf16),
+            jax.ShapeDtypeStruct((8, depth, size), bf16),
             jax.ShapeDtypeStruct((depth, 8 * size), bf16),
         ]
-        + [jax.ShapeDtypeStruct((4, 2, units // 4, width), bf16)],
-        in_specs=[ANYWHERE] * 5 + [IN_VMEM] * 5,
-        out_specs=[IN_VMEM] * 4 + [ANYWHERE],
+        + [jax.ShapeDtypeStruct((4, blocks, quarter, size), bf16)] * 2,
+        in_specs=[ANYWHERE] * 6 + [IN_VMEM] * 3,
+        out_specs=[IN_VMEM] * 4 + [ANYWHERE] * 2,
         scratch_shapes=sum_scratch(size, width)
         + [pltpu.VMEM((8, size, width), bf16)]
         + GATHER_SEMAPHORES
-        + [weights] * 4
+        + [tall_units] * 2
+        + [weights] * 2
         + [
-            pltpu.SemaphoreType.DMA((4,)),
+            pltpu.SemaphoreType.DMA((2,)),
+            pltpu.SemaphoreType.DMA((2, 8)),
             pltpu.VMEM((2, 8, size, size), bf16),
             pltpu.SemaphoreType.DMA((2,)),
-            pltpu.VMEM((2, 2, 4, units // 4, size), bf16),
+            pltpu.VMEM((2, 2, 4, quarter, size), bf16),
             pltpu.SemaphoreType.DMA((2, 2)),
             pltpu.VMEM((depth, width), f32),
+            pltpu.VMEM((size, width), bf16),
+            pltpu.SemaphoreType.DMA,
+            pltpu.VMEM((depth, width), bf16),
+            pltpu.SemaphoreType.DMA((8,)),
         ],
         compiler_params=comm_params(number, VMEM_MOST),
         cost_estimate=lasting(92),
         name="backward_middle",
-    )(dgate, dup, gate_rows, up_rows, rows, output_rows, attended, middle, grads, gain)
+    )(dgate, dup, gate_up, rows, dys, output_rows, attended, middle, gain)
 
 
 class LineGather:
@@ -893,82 +966,37 @@
 LINE_SEMAPHORES = [pltpu.SemaphoreType.DMA((2, 4)), pltpu.SemaphoreType.DMA((2, 4))]
 
 
-def line_greet(f, t):
-    barrier = pltpu.get_barrier_semaphore()
-    for k in range(1, 8):
-        pl.semaphore_signal(barrier, inc=1, device_id=(f ^ k, t), device_id_type=MESH)
-    for there, step in ((t < 3, 1), (t > 0, -1)):
-
-        @pl.when(there)
-        def _(step=step):
-            pl.semaphore_signal(barrier, inc=1, device_id=(f, t + step), device_id_type=MESH)
-
-    ends = (t == 0).astype(jnp.int32) + (t == 3).astype(jnp.int32)
-    pl.semaphore_wait(barrier, 9 - ends)
-
-
 def everyone(f, t):
     return [(f ^ k, t) for k in range(1, 8)] + [(f, lax.rem(t + k, 4)) for k in (1, 2, 3)]
 
 
-def first_exchange(parts, inner, gains, number):
-    _, units, block = parts[0].shape
-    count = len(parts)
-    far_first = (6, 7, 2, 4, 3, 5, 1)
-
-    def kernel(*refs):
-        sources, (inner_ref, gains_ref) = refs[:count], refs[count : count + 2]
-        targets, (inner_all, gains_all) = refs[count + 2 : 2 * count + 2], refs[2 * count + 2 : 2 * count + 4]
-        sent, arrived, z_sent, z_arrived, kept_sem = refs[2 * count + 4 :]
-        f, t = lax.axis_index("fsdp"), lax.axis_index("tp")
-        place = columns(f, block)
-        kept = [
-            pltpu.make_async_copy(s.at[f], o.at[:, place], kept_sem.at[i])
-            for i, (s, o) in enumerate(zip(sources, targets))
-        ] + [pltpu.make_async_copy(inner_ref, inner_all.at[t], kept_sem.at[count])]
-        for c in kept:
-            c.start()
-        gains_all[f] = gains_ref[...]
-        line_greet(f, t)
-        line = LineGather(inner_ref, inner_all, z_sent, z_arrived)
-        line.begin()
-        copies = []
-        for k in far_first:
-            copies.append(
-                remote(gains_ref, gains_all.at[f], sent.at[k, count], arrived.at[k, count], (f ^ k, t))
-            )
-        for i, (s, o) in enumerate(zip(sources, targets)):
-            for k in far_first:
-                copies.append(
-                    remote(s.at[f ^ k], o.at[:, place], sent.at[k, i], arrived.at[k, i], (f ^ k, t))
-                )
-        for c in copies:
-            c.start()
-        for hop in (1, 2, 3):
-            line.take(hop)
-        for c in kept + copies:
-            c.wait()
-        line.finish()
-
-    return pl.pallas_call(
-        kernel,
-        out_shape=[jax.ShapeDtypeStruct((units, 8 * block), jnp.bfloat16)] * count
-        + [
-            jax.ShapeDtypeStruct((4, *inner.shape), inner.dtype),
-            jax.ShapeDtypeStruct((8, *gains.shape), gains.dtype),
-        ],
-        in_specs=[ANYWHERE] * (count + 1) + [IN_VMEM],
-        out_specs=[ANYWHERE] * (count + 1) + [IN_VMEM],
-        scratch_shapes=[
-            pltpu.SemaphoreType.DMA((8, count + 1)),
-            pltpu.SemaphoreType.DMA((8, count + 1)),
-            *LINE_SEMAPHORES,
-            pltpu.SemaphoreType.DMA((count + 1,)),
-        ],
-        compiler_params=comm_params(number),
-        cost_estimate=lasting(32),
-        name="first_exchange",
-    )(*parts, inner, gains)
+def unit_loads(source, target, sems):
+    block = target.shape[2] // 8
+    return [
+        pltpu.make_async_copy(source(j), target.at[:, :, pl.ds(j * block, block)], sems.at[j])
+        for j in range(8)
+    ]
+
+
+class Rows:
+    def __init__(self, ref):
+        self.ref = ref
+
+    def __getitem__(self, index):
+        block = self.ref[:, :, index[1]]
+        return block.reshape(4 * block.shape[1], block.shape[2])
+
+
+def column_loads(source, target, sems):
+    block = source.shape[2]
+    return [
+        pltpu.make_async_copy(source.at[j], target.at[:, pl.ds(j * block, block)], sems.at[j])
+        for j in range(8)
+    ]
+
+
+def as_rows(ref):
+    return ref[...].reshape(4 * ref.shape[1], ref.shape[2])
 
 
 def turn_heads(values, cosine, sine_table):
@@ -982,7 +1010,37 @@
     return jnp.concatenate(turned, axis=0)
 
 
-def first_rows(tokens, gains, inner_all, output_own, cosine, sine_table, grads, number):
+def first_forms(gate, up, query, key_rows, value_rows):
+    bf16, f32 = jnp.bfloat16, jnp.float32
+    block, hidden = gate.shape
+    across = query.shape[1]
+    units = hidden // 8
+
+    def turned(ref):
+        return ref[...].astype(f32).T.astype(bf16)
+
+    def kernel(gate_ref, up_ref, q_ref, k_ref, v_ref, units_ref, inner_ref):
+        inner_ref[:across] = turned(q_ref)
+        inner_ref[across : across + HEAD_DIM] = k_ref[...]
+        inner_ref[across + HEAD_DIM :] = v_ref[...]
+        units_ref[:, 0] = turned(gate_ref).reshape(8, units, block)
+        units_ref[:, 1] = turned(up_ref).reshape(8, units, block)
+
+    return pl.pallas_call(
+        kernel,
+        out_shape=[
+            jax.ShapeDtypeStruct((8, 2, units, block), bf16),
+            jax.ShapeDtypeStruct((across + 2 * HEAD_DIM, block), bf16),
+        ],
+        in_specs=[IN_VMEM] * 5,
+        out_specs=[IN_VMEM] * 2,
+        compiler_params=pltpu.CompilerParams(vmem_limit_bytes=VMEM_MOST),
+        cost_estimate=lasting(5),
+        name="first_forms",
+    )(gate, up, query, key_rows, value_rows)
+
+
+def first_rows(tokens, gains_own, inner_all, output_own, cosine, sine_table, grads, valid, number):
     size, width = tokens.shape
     block = width // 8
     quarter_rows = output_own.shape[0]
@@ -991,13 +1049,14 @@
     f32, bf16 = jnp.float32, jnp.bfloat16
 
     def kernel(
-        x_ref, gains_ref, inner_ref, own_ref, cos_ref, sin_ref, dy_ref,
-        rows_ref, q_ref, pair_ref, w_ref, wo_ref, wo_all, dys_ref,
+        x_ref, gains_own_ref, inner_ref, own_ref, cos_ref, sin_ref, dy_ref, valid_ref,
+        rows_ref, q_ref, pair_ref, w_ref, wo_all, dys_ref, gains_ref,
         rows, rows_sent, rows_arrived, dys, dys_sent, dys_arrived, pair_v,
-        w_sent, w_arrived, o_sent, o_arrived, z_sent, z_arrived,
-        p_sent, p_arrived, on_sent, on_arrived, kept_sem,
+        w_sent, w_arrived, z_sent, z_arrived,
+        p_sent, p_arrived, on_sent, on_arrived, g_sent, g_arrived, kept_sem,
     ):
         f, t = lax.axis_index("fsdp"), lax.axis_index("tp")
+        gains_ref[f] = gains_own_ref[...]
         place = columns(f, block)
         far_first = (6, 7, 2, 4, 3, 5, 1)
 
@@ -1014,13 +1073,6 @@
                 ),
             ]
 
-        def output_slice(j):
-            quarter, side = lax.div(j, 2), lax.rem(j, 2)
-            return (
-                wo_all.at[quarter, pl.ds(pl.multiple_of(side * depth, depth), depth)],
-                wo_ref.at[:, place],
-            )
-
         kept = [
             pltpu.make_async_copy(s, o, kept_sem.at[i]) for i, (s, o) in enumerate(inner_slices(f))
         ]
@@ -1030,19 +1082,27 @@
         greet(everyone(f, t))
         line_output = LineGather(own_ref, wo_all, z_sent, z_arrived)
         line_output.begin()
-        copies, weights = [], []
+        weights, gains = [], []
+        for k in far_first:
+            c = remote(
+                gains_own_ref, gains_ref.at[f], g_sent.at[k], g_arrived.at[k], (f ^ k, t)
+            )
+            c.start()
+            gains.append(c)
         for k in far_first:
             for i, (s, o) in enumerate(inner_slices(f ^ k)):
                 c = remote(s, o, w_sent.at[k, i], w_arrived.at[k, i], (f ^ k, t))
                 c.start()
                 weights.append(c)
-        gain = jnp.concatenate([gains_ref[j, 0:1] for j in range(8)], axis=1)
         wide = x_ref[...].astype(f32)
         inverse = lax.rsqrt(jnp.mean(wide * wide, axis=1, keepdims=True) + epsilon)
+        for c in gains:
+            c.wait()
+        gain = jnp.concatenate([gains_ref[j, 0:1] for j in range(8)], axis=1)
         rows[f] = (wide * inverse * gain).astype(bf16)
         gather = PlaneGather(rows, rows_sent, rows_arrived)
         gather.begin()
-        dys[f] = dy_ref[...]
+        dys[f] = jnp.where(valid_ref[...] > 0, dy_ref[...].astype(f32), 0.0).astype(bf16)
         for k in range(PARTS):
             gather.advance(k)
         gather_dys = PlaneGather(dys, dys_sent, dys_arrived)
@@ -1051,7 +1111,6 @@
             c.wait()
         for c in weights:
             c.wait_recv()
-        line_output.take(1)
 
         def chunk(i, carry):
             owner = f ^ i
@@ -1086,7 +1145,6 @@
         lax.fori_loop(2, 6, chunk, 0)
         spread_pair(2)
         spread_pair(4)
-        line_output.take(2)
         gather.far()
         gather.wait_core(5)
         lax.fori_loop(6, 8, chunk, 0)
@@ -1095,18 +1153,10 @@
         own_pair.start()
         keep_rows = pltpu.make_async_copy(rows, rows_ref, kept_sem.at[4])
         keep_rows.start()
-        kept[2].wait()
-        line_output.take(3)
-        for k in far_first:
-            s, o = output_slice(f ^ k)
-            c = remote(s, o, o_sent.at[k], o_arrived.at[k], (f ^ k, t))
-            c.start()
-            copies.append(c)
-        s, o = output_slice(f)
-        keep_output = pltpu.make_async_copy(s, o, kept_sem.at[5])
-        keep_output.start()
+        line_output.take(1)
         for k in range(PARTS):
             gather_dys.advance(k)
+        line_output.take(2)
         passed = []
         for i, k, c in spread:
             c.wait_recv()
@@ -1119,7 +1169,8 @@
         gather_dys.wait_core(5)
         keep_dys = pltpu.make_async_copy(dys, dys_ref, kept_sem.at[6])
         keep_dys.start()
-        for c in passed + copies:
+        line_output.take(3)
+        for c in passed:
             c.wait()
         for c in weights + [c for _, _, c in spread]:
             c.wait_send()
@@ -1128,7 +1179,7 @@
         gather_dys.finish()
         own_pair.wait()
         keep_rows.wait()
-        keep_output.wait()
+        kept[2].wait()
         keep_dys.wait()
 
     dma = pltpu.SemaphoreType.DMA
@@ -1139,12 +1190,12 @@
             jax.ShapeDtypeStruct((depth, 8 * size), bf16),
             jax.ShapeDtypeStruct((4, 8, size, pair_rows), bf16),
             jax.ShapeDtypeStruct((depth + pair_rows, width), bf16),
-            jax.ShapeDtypeStruct((depth, width), bf16),
             jax.ShapeDtypeStruct((4, quarter_rows, block), bf16),
             jax.ShapeDtypeStruct((8, size, width), bf16),
+            jax.ShapeDtypeStruct((8, *gains_own.shape), f32),
         ],
-        in_specs=[IN_VMEM, IN_VMEM, ANYWHERE, ANYWHERE, IN_VMEM, IN_VMEM, IN_VMEM],
-        out_specs=[ANYWHERE, IN_VMEM, ANYWHERE, IN_VMEM, ANYWHERE, ANYWHERE, ANYWHERE],
+        in_specs=[IN_VMEM, IN_VMEM, ANYWHERE, ANYWHERE] + [IN_VMEM] * 4,
+        out_specs=[ANYWHERE, IN_VMEM, ANYWHERE, IN_VMEM, ANYWHERE, ANYWHERE, IN_VMEM],
         scratch_shapes=[pltpu.VMEM((8, size, width), bf16)]
         + GATHER_SEMAPHORES
         + [pltpu.VMEM((8, size, width), bf16)]
@@ -1153,42 +1204,76 @@
             pltpu.VMEM((8, size, pair_rows), bf16),
             dma((8, 2)),
             dma((8, 2)),
-            dma((8,)),
-            dma((8,)),
             *LINE_SEMAPHORES,
             dma((4, 4)),
             dma((4, 4)),
             dma((4, 4)),
             dma((4, 4)),
+            dma((8,)),
+            dma((8,)),
             dma((7,)),
         ],
-        compiler_params=comm_params(number, 40 << 20),
+        compiler_params=comm_params(number, VMEM_MOST),
         cost_estimate=lasting(100),
         name="first_rows",
-    )(tokens, gains, inner_all, output_own, cosine, sine_table, grads)
-
-
-def backward_pairs(pair_parts, hidden, down_rows, middle, valid, grad_output, number):
+    )(tokens, gains_own, inner_all, output_own, cosine, sine_table, grads, valid)
+
+
+def grads_across(left_ref, rows_v, out_v, target_ref, sent, arrived, kept_sem):
+    f, t = lax.axis_index("fsdp"), lax.axis_index("tp")
+    _, size, width = rows_v.shape
+    block = width // 8
+    copies = []
+
+    def step(k):
+        right = rows_v[:, :, columns(f ^ k, block)].reshape(8 * size, block)
+        out_v[k] = dot_nn(left_ref[...], right).astype(jnp.bfloat16)
+        if k:
+            c = remote(out_v.at[k], target_ref.at[f], sent.at[k], arrived.at[k], (f ^ k, t))
+        else:
+            c = pltpu.make_async_copy(out_v.at[0], target_ref.at[f], kept_sem)
+        c.start()
+        copies.append(c)
+
+    return step, copies
+
+
+def exchange_begin(ways, sent, arrived, kept_sem):
+    f, t = lax.axis_index("fsdp"), lax.axis_index("tp")
+    copies = []
+    for i, (source, target) in enumerate(ways):
+        for k in (6, 7, 2, 4, 3, 5, 1):
+            copies.append(
+                remote(
+                    source.at[f ^ k], target.at[f], sent.at[k, i], arrived.at[k, i], (f ^ k, t)
+                )
+            )
+        copies.append(pltpu.make_async_copy(source.at[f], target.at[f], kept_sem.at[i]))
+    for c in copies:
+        c.start()
+    return copies
+
+
+def backward_pairs(pair_parts, hidden, down_all, middle, valid, grad_query, rows, cosine, sine_table, number):
     size, width = middle.shape
     units = hidden.shape[0]
-    depth = grad_output.shape[0]
+    depth = grad_query.shape[0]
     _, chunks, height, _ = pair_parts.shape
     half = chunks // 2
     f32, bf16 = jnp.float32, jnp.bfloat16
 
     def kernel(
-        p_ref, hidden_hbm, down_hbm, middle_ref, valid_ref, g_ref,
-        pair_ref, out_ref, spread_ref,
+        p_ref, hidden_hbm, down_hbm, middle_ref, valid_ref, g_ref, rows_hbm, cos_ref, sin_ref,
+        single_ref, out_ref, spread_ref,
         stage, other, held, from_x, from_y, last, sum_sent, sum_arrived,
-        hidden_v, down_w, load_sem, ra, s, rz, sent, arrived, g_sent, g_arrived, share,
+        hidden_v, down_w, load_sem, unit_sem, ra, s, rz, sent, arrived, share, pair,
+        rows_v, w_grad, w_sent, w_arrived,
     ):
         f, t = lax.axis_index("fsdp"), lax.axis_index("tp")
-        loads = [
-            pltpu.make_async_copy(hidden_hbm, hidden_v, load_sem.at[0]),
-            pltpu.make_async_copy(down_hbm, down_w, load_sem.at[1]),
-            pltpu.make_async_copy(g_ref.at[:, columns(f, size)], spread_ref.at[f], load_sem.at[2]),
-        ]
-        for c in loads:
+        loads = [pltpu.make_async_copy(hidden_hbm, hidden_v, load_sem.at[0])]
+        loads += unit_loads(lambda j: down_hbm.at[:, j], down_w, unit_sem)
+        load_rows = pltpu.make_async_copy(rows_hbm, rows_v, load_sem.at[1])
+        for c in loads + [load_rows]:
             c.start()
         side = lax.rem(f, 2)
         mine, theirs = pl.ds(side * half, half), pl.ds((1 - side) * half, half)
@@ -1211,34 +1296,32 @@
                 d.start()
                 out.append((k, d))
             else:
-                pair_ref[mine] = both
-        for c in loads[:2]:
+                pair[mine] = both
+        for c in loads:
             c.wait()
         total = PlaneSum(stage, other, held, from_x, from_y, last, sum_sent, sum_arrived)
-        total.begin(chunk_part([(hidden_v, down_w)], size))
-        spread = []
-        for k in (6, 7, 2, 4, 3, 5, 1):
-            c = remote(
-                g_ref.at[:, columns(f ^ k, size)],
-                spread_ref.at[f],
-                g_sent.at[k],
-                g_arrived.at[k],
-                (f ^ k, t),
-            )
-            c.start()
-            spread.append(c)
+        total.begin(chunk_part([(hidden_v, Rows(down_w))], size))
+        load_rows.wait()
+        query_grads, copies = grads_across(
+            g_ref, rows_v, w_grad, spread_ref, w_sent, w_arrived, load_sem.at[2]
+        )
+        for k in (6, 7, 2, 4, 3, 5, 1, 0):
+            query_grads(k)
         total.turn()
         for k, d in out:
             d.wait_recv()
-            pair_ref[mine] += rz[k].astype(f32)
-        back = remote(pair_ref.at[mine], pair_ref.at[mine], sent.at[7], arrived.at[7], core)
+            pair[mine] += rz[k].astype(f32)
+        back = remote(pair.at[mine], pair.at[mine], sent.at[7], arrived.at[7], core)
         back.start()
+        back.wait()
+        for j in range(chunks):
+            lanes = slice(j * size, (j + 1) * size)
+            keys = turn_heads(pair[j, :HEAD_DIM], cos_ref[:, lanes], -sin_ref[:, lanes])
+            single_ref[:, lanes] = jnp.where(side == 0, keys, pair[j, HEAD_DIM:]).astype(bf16)
         total.end(share)
         out_ref[...] = jnp.where(valid_ref[...] > 0, middle_ref[...] + share[...], 0.0).astype(bf16)
-        back.wait()
-        for c in spread:
+        for c in copies:
             c.wait()
-        loads[2].wait()
         for k, c in first + out:
             c.wait_send()
         total.finish()
@@ -1247,59 +1330,64 @@
     return pl.pallas_call(
         kernel,
         out_shape=[
-            jax.ShapeDtypeStruct((chunks, height, size), f32),
+            jax.ShapeDtypeStruct((HEAD_DIM, chunks * size), bf16),
             jax.ShapeDtypeStruct((size, width), bf16),
-            jax.ShapeDtypeStruct((8, depth, size), bf16),
+            jax.ShapeDtypeStruct((8, depth, width // 8), bf16),
         ],
-        in_specs=[IN_VMEM, ANYWHERE, ANYWHERE, IN_VMEM, IN_VMEM, ANYWHERE],
+        in_specs=[IN_VMEM, ANYWHERE, ANYWHERE, IN_VMEM, IN_VMEM, IN_VMEM, ANYWHERE, IN_VMEM, IN_VMEM],
         out_specs=[IN_VMEM, IN_VMEM, ANYWHERE],
         scratch_shapes=sum_scratch(size, width)
-        + [pltpu.VMEM((units, 8 * size), bf16), pltpu.VMEM((units, width), bf16), dma((3,))]
+        + [pltpu.VMEM((units, 8 * size), bf16), pltpu.VMEM((4, units // 4, width), bf16)]
+        + [dma((3,)), dma((8,))]
         + [pltpu.VMEM((4, half, height, size), bf16)] * 3
-        + [dma((8,)), dma((8,)), dma((8,)), dma((8,)), pltpu.VMEM((size, width), f32)],
+        + [dma((8,)), dma((8,)), pltpu.VMEM((size, width), f32)]
+        + [
+            pltpu.VMEM((chunks, height, size), f32),
+            pltpu.VMEM((8, size, width), bf16),
+            pltpu.VMEM((8, depth, width // 8), bf16),
+            dma((8,)),
+            dma((8,)),
+        ],
         compiler_params=comm_params(number, VMEM_MOST),
-        cost_estimate=lasting(50),
+        cost_estimate=lasting(55),
         name="backward_pairs",
-    )(pair_parts, hidden, down_rows, middle, valid, grad_output)
-
-
-def backward_first(grad_inner, weights, rows, tokens, grad_middle, gain, number):
+    )(pair_parts, hidden, down_all, middle, valid, grad_query, rows, cosine, sine_table)
+
+
+def backward_first(
+    grad_query, single, weights, rows, tokens, grad_middle, gain, down_grads, gate_grads, number
+):
     size, width = tokens.shape
-    depth = grad_inner.shape[0]
+    depth = grad_query.shape[0]
     block = width // 8
     f32, bf16 = jnp.float32, jnp.bfloat16
 
     def kernel(
-        g_ref, w_ref, rows_hbm, x_ref, middle_ref, gain_ref,
-        tokens_grad_ref, gain_grad_ref, spread_ref,
+        g_ref, single_ref, w_ref, rows_hbm, x_ref, middle_ref, gain_ref, down_ref, gate_ref,
+        tokens_grad_ref, gain_grad_ref, spread_ref, own_down_ref, own_gate_ref,
         stage, other, held, from_x, from_y, last, sum_sent, sum_arrived,
-        rows_v, load_sem, w_grad, sent, arrived,
+        rows_v, load_sem, w_grad, sent, arrived, single_w, e_sent, e_arrived, e_kept,
     ):
         f, t = lax.axis_index("fsdp"), lax.axis_index("tp")
         load = pltpu.make_async_copy(rows_hbm, rows_v, load_sem.at[0])
         load.start()
+        side = lax.rem(f, 2)
+        single_w[...] = w_ref[
+            pl.ds(pl.multiple_of(depth + side * HEAD_DIM, HEAD_DIM), HEAD_DIM), :
+        ]
         greet([(f ^ k, t) for k in range(1, 8)])
         total = PlaneSum(stage, other, held, from_x, from_y, last, sum_sent, sum_arrived)
-        total.begin(chunk_part([(g_ref, w_ref)], size))
+        total.begin(chunk_part([(g_ref, w_ref.at[pl.ds(0, depth)]), (single_ref, single_w)], size))
         load.wait()
-        spread = []
-
-        def weight_grad(k):
-            j = f ^ k
-            right = rows_v[:, :, columns(j, block)].reshape(8 * size, block)
-            w_grad[k] = dot_nn(g_ref[...], right).astype(bf16)
-            if k:
-                c = remote(w_grad.at[k], spread_ref.at[f], sent.at[k], arrived.at[k], (j, t))
-                c.start()
-                spread.append(c)
-
-        for k in (6, 7, 2, 4):
-            weight_grad(k)
+        single_grads, copies = grads_across(
+            single_ref, rows_v, w_grad, spread_ref, sent, arrived, load_sem.at[1]
+        )
+        for k in (6, 7, 2, 4, 3, 5, 1, 0):
+            single_grads(k)
         total.turn()
-        for k in (3, 5, 1, 0):
-            weight_grad(k)
-        keep = pltpu.make_async_copy(w_grad.at[0], spread_ref.at[f], load_sem.at[1])
-        keep.start()
+        exchange = exchange_begin(
+            ((down_ref, own_down_ref), (gate_ref, own_gate_ref)), e_sent, e_arrived, e_kept
+        )
         wide = x_ref[...].astype(f32)
         inverse = lax.rsqrt(jnp.mean(wide * wide, axis=1, keepdims=True) + epsilon)
         normed = wide * inverse
@@ -1307,9 +1395,8 @@
         grad = tokens_grad_ref[...]
         gain_grad_ref[...] = jnp.sum(grad * normed, axis=0, keepdims=True)
         tokens_grad_ref[...] = middle_ref[...] + norm_back(grad, gain_ref[...], normed, inverse)
-        for c in spread:
+        for c in copies + exchange:
             c.wait()
-        keep.wait()
         total.finish()
 
     dma = pltpu.SemaphoreType.DMA
@@ -1318,64 +1405,60 @@
         out_shape=[
             jax.ShapeDtypeStruct((size, width), f32),
             jax.ShapeDtypeStruct((1, width), f32),
-            jax.ShapeDtypeStruct((8, depth, block), bf16),
+            jax.ShapeDtypeStruct((8, HEAD_DIM, block), bf16),
+            jax.ShapeDtypeStruct(down_grads.shape, bf16),
+            jax.ShapeDtypeStruct(gate_grads.shape, bf16),
         ],
-        in_specs=[IN_VMEM, IN_VMEM, ANYWHERE, IN_VMEM, IN_VMEM, IN_VMEM],
-        out_specs=[IN_VMEM, IN_VMEM, ANYWHERE],
+        in_specs=[IN_VMEM] * 3 + [ANYWHERE] + [IN_VMEM] * 3 + [ANYWHERE] * 2,
+        out_specs=[IN_VMEM, IN_VMEM, ANYWHERE, ANYWHERE, ANYWHERE],
         scratch_shapes=sum_scratch(size, width)
         + [
             pltpu.VMEM((8, size, width), bf16),
             dma((2,)),
-            pltpu.VMEM((8, depth, block), bf16),
+            pltpu.VMEM((8, HEAD_DIM, block), bf16),
             dma((8,)),
             dma((8,)),
+            pltpu.VMEM((HEAD_DIM, width), bf16),
+            dma((8, 2)),
+            dma((8, 2)),
+            dma((2,)),
         ],
         compiler_params=comm_params(number, VMEM_MOST),
-        cost_estimate=lasting(60),
+        cost_estimate=lasting(62),
         name="backward_first",
-    )(grad_inner, weights, rows, tokens, grad_middle, gain)
-
-
-def last_exchange(down_grads, hidden_grads, gain_parts, number):
-    _, units, width = hidden_grads.shape
-    arrays = (down_grads, hidden_grads)
+    )(grad_query, single, weights, rows, tokens, grad_middle, gain, down_grads, gate_grads)
+
+
+def last_sums(gain_first, gain_second, pair_parts, up_grads, number):
+    width = gain_first.shape[1]
     block = width // 8
-    f32, bf16 = jnp.float32, jnp.bfloat16
-    far_first = (6, 7, 2, 4, 3, 5, 1)
+    f32 = jnp.float32
 
     def kernel(
-        source_0, source_1, gains_ref, target_0, target_1, sums_ref, taken, planes, sent, arrived, z_sent, z_arrived, kept_sem
+        first_ref, second_ref, p_ref, up_ref, sums_ref, pair_ref, own_up_ref,
+        gains, taken, planes, pairs, sent, arrived, z_sent, z_arrived, p_sent, p_arrived, e_sent, e_arrived, e_kept,
     ):
         f, t = lax.axis_index("fsdp"), lax.axis_index("tp")
-        ways = ((source_0, target_0), (source_1, target_1))
-        kept = [
-            pltpu.make_async_copy(s.at[:, :, columns(f, block)], o.at[f], kept_sem.at[i])
-            for i, (s, o) in enumerate(ways)
-        ]
-        for c in kept:
-            c.start()
+        for j in range(8):
+            lanes = slice(j * block, (j + 1) * block)
+            gains[j] = jnp.concatenate([first_ref[:, lanes], second_ref[:, lanes]], axis=0)
         greet(everyone(f, t))
-        gains = []
-        for k in far_first:
+        copies = []
+        for k in (2, 1, 3):
+            plane = lax.rem(t + k, 4)
             c = remote(
-                gains_ref.at[f ^ k], taken.at[k], sent.at[k, 0], arrived.at[k, 0], (f ^ k, t)
+                p_ref.at[pl.ds(2 * plane, 2)], pairs.at[k], p_sent.at[k], p_arrived.at[k], (f, plane)
             )
             c.start()
-            gains.append(c)
-        copies = []
-        for i, (s, o) in enumerate(ways):
-            for k in far_first:
-                c = remote(
-                    s.at[:, :, columns(f ^ k, block)],
-                    o.at[f],
-                    sent.at[k, 1 + i],
-                    arrived.at[k, 1 + i],
-                    (f ^ k, t),
-                )
-                c.start()
-                copies.append(c)
-        total = gains_ref[f]
-        for k, c in zip(far_first, gains):
+            copies.append(c)
+        spread = []
+        for k in (6, 7, 2, 4, 3, 5, 1):
+            c = remote(gains.at[f ^ k], taken.at[k], sent.at[k], arrived.at[k], (f ^ k, t))
+            c.start()
+            spread.append((k, c))
+        exchange = exchange_begin(((up_ref, own_up_ref),), e_sent, e_arrived, e_kept)
+        total = gains[f]
+        for k, c in spread:
             c.wait_recv()
             total += taken[k]
         planes[0] = total
@@ -1384,39 +1467,131 @@
             c = remote(planes.at[0], planes.at[k], z_sent.at[k], z_arrived.at[k], (f, lax.rem(t + k, 4)))
             c.start()
             along_z.append(c)
+        pair = p_ref[pl.ds(2 * t, 2)].astype(f32)
+        for k, c in zip((2, 1, 3), copies):
+            c.wait_recv()
+            pair += pairs[k].astype(f32)
+        pair_ref[...] = pair
         for c in along_z:
             c.wait_recv()
-        sums = planes[lax.rem(t, 4)]
+        sums = planes[t]
         for plane in (1, 2, 3):
             sums += planes[lax.rem(t + 4 - plane, 4)]
         sums_ref[...] = sums
-        for c in kept + copies:
+        for c in [c for _, c in spread] + along_z + copies:
+            c.wait_send()
+        for c in exchange:
             c.wait()
-        for c in gains + along_z:
-            c.wait_send()
 
     dma = pltpu.SemaphoreType.DMA
     return pl.pallas_call(
         kernel,
         out_shape=[
-            *(jax.ShapeDtypeStruct((8, len(x), units, block), bf16) for x in arrays),
-            jax.ShapeDtypeStruct(gain_parts.shape[1:], f32),
+            jax.ShapeDtypeStruct((2, block), f32),
+            jax.ShapeDtypeStruct((2, *pair_parts.shape[1:]), f32),
+            jax.ShapeDtypeStruct(up_grads.shape, up_grads.dtype),
         ],
-        in_specs=[ANYWHERE, ANYWHERE, IN_VMEM],
-        out_specs=[ANYWHERE, ANYWHERE, IN_VMEM],
+        in_specs=[IN_VMEM] * 3 + [ANYWHERE],
+        out_specs=[IN_VMEM] * 2 + [ANYWHERE],
         scratch_shapes=[
-            pltpu.VMEM(gain_parts.shape, f32),
-            pltpu.VMEM((4, *gain_parts.shape[1:]), f32),
-            dma((8, 3)),
-            dma((8, 3)),
+            pltpu.VMEM((8, 2, block), f32),
+            pltpu.VMEM((8, 2, block), f32),
+            pltpu.VMEM((4, 2, block), f32),
+            pltpu.VMEM((4, 2, *pair_parts.shape[1:]), pair_parts.dtype),
+            dma((8,)),
+            dma((8,)),
             dma((4,)),
             dma((4,)),
-            dma((2,)),
+            dma((4,)),
+            dma((4,)),
+            dma((8, 1)),
+            dma((8, 1)),
+            dma((1,)),
         ],
-        compiler_params=comm_params(number),
-        cost_estimate=lasting(28),
-        name="last_exchange",
-    )(down_grads, hidden_grads, gain_parts)
+        compiler_params=comm_params(number, VMEM_MOST),
+        cost_estimate=lasting(16),
+        name="last_sums",
+    )(gain_first, gain_second, pair_parts, up_grads)
+
+
+def last_forms(layer_out, tokens_grad, grad_query, grad_output, grad_down, grad_gate, grad_up):
+    f32 = jnp.float32
+    across = grad_query.shape[0]
+    block = grad_query.shape[1]
+    units = grad_down.shape[1]
+    tall = 8 * units
+
+    def kernel(
+        out_in, tokens_in, query_in, output_in, down_in, gate_in, up_in,
+        out_o, tokens_o, query_o, output_o, gate_o, up_o, down_o,
+        out_v, tokens_v, query_v, output_v, down_v, gate_v, up_v,
+        query_w, output_w, gate_w, up_w, down_w, in_sem, out_sem,
+    ):
+        loads = [
+            pltpu.make_async_copy(source, target, in_sem.at[i])
+            for i, (source, target) in enumerate(
+                (
+                    (gate_in, gate_v),
+                    (up_in, up_v),
+                    (down_in, down_v),
+                    (out_in, out_v),
+                    (tokens_in, tokens_v),
+                    (query_in, query_v),
+                    (output_in, output_v),
+                )
+            )
+        ]
+        for c in loads:
+            c.start()
+        stores = []
+
+        def store(source, target):
+            c = pltpu.make_async_copy(source, target, out_sem.at[len(stores)])
+            c.start()
+            stores.append(c)
+
+        for n, (tight, wide, target) in enumerate(((gate_v, gate_w, gate_o), (up_v, up_w, up_o))):
+            loads[n].wait()
+            wide[...] = tight[...].reshape(tall, block).astype(f32).T
+            store(wide, target)
+        loads[2].wait()
+        down_w[...] = down_v[...].reshape(tall, block).astype(f32)
+        store(down_w, down_o)
+        loads[3].wait()
+        store(out_v, out_o)
+        loads[4].wait()
+        store(tokens_v, tokens_o)
+        loads[5].wait()
+        query_w[...] = query_v[...].astype(f32).T
+        store(query_w, query_o)
+        loads[6].wait()
+        output_w[...] = output_v[...].astype(f32)
+        store(output_w, output_o)
+        for c in stores:
+            c.wait()
+
+    operands = (layer_out, tokens_grad, grad_query, grad_output, grad_down, grad_gate, grad_up)
+    results = [
+        jax.ShapeDtypeStruct(layer_out.shape, layer_out.dtype),
+        jax.ShapeDtypeStruct(tokens_grad.shape, f32),
+        jax.ShapeDtypeStruct((block, across), f32),
+        jax.ShapeDtypeStruct((across, block), f32),
+        jax.ShapeDtypeStruct((block, tall), f32),
+        jax.ShapeDtypeStruct((block, tall), f32),
+        jax.ShapeDtypeStruct((tall, block), f32),
+    ]
+    return pl.pallas_call(
+        kernel,
+        out_shape=results,
+        in_specs=[ANYWHERE] * 7,
+        out_specs=[ANYWHERE] * 7,
+        scratch_shapes=[pltpu.VMEM(x.shape, x.dtype) for x in operands]
+        + [pltpu.VMEM(x.shape, x.dtype) for x in results[2:]]
+        + [pltpu.SemaphoreType.DMA((7,)), pltpu.SemaphoreType.DMA((7,))],
+        compiler_params=pltpu.CompilerParams(vmem_limit_bytes=VMEM_MOST),
+        cost_estimate=lasting(8),
+        name="last_forms",
+    )(*operands)
 
 
 def dot_nn(left, right):
@@ -1517,20 +1692,20 @@
             jax.ShapeDtypeStruct((depth, slots), jnp.bfloat16),
             jax.ShapeDtypeStruct((8, 1, span), jnp.float32),
         ],
-        compiler_params=pltpu.CompilerParams(vmem_limit_bytes=40 << 20),
+        compiler_params=pltpu.CompilerParams(vmem_limit_bytes=VMEM_MOST),
         cost_estimate=lasting(50),
         name="attend",
     )(info, begins, queries, pair)
 
 
-def attend_back(info, begins, queries, pair, outputs, grads, totals):
+def attend_back(info, begins, queries, pair, outputs, grads, totals, cosine, sine_table):
     depth, slots = queries.shape
     heads = depth // HEAD_DIM
     size = slots // 8
     span = heads * size
 
     def kernel(
-        info_ref, begin_ref, q_ref, kv_ref, o_ref, g_ref, l_ref, dq_ref, dkv_ref, q_s, g_s, d_s, a_s, w_s
+        info_ref, begin_ref, q_ref, kv_ref, o_ref, g_ref, l_ref, cos_ref, sin_ref, dq_ref, dkv_ref, q_s, g_s, d_s, a_s, w_s
     ):
         f = pl.program_id(0)
         low, middle, own = info_ref[f, 0], info_ref[f, 1], info_ref[f, 2]
@@ -1581,8 +1756,8 @@
         lax.fori_loop(low, middle, masked_step, 0)
         lax.fori_loop(0, lax.div(own - middle, WIDE), plain_step, 0)
         result = a_s[...] * HEAD_DIM ** (-0.5)
-        for h in range(heads):
-            dq_ref[h * HEAD_DIM : (h + 1) * HEAD_DIM] = result[:, h * size : (h + 1) * size]
+        result = jnp.concatenate([result[:, h * size : (h + 1) * size] for h in range(heads)], axis=0)
+        dq_ref[...] = turn_heads(result, cos_ref[...], -sin_ref[...]).astype(jnp.bfloat16)
 
         @pl.when(f == 7)
         def _():
@@ -1600,6 +1775,8 @@
                 pl.BlockSpec((depth, size), lambda f, info: (0, f)),
                 pl.BlockSpec((depth, size), lambda f, info: (0, f)),
                 pl.BlockSpec((1, 1, span), lambda f, info: (f, 0, 0)),
+                pl.BlockSpec((HEAD_DIM // 2, size), lambda f, info: (0, f)),
+                pl.BlockSpec((HEAD_DIM // 2, size), lambda f, info: (0, f)),
             ],
             out_specs=[
                 pl.BlockSpec((depth, size), lambda f, info: (0, f)),
@@ -1614,27 +1791,13 @@
             ],
         ),
         out_shape=[
-            jax.ShapeDtypeStruct((depth, slots), jnp.float32),
+            jax.ShapeDtypeStruct((depth, slots), jnp.bfloat16),
             jax.ShapeDtypeStruct((4, 8, 2 * HEAD_DIM, size), jnp.bfloat16),
         ],
-        compiler_params=pltpu.CompilerParams(vmem_limit_bytes=40 << 20),
+        compiler_params=pltpu.CompilerParams(vmem_limit_bytes=VMEM_MOST),
         cost_estimate=lasting(65),
         name="attend_back",
-    )(info, begins, queries, pair, outputs, grads, totals)
-
-
-def turn(values, cosine, sine_table):
-    heads = values.shape[0] // HEAD_DIM
-    split = values.reshape(heads, 2, HEAD_DIM // 2, values.shape[1])
-    first, second = split[:, 0], split[:, 1]
-    turned = jnp.stack(
-        [first * cosine - second * sine_table, second * cosine + first * sine_table], axis=1
-    )
-    return turned.reshape(values.shape)
-
-
-def turn_back(values, cosine, sine_table):
-    return turn(values, cosine, -sine_table)
+    )(info, begins, queries, pair, outputs, grads, totals, cosine, sine_table)
 
 
 def segment_begins(slots, lengths):
@@ -1667,17 +1830,22 @@
     units = gate_weight.shape[1] // 8
     bf16, f32 = jnp.bfloat16, jnp.float32
 
-    inner_own = jnp.concatenate([query_weight.T, key_weight.T, value_weight.T], axis=0)
-    hidden_parts = [w.reshape(8, units, block) for w in (down_weight, gate_weight.T, up_weight.T)]
+    def across_plane(parts):
+        return lax.all_to_all(parts, "fsdp", 0, 0, tiled=False)
+
+    def planes_together(part):
+        flat = part.reshape(-1, block)
+        return lax.all_gather(flat, "tp", axis=0, tiled=True).reshape(4, *part.shape)
+
+    gate_up, inner_own = first_forms(
+        gate_weight, up_weight, query_weight, key_weight.T, value_weight.T
+    )
+    inner_all = planes_together(inner_own)
+    down_all = across_plane(down_weight.reshape(8, units, block))
+    gate_up = across_plane(gate_up)
+    tokens, down_all = lax.optimization_barrier((tokens, down_all))
+    down_all = planes_together(down_all)
     gains_own = jnp.stack([attn_gain, mlp_gain]).astype(f32)
-    down_part, gate_part, up_part, inner_all, gains_all = first_exchange(
-        hidden_parts, inner_own, gains_own, 1
-    )
-    down_rows = lax.all_gather(down_part, "tp", axis=0, tiled=True)
-    gate_rows = lax.all_gather(gate_part, "tp", axis=0, tiled=True)
-    up_rows = lax.all_gather(up_part, "tp", axis=0, tiled=True)
-    gains = jnp.moveaxis(gains_all, 0, 1).reshape(2, width)
-    gain_first, gain_second = gains[0:1], gains[1:2]
 
     my_slots = (f * 4 + t) * size + jnp.arange(size, dtype=jnp.int32)
     _, my_valid = segment_begins(my_slots, lengths)
@@ -1700,88 +1868,100 @@
     angles = positions.astype(f32)[None, :] * frequency[:, None]
     cosine, sine_table = jnp.cos(angles), jnp.sin(angles)
 
-    grad_rows_own = jnp.where(valid_rows, out_grad, jnp.zeros_like(out_grad))
-    rows_first, queries, pair, inner_rows_w, output_rows, _, grad_rows = first_rows(
-        tokens, gains_all, inner_all, output_weight, cosine, sine_table, grad_rows_own, 2
-    )
+    valid_rows = valid_rows.astype(f32)
+    rows_first, queries, pair, inner_rows_w, output_all, grad_rows, gains_all = first_rows(
+        tokens, gains_own, inner_all, output_weight, cosine, sine_table, out_grad, valid_rows, 2
+    )
+    output_rows = across_plane(output_all.reshape(8, head_rows, block))
+    gate_up, pair = lax.optimization_barrier((gate_up, pair))
+    gate_up = planes_together(gate_up)
+    gains = jnp.moveaxis(gains_all, 0, 1).reshape(2, width)
+    gain_first, gain_second = gains[0:1], gains[1:2]
     attended, totals = attend(info, begins, queries, pair)
-    middle, row_second = forward_output(attended, output_rows, tokens, gain_second, 4)
+    middle, row_second, grad_hidden = forward_output(
+        attended, output_rows, tokens, gain_second, grad_rows, down_all, 4
+    )
     rows_second, hidden, grad_gate_low, grad_up_low, down_grads = forward_hidden(
-        row_second, grad_rows, gate_rows, up_rows, down_rows, 5
+        row_second, grad_rows, grad_hidden, gate_up, 5
     )
     (
         grad_middle,
         gain_second_part,
         grad_output_w,
         grad_attended,
-        hidden_grads,
+        gate_grads,
+        up_grads,
     ) = backward_middle(
         grad_gate_low,
         grad_up_low,
-        gate_rows,
-        up_rows,
+        gate_up,
         rows_second,
+        grad_rows,
         output_rows,
         attended,
         middle,
-        grad_rows_own,
         gain_second,
         6,
     )
-    down_grads = lax.psum_scatter(down_grads, "tp", scatter_dimension=0, tiled=True)
-    hidden_grads, down_grads = lax.optimization_barrier((hidden_grads, down_grads))
-    hidden_grads = lax.psum_scatter(
-        hidden_grads.reshape(8 * units, width), "tp", scatter_dimension=0, tiled=True
-    )
-    grad_queries, grad_pair_parts = attend_back(
-        info, begins, queries, pair, attended, grad_attended, totals
-    )
-    grad_pair, layer_out, output_parts = backward_pairs(
-        grad_pair_parts, hidden, down_rows, middle, valid_rows.astype(f32), grad_output_w, 7
-    )
-    grad_pair = jnp.moveaxis(grad_pair, 0, 1).reshape(2 * HEAD_DIM, 8 * size)
-    grad_query_low = turn_back(grad_queries, cosine, sine_table).astype(bf16)
-    grad_key_low = turn_back(grad_pair[:HEAD_DIM], cosine, sine_table)
-    first_core = lax.rem(f, 2) == 0
-    grad_single = jnp.where(first_core, grad_key_low, grad_pair[HEAD_DIM:]).astype(bf16)
-    grad_inner = jnp.concatenate([grad_query_low, grad_single], axis=0)
-    single_rows = jnp.where(
-        first_core,
-        inner_rows_w[head_rows : head_rows + HEAD_DIM],
-        inner_rows_w[head_rows + HEAD_DIM :],
-    )
-    single_weights = jnp.concatenate([inner_rows_w[:head_rows], single_rows], axis=0)
-    tokens_grad, gain_first_part, inner_parts = backward_first(
-        grad_inner, single_weights, rows_first, tokens, grad_middle, gain_first, 8
-    )
-
-    def along_z(parts):
-        rows = parts.shape[1]
-        flat = parts.reshape(8 * rows, block)
-        return lax.psum_scatter(flat, "tp", scatter_dimension=0, tiled=True).reshape(2, rows, block)
-
-    output_parts, hidden_grads = lax.optimization_barrier((output_parts, hidden_grads))
-    output_own = along_z(output_parts)
-    inner_parts, output_own = lax.optimization_barrier((inner_parts, output_own))
-    inner_grads = along_z(inner_parts)
-    gain_parts = jnp.concatenate([gain_first_part, gain_second_part], axis=0)
-    gain_parts = jnp.moveaxis(gain_parts.reshape(2, 8, block), 1, 0)
-    own_down, hidden_own, gain_sums = last_exchange(
-        down_grads.reshape(1, units, width), hidden_grads.reshape(2, units, width), gain_parts, 9
-    )
-    own_gate, own_up = (hidden_own[:, n].reshape(8 * units, block) for n in range(2))
+    def own_plane(parts, *shape):
+        flat = parts.reshape(-1, block)
+        return lax.psum_scatter(flat, "tp", scatter_dimension=0, tiled=True).reshape(*shape)
+
+    down_grads = own_plane(down_grads, 8, units, block)
+    gate_grads, down_grads = lax.optimization_barrier((gate_grads, down_grads))
+    gate_grads = own_plane(gate_grads, 8, units, block)
+    output_parts = across_plane(grad_output_w)
+    output_parts, gate_grads = lax.optimization_barrier((output_parts, gate_grads))
+    output_own = own_plane(output_parts, 2 * head_rows, block)
+    grad_query, grad_pair_parts = attend_back(
+        info, begins, queries, pair, attended, grad_attended, totals, cosine, sine_table
+    )
+    single, layer_out, query_parts = backward_pairs(
+        grad_pair_parts,
+        hidden,
+        down_all,
+        middle,
+        valid_rows,
+        grad_query,
+        rows_first,
+        cosine,
+        sine_table,
+        7,
+    )
+    up_grads, query_parts, output_own = lax.optimization_barrier((up_grads, query_parts, output_own))
+    up_grads = own_plane(up_grads, 8, units, block)
+    tokens_grad, gain_first_part, single_parts, own_down, own_gate = backward_first(
+        grad_query,
+        single,
+        inner_rows_w,
+        rows_first,
+        tokens,
+        grad_middle,
+        gain_first,
+        down_grads,
+        gate_grads,
+        8,
+    )
+    query_parts, up_grads = lax.optimization_barrier((query_parts, up_grads))
+    query_own = own_plane(query_parts, 2 * head_rows, block)
+    gain_sums, pair_own, own_up = last_sums(
+        gain_first_part, gain_second_part, single_parts, up_grads, 9
+    )
+    layer_out, tokens_grad, query, output, gate, up, down = last_forms(
+        layer_out, tokens_grad, query_own, output_own, own_down, own_gate, own_up
+    )
     return (
         layer_out,
         tokens_grad,
         gain_sums[0],
-        inner_grads[:, :head_rows].reshape(2 * head_rows, block).T.astype(f32),
-        inner_grads[0, head_rows:].T.astype(f32),
-        inner_grads[1, head_rows:].T.astype(f32),
-        output_own.reshape(2 * head_rows, block).astype(f32),
+        query,
+        pair_own[0].T,
+        pair_own[1].T,
+        output,
         gain_sums[1],
-        own_gate.T.astype(f32),
-        own_up.T.astype(f32),
-        own_down.reshape(8 * units, block).astype(f32),
+        gate,
+        up,
+        down,
     )
 
 

time: 665 us -> 645 us (0.970)
  waiting for transfers between devices: 1.49 us -> 53.3 us
  Pallas kernels: 591 us -> 544 us
  local copies, waits for them, and re-layouts: 29.8 us -> 5.06 us
  starting transfers between devices: 0.28 us -> 17 us
  other arithmetic: 17 us -> 5.38 us
    pallas_call x3 -> x4, Pallas kernels: 158 us -> 101 us  [the longest x1 73.6 us: backward_pairs(): pl.pallas_call(kernel, out_shape=[jax.ShapeDtypeStruct((HEAD_DIM, chunks...]
    all_gather x3, waiting for transfers between devices: 0.01 us -> 41.2 us  [planes_together(): lax.all_gather(flat, 'tp', axis=0, tiled=True).reshape(4, *part.shape)]
    all_to_all x0 -> x4, starting transfers between devices: none -> 16 us  [across_plane(): return lax.all_to_all(parts, 'fsdp', 0, 0, tiled=False)]
    unnamed x79 -> x19, local copies, waits for them, and re-layouts: 15.2 us -> 1.01 us
    pallas_call x1, Pallas kernels: 110 us -> 99.4 us  [first_rows(): pl.pallas_call(kernel, out_shape=[jax.ShapeDtypeStruct((8, size, width),...]
    pallas_call x1, Pallas kernels: 45.3 us -> 55.4 us  [attend_back(): pl.pallas_call(kernel, grid_spec=pltpu.PrefetchScalarGridSpec(num_scalar_...]
    pallas_call x1, Pallas kernels: 31.9 us -> 40 us  [attend(): pl.pallas_call(kernel, grid_spec=pltpu.PrefetchScalarGridSpec(num_scalar_...]
    reduce_scatter x4 -> x5, waiting for transfers between devices: 0.03 us -> 7.47 us  [own_plane(): lax.psum_scatter(flat, 'tp', scatter_dimension=0, tiled=True)]
  transfers between devices with their start and end apart: 7 -> 12, of which waited for: 0 -> 5; matrix products, arithmetic and copies ran while one was open for 4% -> 1% of each run, Pallas kernels for 77% -> 77%
where the time goes in v4:
time: 645 us; the launch traced here: 640 us
  Pallas kernels  544 us (84%)
  waiting for transfers between devices  53.3 us (8%)
  starting transfers between devices  17 us (3%)
  between operations  14.7 us (2%)
    pallas_call x1, Pallas kernels, first_rows(): pl.pallas_call(kernel, out_shape=[jax.ShapeDtypeStruct((8, size, width),...  99.4 us
    pallas_call x1, Pallas kernels, backward_middle(): pl.pallas_call(kernel, out_shape=[jax.ShapeDtypeStruct((size, width), f32...  90.3 us
    pallas_call x1, Pallas kernels, backward_pairs(): pl.pallas_call(kernel, out_shape=[jax.ShapeDtypeStruct((HEAD_DIM, chunks...  73.6 us
    pallas_call x1, Pallas kernels, backward_first(): pl.pallas_call(kernel, out_shape=[jax.ShapeDtypeStruct((size, width), f32...  64.6 us
    pallas_call x1, Pallas kernels, attend_back(): pl.pallas_call(kernel, grid_spec=pltpu.PrefetchScalarGridSpec(num_scalar_...  55.4 us
    pallas_call x1, Pallas kernels, forward_hidden(): pl.pallas_call(kernel, out_shape=[jax.ShapeDtypeStruct((8, size, width),...  47.3 us
    pallas_call x1, Pallas kernels, forward_output(): pl.pallas_call(kernel, out_shape=[jax.ShapeDtypeStruct((size, width), f32...  46.6 us
    all_gather x3, waiting for transfers between devices, planes_together(): lax.all_gather(flat, 'tp', axis=0, tiled=True).reshape(4, *part.shape)  41.2 us
  transfers between devices with their start and end apart: 12, of which 5 were waited for; matrix products, arithmetic and copies ran while one was open for 1% of the time, Pallas kernels for 77%

profile of v4, /device:TPU:0, one launch (start us, length us, event | category | flops | bytes accessed | tf_op | source)
XLA Modules:
  0.0 639.8 jit_solution(946197597082152762)
XLA Ops:
  7.2 5.2 all-to-all-start
  12.4 0.0 all-gather.4.cloned.1.call-start
  12.4 3.1 first_forms.1
  15.6 0.1 add_bitcast_fusion
  15.6 0.1 fusion.7
  15.7 0.6 slice.36
  16.4 0.6 maximum_convert_fusion.gains_own_ref
  17.0 0.1 fusion.1
  17.1 0.1 fusion.9
  17.2 0.7 pad_add_fusion.info_ref
  17.8 0.6 select_convert_fusion
  18.5 1.3 fusion.valid_ref
  19.8 1.8 multiply_sine_fusion
  21.6 2.7 all-to-all-done
  24.3 3.6 all-to-all-start.1
  27.8 0.0 all-gather.6.cloned.1.call-start
  27.9 0.7 all-gather.6.cloned.1.call-update
  28.6 21.5 %all-gather.4.cloned.1.call-done = bf16[2560,256]{1,0:T(8,128)(2,1)} async-done(((bf16[640,256]{1,0:T(8,128)(2,1)}), bf16[2560,256]{1,0:T(8,128)(2,1)}) %all-gather.4.cloned.1.call-update) | async-done | bytes 1310736 | tf_op jit(solution)/shard_map/all_gather | solution.py:1838
  50.1 99.4 %first_rows.1 = (bf16[8,256,2048]{2,1,0:T(8,128)(2,1)}, bf16[256,2048]{1,0:T(8,128)(2,1)}, bf16[4,8,256,128]{3,2,1,0:T(8,128)(2,1)}, bf16[384,2048]{1,0:T(8,128)...) custom-call(bf16[256,2048]{1,0:T(8,128)(2,1)} %x_ref.2, ...), custom_call_target="tpu_custom_call" | custom-call | flops 109999996928 | bytes 1000000 | tf_op jit(solution)/shard_map/first_rows/pallas_call | solution.py:1186
  149.5 3.6 all-to-all-start.2
  153.1 0.0 all-gather.8.cloned.1.call-start
  153.1 0.7 all-gather.8.cloned.1.call-update
  153.8 0.2 reduce-scatter.6.cloned.1.call-start
  154.0 40.0 %attend.1 = (bf16[256,2048]{1,0:T(8,128)(2,1)}, f32[8,1,1024]{2,1,0:T(1,128)}) custom-call(s32[8,3]{1,0:T(8,128)} %pad_add_fusion.info_ref, s32[8,1,256]{2,1,0:T(1,128)} %bitcast.47, bf16[256,2048]{1,0:T(8,128)(2,1)} %get-tuple-element.71.q_ref, bf16[4,8,256,128]{3,2,1,0:T(8,128)(2,1)} %get-tuple-element.74.kv_ref), custom_call_target="tpu_custom_call" | custom-call | flops 54999998464 | bytes 1000000 | tf_op jit(solution)/shard_map/attend/pallas_call | solution.py:1670
  194.1 0.6 fusion.8
  194.7 1.0 copy-done.3
  195.7 46.6 %forward_output.1 = (f32[256,2048]{1,0:T(8,128)}, bf16[256,2048]{1,0:T(8,128)(2,1)}, f32[8,704,256]{2,1,0:T(8,128)}) custom-call(bf16[256,2048]{1,0:T(8,128)(2,1)} %get-tuple-element.75.o_ref, bf16[256,2048]{1,0:T(8,128)(2,1)} %x_ref.2, f32[1,2048]{1,0:T(1,128)} %bitcast.55, bf16[8,256,256]{2,1,0:T(8,128)(2,1)} %copy-done.3, ...), custom_call_target="tpu_custom_call" | custom-call | flops 49500000256 | bytes 1000000 | tf_op jit(solution)/shard_map/forward_output/pallas_call | solution.py:597
  242.3 19.8 %all-gather.8.cloned.1.call-done = bf16[11264,256]{1,0:T(8,128)(2,1)} async-done(((bf16[2816,256]{1,0:T(8,128)(2,1)}), bf16[11264,256]{1,0:T(8,128)(2,1)}) %all-gather.8.cloned.1.call-update) | async-done | bytes 5767184 | tf_op jit(solution)/shard_map/all_gather | solution.py:1838
  262.1 47.3 %forward_hidden.1 = (bf16[8,256,2048]{2,1,0:T(8,128)(2,1)}, bf16[704,2048]{1,0:T(8,128)(2,1)}, bf16[704,2048]{1,0:T(8,128)(2,1)}, bf16[704,2048]{1,0:T(8,128)(2,1)}, bf16[4,8,176,256]{3,2,1,0:T(8,128)(2,1)}) custom-call(bf16[256,2048]{1,0:T(8,128)(2,1)} %get-tuple-element.80.row_ref, bf16[8,256,2048]{2,1,0:T(8,128)(2,1)} %get-tuple-element.78.dys_hbm, ...), custom_call_target="tpu_custom_call" | custom-call | flops 54999998464 | bytes 1000000 | tf_op jit(solution)/shard_map/forward_hidden/pallas_call | solution.py:732
  309.4 90.3 %backward_middle.1 = (f32[256,2048]{1,0:T(8,128)}, f32[1,2048]{1,0:T(1,128)}, bf16[8,256,256]{2,1,0:T(8,128)(2,1)}, bf16[256,2048]{1,0:T(8,128)(2,1)}, bf16[4,8,...) custom-call(bf16[704,2048]{1,0:T(8,128)(2,1)} %get-tuple-element.83.dgate_hbm, ...), custom_call_target="tpu_custom_call" | custom-call | flops 101200003072 | bytes 1000000 | tf_op jit(solution)/shard_map/backward_middle/pallas_call | solution.py:884
  399.7 3.7 all-to-all-start.3
  403.4 0.0 reduce-scatter.8.cloned.1.call-start
  403.4 0.0 reduce-scatter.6.cloned.1.call-done
  403.5 0.5 reduce-scatter.8.cloned.1.call-update
  404.0 0.0 reduce-scatter.10.cloned.1.call-start
  404.0 55.4 %attend_back.1 = (bf16[256,2048]{1,0:T(8,128)(2,1)}, bf16[4,8,128,256]{3,2,1,0:T(8,128)(2,1)}) custom-call(s32[8,3]{1,0:T(8,128)} %pad_add_fusion.info_ref, s32[8,1,256]{2,1,0:T(1,128)} %bitcast.48, bf16[256,2048]{1,0:T(8,128)(2,1)} %get-tuple-element.71.q_ref, bf16[4,8,256,128]{3,2,1,0:T(8,128)(2,1)} %get-tuple-element.74.kv_ref, ...), custom_call_target="tpu_custom_call" | custom-call | flops 71499997184 | bytes 1000000 | tf_op jit(solution)/shard_map/attend_back/pallas_call | solution.py:1766
  459.4 1.8 reduce-scatter.8.cloned.1.call-done
  461.2 0.3 reduce-scatter.12.cloned.1.call-start
  461.5 73.6 %backward_pairs.1 = (bf16[64,2048]{1,0:T(8,128)(2,1)}, bf16[256,2048]{1,0:T(8,128)(2,1)}, bf16[8,256,256]{2,1,0:T(8,128)(2,1)}) custom-call(bf16[4,8,128,256]{3,2,1,0:T(8,128)(2,1)} %get-tuple-element.89.p_ref, bf16[704,2048]{1,0:T(8,128)(2,1)} %get-tuple-element.90.hidden_hbm, bf16[4,8,176,256]{3,2,1,0:T(8,128)(2,1)} %bitcast.62, ...), custom_call_target="tpu_custom_call" | custom-call | flops 60500000768 | bytes 1000000 | tf_op jit(solution)/shard_map/backward_pairs/pallas_call | solution.py:1330
  535.1 0.0 reduce-scatter.10.cloned.1.call-done.output_in
  535.1 0.3 reduce-scatter.14.cloned.1.call-start
  535.4 64.6 %backward_first.1 = (f32[256,2048]{1,0:T(8,128)}, f32[1,2048]{1,0:T(1,128)}, bf16[8,64,256]{2,1,0:T(8,128)(2,1)}, bf16[8,176,256]{2,1,0:T(8,128)(2,1)}, bf16[8,176,256]{2,1,0:T(8,128)(2,1)}) custom-call(bf16[256,2048]{1,0:T(8,128)(2,1)} %get-tuple-element.91.g_ref, bf16[64,2048]{1,0:T(8,128)(2,1)} %get-tuple-element.94.single_ref, ...), custom_call_target="tpu_custom_call" | custom-call | flops 68200001536 | bytes 1000000 | tf_op jit(solution)/shard_map/backward_first/pallas_call | solution.py:1403
  600.0 0.0 reduce-scatter.12.cloned.1.call-done
  600.1 19.2 %last_sums.1 = (f32[2,256]{1,0:T(2,128)}, f32[2,64,256]{2,1,0:T(8,128)}, bf16[8,176,256]{2,1,0:T(8,128)(2,1)}) custom-call(f32[1,2048]{1,0:T(1,128)} %get-tuple-element.113.first_ref, f32[1,2048]{1,0:T(1,128)} %get-tuple-element.114.second_ref, bf16[8,64,256]{2,1,0:T(8,128)(2,1)} %get-tuple-element.115.p_ref, bf16[8,176,256]{2,1,0:T(8,128)(2,1)} %bitcast.66), custom_call_target="tpu_custom_call" | custom-call | flops 17600000000 | bytes 1000000 | tf_op jit(solution)/shard_map/last_sums/pallas_call | solution.py:1487
  619.3 1.3 fusion.10
  620.6 1.5 slice_bitcast_fusion
  622.2 5.6 reduce-scatter.14.cloned.1.call-done.query_in
  627.8 4.8 last_forms.1
  (33 shorter events, 0.2 us)
Async XLA Ops:
  7.2 17.1 %all-to-all-start = ((bf16[8,176,256]{2,1,0:T(8,128)(2,1)}), bf16[8,176,256]{2,1,0:T(8,128)(2,1)S(1)}, u32[]{:S(2)}, u32[]{:S(2)}) async-start(bf16[8,176,256]{2,1,0:T(8,128)(2,1)} %bitcast.45), calls=%async_computation | async-start | bytes 1441792 | tf_op jit(solution)/shard_map/all_to_all | solution.py:1834
  12.4 37.7 %all-gather.4.cloned.1.call-start = ((), (), s32[]{:S(2)}) async-start(), calls=%async_computation.9 | async-start | bytes 1638400 | tf_op jit(solution)/shard_map/all_gather | solution.py:1838
  12.4 3.2 copy-start.6
  12.4 3.9 copy-start.7
  12.4 3.9 copy-start.8
  17.0 11.6 %copy-start.4 = (s32[2048]{0:T(1024)}, s32[2048]{0:T(1024)S(1)}, u32[]{:S(2)}) copy-start(s32[2048]{0:T(1024)S(1)} %fusion.1) | copy-start | bytes 24580
  24.3 3.6 copy-start.2
  24.3 125.2 %all-to-all-start.1 = ((bf16[8,2,176,256]{3,2,1,0:T(8,128)(2,1)}), bf16[8,2,176,256]{3,2,1,0:T(8,128)(2,1)S(1)}, u32[]{:S(2)}, u32[]{:S(2)}) async-start(bf16[8,2,176,256]{3,2,1,0:T(8,128)(2,1)} %get-tuple-element.72), calls=%async_computation.1 | async-start | bytes 2883584 | tf_op jit(solution)/shard_map/all_to_all | solution.py:1834
  27.8 166.9 %all-gather.6.cloned.1.call-start = ((), (), s32[]{:S(2)}) async-start(), calls=%async_computation.10 | async-start | bytes 3604480 | tf_op jit(solution)/shard_map/all_gather | solution.py:1838
  149.5 3.6 copy-start
  149.5 45.2 %all-to-all-start.2 = ((bf16[8,256,256]{2,1,0:T(8,128)(2,1)}), bf16[8,256,256]{2,1,0:T(8,128)(2,1)S(1)}, u32[]{:S(2)}, u32[]{:S(2)}) async-start(bf16[8,256,256]{2,1,0:T(8,128)(2,1)} %bitcast.44), calls=%async_computation.2 | async-start | bytes 2097152 | tf_op jit(solution)/shard_map/all_to_all | solution.py:1834
  153.1 109.0 %all-gather.8.cloned.1.call-start = ((), (), s32[]{:S(2)}) async-start(), calls=%async_computation.11 | async-start | bytes 7208960 | tf_op jit(solution)/shard_map/all_gather | solution.py:1838
  153.8 249.6 %reduce-scatter.6.cloned.1.call-start = ((), (), s32[]{:S(2)}) async-start(), calls=%async_computation.12 | async-start | bytes 3604480 | tf_op jit(solution)/shard_map/reduce_scatter | solution.py:1908
  154.0 40.0 %copy-start.5 = (f32[8,2,256]{2,1,0:T(2,128)S(1)}, f32[8,2,256]{2,1,0:T(2,128)}, u32[]{:S(2)}) copy-start(f32[8,2,256]{2,1,0:T(2,128)} %get-tuple-element.76) | copy-start | bytes 49156
  194.7 1.0 copy-start.3
  399.7 59.7 %all-to-all-start.3 = ((bf16[8,256,256]{2,1,0:T(8,128)(2,1)}), bf16[8,256,256]{2,1,0:T(8,128)(2,1)S(1)}, u32[]{:S(2)}, u32[]{:S(2)}) async-start(bf16[8,256,256]{2,1,0:T(8,128)(2,1)} %get-tuple-element.100), calls=%async_computation.4 | async-start | bytes 2097152 | tf_op jit(solution)/shard_map/all_to_all | solution.py:1834
  403.4 57.8 %reduce-scatter.8.cloned.1.call-start = ((), (), s32[]{:S(2)}) async-start(), calls=%async_computation.13 | async-start | bytes 3604480 | tf_op jit(solution)/shard_map/reduce_scatter | solution.py:1908
  404.0 131.1 %reduce-scatter.10.cloned.1.call-start = ((), (), s32[]{:S(2)}) async-start(), calls=%async_computation.14 | async-start | bytes 1310720 | tf_op jit(solution)/shard_map/reduce_scatter | solution.py:1908
  459.4 1.8 copy-start.1
  461.2 138.9 %reduce-scatter.12.cloned.1.call-start = ((), (), s32[]{:S(2)}) async-start(), calls=%async_computation.15 | async-start | bytes 3604480 | tf_op jit(solution)/shard_map/reduce_scatter | solution.py:1908
  535.1 92.7 %reduce-scatter.14.cloned.1.call-start = ((), (), s32[]{:S(2)}) async-start(), calls=%async_computation.16 | async-start | bytes 1310720 | tf_op jit(solution)/shard_map/reduce_scatter | solution.py:1908
Sparse Core Ops, SparseCore 0:
  15.7 34.3 all-gather.3
  52.2 74.8 all-gather.5
  156.1 105.9 all-gather.7
  309.5 53.3 reduce-scatter.5
  406.2 54.9 reduce-scatter.7
  463.9 52.3 reduce-scatter.9
  535.3 54.5 reduce-scatter.11
  600.2 27.5 reduce-scatter.13

commit v5 on v4

--- a/solution.py
+++ b/solution.py
@@ -1105,6 +1105,8 @@
         dys[f] = jnp.where(valid_ref[...] > 0, dy_ref[...].astype(f32), 0.0).astype(bf16)
         for k in range(PARTS):
             gather.advance(k)
+            if k in (2, 3):
+                line_output.take(k - 1)
         gather_dys = PlaneGather(dys, dys_sent, dys_arrived)
         gather_dys.begin()
         for c in kept[:2]:
@@ -1153,10 +1155,8 @@
         own_pair.start()
         keep_rows = pltpu.make_async_copy(rows, rows_ref, kept_sem.at[4])
         keep_rows.start()
-        line_output.take(1)
         for k in range(PARTS):
             gather_dys.advance(k)
-        line_output.take(2)
         passed = []
         for i, k, c in spread:
             c.wait_recv()
@@ -1621,46 +1621,77 @@
     size = slots // 8
     span = heads * size
 
-    def kernel(info_ref, begin_ref, q_ref, kv_ref, o_ref, l_ref, q_s, m_s, t_s, a_s):
+    def kernel(info_ref, begin_ref, q_ref, kv_ref, o_ref, l_ref, q_s, m_s, t_s, a_s, even_s, odd_s):
         f = pl.program_id(0)
         low, middle, own = info_ref[f, 0], info_ref[f, 1], info_ref[f, 2]
-        middle = middle + lax.rem(own - middle, WIDE)
         q_s[...] = head_lanes(q_ref[...], heads)
         m_s[...] = jnp.full_like(m_s, -1e30)
         t_s[...] = jnp.zeros_like(t_s)
         a_s[...] = jnp.zeros_like(a_s)
 
-        def step(g, count, masked):
-            block = key_block(kv_ref, g, count)
-            keys, values = block[:, :HEAD_DIM], block[:, HEAD_DIM:]
+        def scores_of(g, count):
+            return dot_nn(key_block(kv_ref, g, count)[:, :HEAD_DIM], q_s[...])
+
+        def add(scores, g, count):
+            values = key_block(kv_ref, g, count)[:, HEAD_DIM:]
             value_cols = values.astype(jnp.float32).T.astype(jnp.bfloat16)
-            if masked:
-                seen = seen_keys(begin_ref[0], g * size, own * size, (size, size))
-                seen = jnp.concatenate([seen] * heads, axis=1)
-            scores = dot_nn(keys, q_s[...])
-            if masked:
-                scores = jnp.where(seen, scores, -1e30)
             largest = m_s[...]
             higher = jnp.maximum(largest, jnp.max(scores, axis=0, keepdims=True))
             raised = jnp.exp(scores - higher)
             fade = jnp.exp(largest - higher)
             m_s[...] = higher
             t_s[...] = t_s[...] * fade + jnp.sum(raised, axis=0, keepdims=True)
-            a_s[...] = a_s[...] * fade + dot_nn(
-                value_cols, raised.astype(jnp.bfloat16)
-            )
-
-        def masked_step(g, carry):
-            step(g, 1, True)
+            a_s[...] = a_s[...] * fade + dot_nn(value_cols, raised.astype(jnp.bfloat16))
+
+        def step(g, count, masked):
+            scores = scores_of(g, count)
+            if masked:
+                seen = seen_keys(begin_ref[0], g * size, own * size, (count * size, size))
+                seen = jnp.concatenate([seen] * heads, axis=1)
+                scores = jnp.where(seen, scores, -1e30)
+            add(scores, g, count)
+
+        count = own + 1 - low
+        odd = lax.rem(count, WIDE) == 1
+
+        @pl.when(odd)
+        def _():
+            step(own, 1, True)
+
+        @pl.when(jnp.logical_not(odd))
+        def _():
+            step(own - 1, WIDE, True)
+
+        units = lax.div(count - 1, WIDE)
+        bounded = jnp.minimum(lax.div(middle - low + WIDE - 1, WIDE), units)
+
+        def masked_step(n, carry):
+            step(low + n * WIDE, WIDE, True)
             return carry
 
-        def plain_step(n, carry):
-            step(middle + n * WIDE, WIDE, False)
+        lax.fori_loop(0, bounded, masked_step, 0)
+        def unit(n):
+            return low + jnp.minimum(n, units - 1) * WIDE
+
+        def two(j, carry):
+            n = bounded + 2 * j
+            odd_s[...] = scores_of(unit(n + 1), WIDE)
+            add(even_s[...], unit(n), WIDE)
+            even_s[...] = scores_of(unit(n + 2), WIDE)
+            add(odd_s[...], unit(n + 1), WIDE)
             return carry
 
-        step(own, 1, True)
-        lax.fori_loop(low, middle, masked_step, 0)
-        lax.fori_loop(0, lax.div(own - middle, WIDE), plain_step, 0)
+        rest = units - bounded
+
+        @pl.when(rest > 0)
+        def _():
+            even_s[...] = scores_of(unit(bounded), WIDE)
+            lax.fori_loop(0, lax.div(rest, 2), two, 0)
+
+            @pl.when(lax.rem(rest, 2) == 1)
+            def _():
+                add(even_s[...], unit(units - 1), WIDE)
+
         result = a_s[...] / t_s[...]
         for h in range(heads):
             o_ref[h * HEAD_DIM : (h + 1) * HEAD_DIM] = result[:, h * size : (h + 1) * size].astype(
@@ -1686,6 +1717,8 @@
                 pltpu.VMEM((1, span), jnp.float32),
                 pltpu.VMEM((1, span), jnp.float32),
                 pltpu.VMEM((HEAD_DIM, span), jnp.float32),
+                pltpu.VMEM((WIDE * size, span), jnp.float32),
+                pltpu.VMEM((WIDE * size, span), jnp.float32),
             ],
         ),
         out_shape=[
@@ -1869,12 +1902,12 @@
     cosine, sine_table = jnp.cos(angles), jnp.sin(angles)
 
     valid_rows = valid_rows.astype(f32)
+    cosine, gate_up = lax.optimization_barrier((cosine, gate_up))
+    gate_up = planes_together(gate_up)
     rows_first, queries, pair, inner_rows_w, output_all, grad_rows, gains_all = first_rows(
         tokens, gains_own, inner_all, output_weight, cosine, sine_table, out_grad, valid_rows, 2
     )
     output_rows = across_plane(output_all.reshape(8, head_rows, block))
-    gate_up, pair = lax.optimization_barrier((gate_up, pair))
-    gate_up = planes_together(gate_up)
     gains = jnp.moveaxis(gains_all, 0, 1).reshape(2, width)
     gain_first, gain_second = gains[0:1], gains[1:2]
     attended, totals = attend(info, begins, queries, pair)

time: 645 us -> 625 us (0.969)
  Pallas kernels: 544 us -> 520 us
  blocking collectives: 0 us -> 16.9 us
  waiting for transfers between devices: 53.3 us -> 40.1 us
    all_gather x3, waiting for transfers between devices: 41.2 us -> 1.66 us  [planes_together(): lax.all_gather(flat, 'tp', axis=0, tiled=True).reshape(4, *part.shape)]
    all_to_all x0 -> x1, blocking collectives: none -> 16.9 us  [across_plane(): return lax.all_to_all(parts, 'fsdp', 0, 0, tiled=False)]
    reduce_scatter x5, waiting for transfers between devices: 7.47 us -> 24.4 us  [own_plane(): lax.psum_scatter(flat, 'tp', scatter_dimension=0, tiled=True)]
    all_to_all x4 -> x3, waiting for transfers between devices: 2.66 us -> 13.4 us  [across_plane(): return lax.all_to_all(parts, 'fsdp', 0, 0, tiled=False)]
    pallas_call x1, Pallas kernels: 40 us -> 30.4 us  [attend(): pl.pallas_call(kernel, grid_spec=pltpu.PrefetchScalarGridSpec(num_scalar_...]
    pallas_call x1, Pallas kernels: 73.6 us -> 66 us  [backward_pairs(): pl.pallas_call(kernel, out_shape=[jax.ShapeDtypeStruct((HEAD_DIM, chunks...]
    pallas_call x1, Pallas kernels: 55.4 us -> 48.6 us  [attend_back(): pl.pallas_call(kernel, grid_spec=pltpu.PrefetchScalarGridSpec(num_scalar_...]
    all_to_all x4 -> x3, starting transfers between devices: 16 us -> 11.6 us  [across_plane(): return lax.all_to_all(parts, 'fsdp', 0, 0, tiled=False)]
  transfers between devices with their start and end apart: 12 -> 11, of which waited for: 5 -> 4; matrix products, arithmetic and copies ran while one was open for 1% -> 2% of each run, Pallas kernels for 77% -> 75%
where the time goes in v5:
time: 625 us; the launch traced here: 616 us
  Pallas kernels  520 us (83%)
  waiting for transfers between devices  40.1 us (6%)
  blocking collectives  16.9 us (3%)
  between operations  14.6 us (2%)
  starting transfers between devices  12.8 us (2%)
    pallas_call x1, Pallas kernels, first_rows(): pl.pallas_call(kernel, out_shape=[jax.ShapeDtypeStruct((8, size, width),...  100 us
    pallas_call x1, Pallas kernels, backward_middle(): pl.pallas_call(kernel, out_shape=[jax.ShapeDtypeStruct((size, width), f32...  89.7 us
    pallas_call x1, Pallas kernels, backward_pairs(): pl.pallas_call(kernel, out_shape=[jax.ShapeDtypeStruct((HEAD_DIM, chunks...  66 us
    pallas_call x1, Pallas kernels, backward_first(): pl.pallas_call(kernel, out_shape=[jax.ShapeDtypeStruct((size, width), f32...  64.6 us
    pallas_call x1, Pallas kernels, attend_back(): pl.pallas_call(kernel, grid_spec=pltpu.PrefetchScalarGridSpec(num_scalar_...  48.6 us
    pallas_call x1, Pallas kernels, forward_hidden(): pl.pallas_call(kernel, out_shape=[jax.ShapeDtypeStruct((8, size, width),...  47.2 us
    pallas_call x1, Pallas kernels, forward_output(): pl.pallas_call(kernel, out_shape=[jax.ShapeDtypeStruct((size, width), f32...  46.6 us
    pallas_call x1, Pallas kernels, attend(): pl.pallas_call(kernel, grid_spec=pltpu.PrefetchScalarGridSpec(num_scalar_...  30.4 us
  transfers between devices with their start and end apart: 11, of which 4 were waited for; matrix products, arithmetic and copies ran while one was open for 2% of the time, Pallas kernels for 75%

profile of v5, /device:TPU:0, one launch (start us, length us, event | category | flops | bytes accessed | tf_op | source)
XLA Modules:
  0.0 616.3 jit_solution(12300698000775957480)
XLA Ops:
  7.2 0.0 all-gather.4.cloned.1.call-start
  7.2 3.1 first_forms.1
  10.4 0.0 all-gather.4.cloned.1.call-update
  10.4 0.0 all-gather.6.cloned.1.call-start
  10.4 16.9 %all_to_all.20 = bf16[8,176,256]{2,1,0:T(8,128)(2,1)} all-to-all(bf16[8,176,256]{2,1,0:T(8,128)(2,1)S(1)} %bitcast.45), channel_id=1, replica_groups=mesh['fsdp'=8,'tp'=4] {'fsdp'}, dimensions={0} | all-to-all | bytes 1441792 | tf_op jit(solution)/shard_map/all_to_all | solution.py:1867
  27.4 3.7 all-to-all-start.1
  31.1 0.0 all-gather.8.cloned.1.call-start
  31.2 0.1 add_bitcast_fusion
  31.3 0.1 fusion.7
  31.4 0.1 fusion.1
  31.5 0.1 fusion.9
  31.6 0.6 slice.36
  32.2 0.6 maximum_convert_fusion.gains_own_ref
  32.8 0.7 pad_add_fusion.info_ref
  33.5 1.3 fusion.valid_ref
  34.8 0.6 select_convert_fusion
  35.4 1.8 multiply_sine_fusion
  37.2 13.4 %all-to-all-done.1 = bf16[8,2,176,256]{3,2,1,0:T(8,128)(2,1)S(1)} async-done(((bf16[8,2,176,256]{3,2,1,0:T(8,128)(2,1)}), bf16[8,2,176,256]{3,2,1,0:T(8,128)(2,1)S(1)}, u32[]{:S(2)}, u32[]{:S(2)}) %all-to-all-start.1) | async-done | bytes 1441824 | tf_op jit(solution)/shard_map/all_to_all | solution.py:1867
  50.7 1.1 copy-done
  51.8 0.0 all-gather.4.cloned.1.call-done
  51.8 100.1 %first_rows.1 = (bf16[8,256,2048]{2,1,0:T(8,128)(2,1)}, bf16[256,2048]{1,0:T(8,128)(2,1)}, bf16[4,8,256,128]{3,2,1,0:T(8,128)(2,1)}, bf16[384,2048]{1,0:T(8,128)...) custom-call(bf16[256,2048]{1,0:T(8,128)(2,1)} %x_ref.2, ...), custom_call_target="tpu_custom_call" | custom-call | flops 109999996928 | bytes 1000000 | tf_op jit(solution)/shard_map/first_rows/pallas_call | solution.py:1186
  152.0 4.3 all-to-all-start.2
  156.2 0.3 reduce-scatter.6.cloned.1.call-start
  156.6 30.4 %attend.1 = (bf16[256,2048]{1,0:T(8,128)(2,1)}, f32[8,1,1024]{2,1,0:T(1,128)}) custom-call(s32[8,3]{1,0:T(8,128)} %pad_add_fusion.info_ref, s32[8,1,256]{2,1,0:T(1,128)} %bitcast.47, bf16[256,2048]{1,0:T(8,128)(2,1)} %get-tuple-element.73.q_ref, bf16[4,8,256,128]{3,2,1,0:T(8,128)(2,1)} %get-tuple-element.74.kv_ref), custom_call_target="tpu_custom_call" | custom-call | flops 54999998464 | bytes 1000000 | tf_op jit(solution)/shard_map/attend/pallas_call | solution.py:1701
  187.0 0.6 fusion.8
  187.6 1.0 copy-done.2
  188.6 46.6 %forward_output.1 = (f32[256,2048]{1,0:T(8,128)}, bf16[256,2048]{1,0:T(8,128)(2,1)}, f32[8,704,256]{2,1,0:T(8,128)}) custom-call(bf16[256,2048]{1,0:T(8,128)(2,1)} %get-tuple-element.75.o_ref, bf16[256,2048]{1,0:T(8,128)(2,1)} %x_ref.2, f32[1,2048]{1,0:T(1,128)} %bitcast.55, bf16[8,256,256]{2,1,0:T(8,128)(2,1)} %copy-done.2, ...), custom_call_target="tpu_custom_call" | custom-call | flops 49500000256 | bytes 1000000 | tf_op jit(solution)/shard_map/forward_output/pallas_call | solution.py:597
  235.1 1.6 all-gather.8.cloned.1.call-done
  236.7 47.2 %forward_hidden.1 = (bf16[8,256,2048]{2,1,0:T(8,128)(2,1)}, bf16[704,2048]{1,0:T(8,128)(2,1)}, bf16[704,2048]{1,0:T(8,128)(2,1)}, bf16[704,2048]{1,0:T(8,128)(2,1)}, bf16[4,8,176,256]{3,2,1,0:T(8,128)(2,1)}) custom-call(bf16[256,2048]{1,0:T(8,128)(2,1)} %get-tuple-element.80.row_ref, bf16[8,256,2048]{2,1,0:T(8,128)(2,1)} %get-tuple-element.78.dys_hbm, ...), custom_call_target="tpu_custom_call" | custom-call | flops 54999998464 | bytes 1000000 | tf_op jit(solution)/shard_map/forward_hidden/pallas_call | solution.py:732
  284.0 89.7 %backward_middle.1 = (f32[256,2048]{1,0:T(8,128)}, f32[1,2048]{1,0:T(1,128)}, bf16[8,256,256]{2,1,0:T(8,128)(2,1)}, bf16[256,2048]{1,0:T(8,128)(2,1)}, bf16[4,8,...) custom-call(bf16[704,2048]{1,0:T(8,128)(2,1)} %get-tuple-element.83.dgate_hbm, ...), custom_call_target="tpu_custom_call" | custom-call | flops 101200003072 | bytes 1000000 | tf_op jit(solution)/shard_map/backward_middle/pallas_call | solution.py:884
  373.7 3.7 all-to-all-start.3
  377.4 0.0 reduce-scatter.8.cloned.1.call-start
  377.4 0.0 reduce-scatter.6.cloned.1.call-done
  377.4 0.5 reduce-scatter.8.cloned.1.call-update
  377.9 0.0 reduce-scatter.10.cloned.1.call-start
  378.0 48.6 %attend_back.1 = (bf16[256,2048]{1,0:T(8,128)(2,1)}, bf16[4,8,128,256]{3,2,1,0:T(8,128)(2,1)}) custom-call(s32[8,3]{1,0:T(8,128)} %pad_add_fusion.info_ref, s32[8,1,256]{2,1,0:T(1,128)} %bitcast.48, bf16[256,2048]{1,0:T(8,128)(2,1)} %get-tuple-element.73.q_ref, bf16[4,8,256,128]{3,2,1,0:T(8,128)(2,1)} %get-tuple-element.74.kv_ref, ...), custom_call_target="tpu_custom_call" | custom-call | flops 71499997184 | bytes 1000000 | tf_op jit(solution)/shard_map/attend_back/pallas_call | solution.py:1799
  426.6 18.7 %reduce-scatter.8.cloned.1.call-done = bf16[1408,256]{1,0:T(8,128)(2,1)} async-done(((bf16[5632,256]{1,0:T(8,128)(2,1)}), bf16[1408,256]{1,0:T(8,128)(2,1)}) %reduce-scatter.8.cloned.1.call-update) | async-done | bytes 720912 | tf_op jit(solution)/shard_map/reduce_scatter | solution.py:1941
  445.3 0.4 reduce-scatter.12.cloned.1.call-start
  445.8 66.0 %backward_pairs.1 = (bf16[64,2048]{1,0:T(8,128)(2,1)}, bf16[256,2048]{1,0:T(8,128)(2,1)}, bf16[8,256,256]{2,1,0:T(8,128)(2,1)}) custom-call(bf16[4,8,128,256]{3,2,1,0:T(8,128)(2,1)} %get-tuple-element.89.p_ref, bf16[704,2048]{1,0:T(8,128)(2,1)} %get-tuple-element.90.hidden_hbm, bf16[4,8,176,256]{3,2,1,0:T(8,128)(2,1)} %bitcast.62, ...), custom_call_target="tpu_custom_call" | custom-call | flops 60500000768 | bytes 1000000 | tf_op jit(solution)/shard_map/backward_pairs/pallas_call | solution.py:1330
  511.8 0.0 reduce-scatter.10.cloned.1.call-done.output_in
  511.8 0.2 reduce-scatter.14.cloned.1.call-start
  512.0 64.6 %backward_first.1 = (f32[256,2048]{1,0:T(8,128)}, f32[1,2048]{1,0:T(1,128)}, bf16[8,64,256]{2,1,0:T(8,128)(2,1)}, bf16[8,176,256]{2,1,0:T(8,128)(2,1)}, bf16[8,176,256]{2,1,0:T(8,128)(2,1)}) custom-call(bf16[256,2048]{1,0:T(8,128)(2,1)} %get-tuple-element.91.g_ref, bf16[64,2048]{1,0:T(8,128)(2,1)} %get-tuple-element.94.single_ref, ...), custom_call_target="tpu_custom_call" | custom-call | flops 68200001536 | bytes 1000000 | tf_op jit(solution)/shard_map/backward_first/pallas_call | solution.py:1403
  576.7 0.0 reduce-scatter.12.cloned.1.call-done
  576.7 19.2 %last_sums.1 = (f32[2,256]{1,0:T(2,128)}, f32[2,64,256]{2,1,0:T(8,128)}, bf16[8,176,256]{2,1,0:T(8,128)(2,1)}) custom-call(f32[1,2048]{1,0:T(1,128)} %get-tuple-element.113.first_ref, f32[1,2048]{1,0:T(1,128)} %get-tuple-element.114.second_ref, bf16[8,64,256]{2,1,0:T(8,128)(2,1)} %get-tuple-element.115.p_ref, bf16[8,176,256]{2,1,0:T(8,128)(2,1)} %bitcast.66), custom_call_target="tpu_custom_call" | custom-call | flops 17600000000 | bytes 1000000 | tf_op jit(solution)/shard_map/last_sums/pallas_call | solution.py:1487
  596.0 1.3 fusion.10
  597.3 1.5 slice_bitcast_fusion
  598.8 5.6 reduce-scatter.14.cloned.1.call-done.query_in
  604.4 4.8 last_forms.1
  (32 shorter events, 0.2 us)
Async XLA Ops:
  7.2 44.6 %all-gather.4.cloned.1.call-start = ((), (), s32[]{:S(2)}) async-start(), calls=%async_computation.9 | async-start | bytes 1638400 | tf_op jit(solution)/shard_map/all_gather | solution.py:1871
  7.2 3.2 copy-start.3
  10.4 177.2 %all-gather.6.cloned.1.call-start = ((), (), s32[]{:S(2)}) async-start(), calls=%async_computation.10 | async-start | bytes 3604480 | tf_op jit(solution)/shard_map/all_gather | solution.py:1871
  27.4 3.9 copy-start.6
  27.4 4.8 copy-start.7
  27.4 4.8 copy-start.8
  27.4 23.3 %all-to-all-start.1 = ((bf16[8,2,176,256]{3,2,1,0:T(8,128)(2,1)}), bf16[8,2,176,256]{3,2,1,0:T(8,128)(2,1)S(1)}, u32[]{:S(2)}, u32[]{:S(2)}) async-start(bf16[8,2,176,256]{3,2,1,0:T(8,128)(2,1)} %get-tuple-element.71), calls=%async_computation.1 | async-start | bytes 2883584 | tf_op jit(solution)/shard_map/all_to_all | solution.py:1867
  31.1 205.6 %all-gather.8.cloned.1.call-start = ((), (), s32[]{:S(2)}) async-start(), calls=%async_computation.11 | async-start | bytes 7208960 | tf_op jit(solution)/shard_map/all_gather | solution.py:1871
  31.5 120.5 %copy-start.4 = (s32[2048]{0:T(1024)}, s32[2048]{0:T(1024)S(1)}, u32[]{:S(2)}) copy-start(s32[2048]{0:T(1024)S(1)} %fusion.1) | copy-start | bytes 24580
  50.7 1.1 copy-start
  152.0 35.6 %all-to-all-start.2 = ((bf16[8,256,256]{2,1,0:T(8,128)(2,1)}), bf16[8,256,256]{2,1,0:T(8,128)(2,1)S(1)}, u32[]{:S(2)}, u32[]{:S(2)}) async-start(bf16[8,256,256]{2,1,0:T(8,128)(2,1)} %bitcast.44), calls=%async_computation.2 | async-start | bytes 2097152 | tf_op jit(solution)/shard_map/all_to_all | solution.py:1867
  156.2 221.2 %reduce-scatter.6.cloned.1.call-start = ((), (), s32[]{:S(2)}) async-start(), calls=%async_computation.12 | async-start | bytes 3604480 | tf_op jit(solution)/shard_map/reduce_scatter | solution.py:1941
  156.6 30.4 %copy-start.5 = (f32[8,2,256]{2,1,0:T(2,128)S(1)}, f32[8,2,256]{2,1,0:T(2,128)}, u32[]{:S(2)}) copy-start(f32[8,2,256]{2,1,0:T(2,128)} %get-tuple-element.76) | copy-start | bytes 49156
  187.6 1.0 copy-start.2
  373.7 52.9 %all-to-all-start.3 = ((bf16[8,256,256]{2,1,0:T(8,128)(2,1)}), bf16[8,256,256]{2,1,0:T(8,128)(2,1)S(1)}, u32[]{:S(2)}, u32[]{:S(2)}) async-start(bf16[8,256,256]{2,1,0:T(8,128)(2,1)} %get-tuple-element.100), calls=%async_computation.4 | async-start | bytes 2097152 | tf_op jit(solution)/shard_map/all_to_all | solution.py:1867
  377.4 67.9 %reduce-scatter.8.cloned.1.call-start = ((), (), s32[]{:S(2)}) async-start(), calls=%async_computation.13 | async-start | bytes 3604480 | tf_op jit(solution)/shard_map/reduce_scatter | solution.py:1941
  377.9 133.8 %reduce-scatter.10.cloned.1.call-start = ((), (), s32[]{:S(2)}) async-start(), calls=%async_computation.14 | async-start | bytes 1310720 | tf_op jit(solution)/shard_map/reduce_scatter | solution.py:1941
  426.6 18.7 %copy-start.1 = (bf16[8,256,256]{2,1,0:T(8,128)(2,1)}, bf16[8,256,256]{2,1,0:T(8,128)(2,1)S(1)}, u32[]{:S(2)}) copy-start(bf16[8,256,256]{2,1,0:T(8,128)(2,1)S(1)} %all-to-all-done.3) | copy-start | bytes 3145732
  445.3 131.4 %reduce-scatter.12.cloned.1.call-start = ((), (), s32[]{:S(2)}) async-start(), calls=%async_computation.15 | async-start | bytes 3604480 | tf_op jit(solution)/shard_map/reduce_scatter | solution.py:1941
  511.8 92.6 %reduce-scatter.14.cloned.1.call-start = ((), (), s32[]{:S(2)}) async-start(), calls=%async_computation.16 | async-start | bytes 1310720 | tf_op jit(solution)/shard_map/reduce_scatter | solution.py:1941
Sparse Core Ops, SparseCore 0:
  10.5 35.3 all-gather.3
  47.5 80.4 all-gather.5
  130.2 106.5 all-gather.7
  284.1 63.2 reduce-scatter.5
  380.2 65.0 reduce-scatter.7
  448.0 44.6 reduce-scatter.9
  511.9 54.5 reduce-scatter.11
  576.8 27.5 reduce-scatter.13
